TPU v7x, 512 devices: a whole 4x4x16 slice. The times are simulated.
512 devices in a mesh: seq: 8 (over y, core), exp: 16 (over z), hid: 4 (over x).
Axes of the slice: x: 4, y: 4, z: 16, core: 2. Of those that a mesh axis runs over, the one named last changes fastest.
Arguments:
- x_in: bfloat16 [1536, 4096], P(('seq', 'exp', 'hid')), may hold values from -6 to 6
- norm_gain: float32 [4096], replicated, may hold values from 0.1 to 1.9
- w_in_x: bfloat16 [4096, 8192], P('seq', ('exp', 'hid')), may hold values from -0.09375 to 0.09375
- w_in_z: bfloat16 [4096, 8192], P('seq', ('exp', 'hid')), may hold values from -0.09375 to 0.09375
- conv_weight: float32 [4, 8192], P(None, ('exp', 'hid')), may hold values from -3 to 3
- conv_bias: float32 [8192], P(('exp', 'hid')), may hold values from -3 to 3
- w_xproj: bfloat16 [8192, 288], P(('exp', 'hid')), may hold values from -0.125 to 0.125
- w_dt: bfloat16 [256, 8192], P(None, ('exp', 'hid')), may hold values from -0.375 to 0.375
- dt_bias: float32 [8192], P(('exp', 'hid')), may hold values from -5 to -2.5
- a_log: float32 [16, 8192], P(None, ('exp', 'hid')), may hold values from -6 to 3
- d_skip: float32 [8192], P(('exp', 'hid')), may hold values from 0.5 to 1.5
- w_out: bfloat16 [8192, 4096], P(('exp', 'hid'), 'seq'), may hold values from -0.0625 to 0.0625
- moe_gain: float32 [4096], replicated, may hold values from 0.1 to 1.9
- route_ids: int32 [1536, 2], P(('seq', 'exp', 'hid')), may hold values from 0 to 15, all different within a row; in each aligned block of 12 rows (0 to 11, 12 to 23, ...) at most 3 rows name the same one
- route_weights: bfloat16 [1536, 2], P(('seq', 'exp', 'hid')), may hold values from 0.099609375 to 1
- w_gate: bfloat16 [16, 4096, 12288], P('exp', None, ('seq', 'hid')), may hold values from -0.09375 to 0.09375
Outputs:
- resid: bfloat16 [1536, 4096], P(('seq', 'exp', 'hid'))
- expert_act: bfloat16 [16, 384, 12288], P('exp', None, ('seq', 'hid'))
Inputs may be any that keep to these rules, and one draw needn't show every extreme that they name: `route_ids`: in each aligned block of 12 tokens no expert is named by more than 3 rows, and in some block one expert is named by exactly 3; a token names 2 different experts.
All inputs are finite; a program needn't handle non-finite values.
Results may differ from a plain program's by a relative error of at most 0.015.
Values may be sent and summed in bfloat16 or wider, within the bound.
No kernel may reach another device: no remote copies, remote signals or barrier semaphores. Data moves between devices by JAX's collectives and lax.ppermute only.
A program may use at most 64 MiB of HBM per device.

v0:
```python
import jax
import jax.numpy as jnp
from jax import lax
from jax.sharding import PartitionSpec as P

BLOCKLEN = 16
TOK_DEV = 192


def shifted(block, axis, distance):
    devices = range(lax.axis_size(axis))
    route = [(i - distance, i) for i in devices if i - distance in devices]
    return lax.ppermute(block, axis, route)


def carried_in(x, axis, combine, identity):
    peers, index = (lax.axis_size(axis), lax.axis_index(axis))
    everything = jax.tree.map(lambda part: lax.all_gather(part, axis), x)
    start = jax.tree.map(
        lambda part, zero: jnp.broadcast_to(jnp.asarray(zero, part.dtype), part.shape), x, identity
    )

    def step(k, before):
        reached = k < index
        new = combine(before, jax.tree.map(lambda part: part[k], everything))
        return jax.tree.map(lambda a, b: jnp.where(reached, a, b), new, before)

    return lax.fori_loop(0, peers, step, start)


def normalize(values, gain):
    wide = values.astype(jnp.float32)
    scale = lax.rsqrt(jnp.mean(wide * wide, axis=-1, keepdims=True) + 1e-05)
    return (wide * scale * gain).astype(jnp.bfloat16)


def chain_link(earlier, later):
    return (earlier[0] * later[0], later[0] * earlier[1] + later[1])


def shards(
    x_in,
    norm_gain,
    w_in_x,
    w_in_z,
    conv_weight,
    conv_bias,
    w_xproj,
    w_dt,
    dt_bias,
    a_log,
    d_skip,
    w_out,
    moe_gain,
    route_ids,
    route_weights,
    w_gate,
):
    n_exp = lax.axis_size("exp")
    normed = normalize(x_in, norm_gain)
    gathered = lax.all_gather(normed, ("exp", "hid"), axis=0, tiled=True)
    tok_count = gathered.shape[0]
    channels = w_in_x.shape[1]
    stream_sum = jnp.dot(
        gathered,
        lax.all_gather(w_in_x, "seq", axis=0, tiled=True),
        preferred_element_type=jnp.float32,
    )
    gate_sum = jnp.dot(
        gathered,
        lax.all_gather(w_in_z, "seq", axis=0, tiled=True),
        preferred_element_type=jnp.float32,
    )
    stream = stream_sum.astype(jnp.bfloat16)
    gate_in = gate_sum.astype(jnp.bfloat16)
    tap_count = conv_weight.shape[0]
    before = shifted(stream[tok_count - (tap_count - 1) :], "seq", 1)
    padded = jnp.concatenate([before, stream], 0).astype(jnp.float32)
    convolved = conv_bias + jnp.zeros((tok_count, channels), jnp.float32)
    for offset in range(tap_count):
        convolved = convolved + conv_weight[offset] * padded[offset : offset + tok_count]
    inner_act = jax.nn.silu(convolved).astype(jnp.bfloat16)
    projected = lax.psum(
        jnp.dot(inner_act, w_xproj, preferred_element_type=jnp.float32), ("exp", "hid")
    )
    low_rank = w_dt.shape[0]
    states = a_log.shape[0]
    step_low = projected[:, :low_rank].astype(jnp.bfloat16)
    input_mat = projected[:, low_rank : low_rank + states]
    output_mat = projected[:, low_rank + states :]
    step_size = jax.nn.softplus(
        jnp.dot(step_low, w_dt, preferred_element_type=jnp.float32) + dt_bias
    )
    decay = -jnp.exp(a_log)
    inner_f = inner_act.astype(jnp.float32)
    blocks = tok_count // BLOCKLEN
    log_decay = (step_size[:, None, :] * decay[None]).reshape(blocks, BLOCKLEN, states, channels)
    drive = ((step_size * inner_f)[:, None, :] * input_mat[:, :, None]).reshape(
        blocks, BLOCKLEN, states, channels
    )
    out_blocks = output_mat.reshape(blocks, BLOCKLEN, states)
    lower = jnp.arange(BLOCKLEN)[:, None] >= jnp.arange(BLOCKLEN)[None, :]

    def block_step(carry, inputs):
        state, total = carry
        block_decay, block_drive, block_out = inputs
        running = jnp.cumsum(block_decay, 0)
        spread = running[:, None] - running[None, :]
        weights = jnp.exp(jnp.where(lower[:, :, None, None], spread, -1e30))
        inside = jnp.einsum("tsnc,snc->tnc", weights, block_drive) + jnp.exp(running) * state[None]
        local_out = jnp.sum(block_out[:, :, None] * inside, 1)
        carried = block_out[:, :, None] * jnp.exp(running + total[None])
        return ((inside[-1], total + running[-1]), (local_out, carried))

    start_pair = (
        jnp.zeros((states, channels), jnp.float32),
        jnp.zeros((states, channels), jnp.float32),
    )
    final_pair, per_block = lax.scan(block_step, start_pair, (log_decay, drive, out_blocks))
    local_final, total_log = final_pair
    local_out, carried = per_block
    shard_decay = jnp.exp(total_log)
    identity = (
        jnp.ones((states, channels), jnp.float32),
        jnp.zeros((states, channels), jnp.float32),
    )
    incoming = carried_in((shard_decay, local_final), "seq", chain_link, identity)[1]
    correction = jnp.einsum("tnc,nc->tc", carried.reshape(tok_count, states, channels), incoming)
    ssm = local_out.reshape(tok_count, channels) + correction + d_skip * inner_f
    gated = (ssm * jax.nn.silu(gate_in.astype(jnp.float32))).astype(jnp.bfloat16)
    out_full = lax.all_gather(w_out, "seq", axis=1, tiled=True)
    mixed = lax.psum_scatter(
        jnp.dot(gated, out_full, preferred_element_type=jnp.float32),
        ("exp", "hid"),
        scatter_dimension=0,
        tiled=True,
    )
    resid = (x_in.astype(jnp.float32) + mixed).astype(jnp.bfloat16)
    moe_in = normalize(resid, moe_gain)
    blk_tok, blk_ids, blk_wts = (
        lax.all_gather(moe_in, "hid", axis=0, tiled=True),
        lax.all_gather(route_ids, "hid", axis=0, tiled=True),
        lax.all_gather(route_weights, "hid", axis=0, tiled=True),
    )
    slot_most = max(2, 4 * TOK_DEV // (n_exp * n_exp))
    block_len = blk_ids.shape[0]
    top_count = blk_ids.shape[1]
    flat_ids = blk_ids.reshape(-1)
    onehot = (flat_ids[:, None] == jnp.arange(n_exp, dtype=jnp.int32)[None, :]).astype(jnp.int32)
    position = jnp.sum((jnp.cumsum(onehot, 0) - 1) * onehot, 1)
    target = flat_ids * slot_most + position
    select = target[None, :] == jnp.arange(n_exp * slot_most, dtype=jnp.int32)[:, None]
    select_tok = jnp.sum(
        select.reshape(n_exp * slot_most, block_len, top_count).astype(jnp.float32), 2
    ).astype(jnp.bfloat16)
    send_tok = jnp.dot(select_tok, blk_tok, preferred_element_type=jnp.float32).astype(jnp.bfloat16)
    send_wts = jnp.sum(
        jnp.where(select, blk_wts.reshape(-1)[None, :].astype(jnp.float32), 0.0), 1
    ).astype(jnp.bfloat16)
    got_tok, got_wts = (
        lax.all_to_all(
            send_tok.reshape(n_exp, slot_most, -1), "exp", split_axis=0, concat_axis=0, tiled=True
        ),
        lax.all_to_all(
            send_wts.reshape(n_exp, slot_most), "exp", split_axis=0, concat_axis=0, tiled=True
        ),
    )
    all_tok, all_wts = (
        lax.all_gather(got_tok.reshape(n_exp * slot_most, -1), "seq", axis=0, tiled=True),
        lax.all_gather(got_wts.reshape(-1), "seq", axis=0, tiled=True),
    )
    activated = (
        jax.nn.silu(jnp.dot(all_tok, w_gate[0], preferred_element_type=jnp.float32))
        * all_wts.astype(jnp.float32)[:, None]
    )
    return (resid, activated.astype(jnp.bfloat16)[None])


def solution(mesh):
    in_specs = (
        P(("seq", "exp", "hid"), None),
        P(),
        P("seq", ("exp", "hid")),
        P("seq", ("exp", "hid")),
        P(None, ("exp", "hid")),
        P(("exp", "hid")),
        P(("exp", "hid"), None),
        P(None, ("exp", "hid")),
        P(("exp", "hid")),
        P(None, ("exp", "hid")),
        P(("exp", "hid")),
        P(("exp", "hid"), "seq"),
        P(),
        P(("seq", "exp", "hid"), None),
        P(("seq", "exp", "hid"), None),
        P("exp", None, ("seq", "hid")),
    )
    out_specs = (P(("seq", "exp", "hid"), None), P("exp", None, ("seq", "hid")))
    return jax.shard_map(shards, mesh=mesh, in_specs=in_specs, out_specs=out_specs, check_vma=False)
```

profile of v0, /device:TPU:1, one launch (start us, length us, event | category | flops | bytes accessed | tf_op | source)
XLA Modules:
  0.0 915.0 jit_solution(7748439034888621030)
XLA Ops:
  8.3 1.5 fusion.34
  10.6 138.4 %all-gather.20.cloned.1.call-done = bf16[64,3,4096]{2,1,0:T(4,128)(2,1)} async-done(((bf16[1,3,4096]{2,1,0:T(4,128)(2,1)}), bf16[64,3,4096]{2,1,0:T(4,128)(2,1)}) %all-gather.20.cloned.1.call-update) | async-done | bytes 1572880 | tf_op jit(solution)/shard_map/all_gather | solution.py:61
  148.9 4.3 reshape.134
  153.2 34.4 %all-gather.12.cloned.1.call-done = bf16[4096,128]{1,0:T(8,128)(2,1)} async-done(((bf16[512,128]{1,0:T(8,128)(2,1)}), bf16[4096,128]{1,0:T(8,128)(2,1)}) %all-gather.12.cloned.1.call-update) | async-done | bytes 1048592 | tf_op jit(solution)/shard_map/all_gather | solution.py:66
  187.6 2.3 convolution_convert_fusion.2
  189.9 1.9 collective-permute-start
  195.3 252.8 %all-reduce.5.cloned.1.call-done = f32[192,288]{1,0:T(8,128)} async-done(((f32[192,288]{1,0:T(8,128)}), f32[192,288]{1,0:T(8,128)}) %all-reduce.5.cloned.1.call-update) | async-done | bytes 221200 | tf_op jit(solution)/shard_map/psum | solution.py:83
  450.4 2.2 broadcast_multiply_fusion
  452.6 42.2 %while.31 = (s32[]{:T(128)}, f32[16,128]{1,0:T(8,128)S(1)}, f32[16,128]{1,0:T(8,128)S(1)}, f32[12,16,128]{2,1,0:T(8,128)S(1)}, f32[12,16,16,128]{3,2,1,0:T(8,128...) while((s32[]{:T(128)}, f32[16,128]{1,0:T(8,128)S(1)}, ...), condition=%wide.region_5.6_spmd.clone, body=%wide.region_2.5_spmd.clone.sunk | while | flops 2754819 | bytes 1668731 | solution.py:119
  494.8 23.6 %all-gather = f32[128,128]{1,0:T(8,128)S(1)} all-gather(f32[16,128]{1,0:T(8,128)S(1)} %exp.40), channel_id=2, replica_groups=mesh['seq'=8,'exp'=16,'hid'=4] {'seq'}, dimensions={0}, use_global_device_ids=true | all-gather | bytes 73728 | tf_op jit(solution)/shard_map/all_gather | solution.py:18
  518.3 12.7 %all-gather.1 = f32[128,128]{1,0:T(8,128)S(1)} all-gather(f32[16,128]{1,0:T(8,128)S(1)} %get-tuple-element.148), channel_id=3, replica_groups=mesh['seq'=8,'exp'=16,'hid'=4] {'seq'}, dimensions={0}, use_global_device_ids=true | all-gather | bytes 73728 | tf_op jit(solution)/shard_map/all_gather | solution.py:18
  531.3 1.7 fusion.13
  533.1 2.3 fusion.22
  535.4 3.4 fusion.42
  539.5 5.8 all-gather.3
  548.5 260.6 %all-reduce.7.cloned.1.call-done = f32[192,4096]{1,0:T(8,128)} async-done(((f32[192,4096]{1,0:T(8,128)}), f32[192,4096]{1,0:T(8,128)}) %all-reduce.7.cloned.1.call-update) | async-done | bytes 3145744
  810.9 9.4 %all-gather.4 = bf16[4,3,4096]{2,1,0:T(4,128)(2,1)S(1)} all-gather(bf16[1,3,4096]{2,1,0:T(4,128)(2,1)S(1)} %fusion.35), channel_id=1, replica_groups=mesh['seq'=8,'exp'=16,'hid'=4] {'hid'}, dimensions={0}, use_global_device_ids=true | all-gather | bytes 122880 | tf_op jit(solution)/shard_map/all_gather | solution.py:141
  823.3 22.8 %all_to_all.11 = bf16[16,3,4096]{2,1,0:T(4,128)(2,1)} all-to-all(bf16[16,3,4096]{2,1,0:T(4,128)(2,1)} %reshape.124), channel_id=1, replica_groups=mesh['seq'=8,'exp'=16,'hid'=4] {'exp'}, dimensions={0} | all-to-all | bytes 786432 | tf_op jit(solution)/shard_map/all_to_all | solution.py:161
  846.1 2.1 reshape.125
  848.2 7.1 all-gather.5
  856.4 7.7 all-to-all-start.1
  866.0 9.3 %all-to-all-done.1 = bf16[16,1,3]{2,1,0:T(2,128)(2,1)S(1)} async-done(((bf16[16,1,3]{2,1,0:T(2,128)(2,1)}), bf16[16,1,3]{2,1,0:T(2,128)(2,1)S(1)}, u32[]{:S(2)}, u32[]{:S(2)}) %all-to-all-start.1) | async-done | bytes 128 | tf_op jit(solution)/shard_map/all_to_all | solution.py:164
  875.7 27.9 %all-reduce = bf16[384]{0:T(512)(128)(2,1)S(1)} all-reduce(bf16[384]{0:T(512)(128)(2,1)S(1)} %dynamic-update-slice), channel_id=1, replica_groups=mesh['seq'=8,'exp'=16,'hid'=4] {'seq'}, use_global_device_ids=true, to_apply=%add | all-reduce | flops 384 | bytes 1536
  903.7 4.5 fusion.17
  (220 shorter events, 59.9 us)
Async XLA Ops:
  7.2 896.5 %copy-start = (bf16[1,4096,384]{2,1,0:T(8,128)(2,1)S(1)}, bf16[1,4096,384]{2,1,0:T(8,128)(2,1)}, u32[]{:S(2)}) copy-start(bf16[1,4096,384]{2,1,0:T(8,128)(2,1)} %param.35) | copy-start | bytes 9437188
  7.2 141.8 %all-gather.20.cloned.1.call-start = ((), (), s32[]{:S(2)}) async-start(), calls=%async_computation.7 | async-start | bytes 2129920 | tf_op jit(solution)/shard_map/all_gather | solution.py:61
  9.8 177.9 %all-gather.12.cloned.1.call-start = ((), (), s32[]{:S(2)}) async-start(), calls=%async_computation.2 | async-start | bytes 1179648 | tf_op jit(solution)/shard_map/all_gather | solution.py:66
  10.5 437.6 %all-reduce.5.cloned.1.call-start = ((), (), s32[]{:S(2)}) async-start(), calls=%async_computation.3 | async-start | bytes 589824 | tf_op jit(solution)/shard_map/psum | solution.py:83
  153.2 38.7 %copy-start.6 = (f32[4,128]{1,0:T(4,128)S(1)}, f32[4,128]{1,0:T(4,128)}, u32[]{:S(2)}) copy-start(f32[4,128]{1,0:T(4,128)} %param.24) | copy-start | bytes 6148
  153.2 39.8 %copy-start.11 = (f32[128]{0:T(128)S(1)}, f32[128]{0:T(128)}, u32[]{:S(2)}) copy-start(f32[128]{0:T(128)} %param.25) | copy-start | bytes 1540
  153.2 39.9 %copy-start.3 = (bf16[128,288]{0,1:T(8,128)(2,1)S(1)}, bf16[128,288]{0,1:T(8,128)(2,1)}, u32[]{:S(2)}) copy-start(bf16[128,288]{0,1:T(8,128)(2,1)} %param.26) | copy-start | bytes 221188
  153.2 42.1 %copy-start.5 = (f32[16,128]{1,0:T(8,128)S(1)}, f32[16,128]{1,0:T(8,128)}, u32[]{:S(2)}) copy-start(f32[16,128]{1,0:T(8,128)} %param.29) | copy-start | bytes 24580
  189.9 259.3 %copy-start.8 = (f32[128]{0:T(128)S(1)}, f32[128]{0:T(128)}, u32[]{:S(2)}) copy-start(f32[128]{0:T(128)} %param.28) | copy-start | bytes 1540
  189.9 3.0 collective-permute-start
  194.0 339.1 %all-gather.14.cloned.1.call-start = ((), (), s32[]{:S(2)}) async-start(), calls=%async_computation.4 | async-start | bytes 1179648 | tf_op jit(solution)/shard_map/all_gather | solution.py:71
  194.6 340.8 %all-gather.16.cloned.1.call-start = ((), (), s32[]{:S(2)}) async-start(), calls=%async_computation.5 | async-start | bytes 1179648 | tf_op jit(solution)/shard_map/all_gather | solution.py:131
  195.2 613.9 %all-reduce.7.cloned.1.call-start = ((), (), s32[]{:S(2)}) async-start(), calls=%async_computation.8 | async-start | bytes 6291456
  494.8 38.4 %copy-start.9 = (f32[128]{0:T(128)S(1)}, f32[128]{0:T(128)}, u32[]{:S(2)}) copy-start(f32[128]{0:T(128)} %param.30) | copy-start | bytes 1540
  538.9 0.7 copy-start.7
  538.9 270.3 %copy-start.1 = (bf16[3,4096]{1,0:T(4,128)(2,1)S(1)}, bf16[3,4096]{1,0:T(4,128)(2,1)}, u32[]{:S(2)}) copy-start(bf16[3,4096]{1,0:T(4,128)(2,1)} %param.20) | copy-start | bytes 73732
  538.9 272.0 %copy-start.4 = (f32[4096]{0:T(1024)S(1)}, f32[4096]{0:T(1024)}, u32[]{:S(2)}) copy-start(f32[4096]{0:T(1024)} %param.32) | copy-start | bytes 49156
  538.9 364.8 %all-gather.18.cloned.1.call-start = ((), (), s32[]{:S(2)}) async-start(), calls=%async_computation.6 | async-start | bytes 3538944 | tf_op jit(solution)/shard_map/all_gather | solution.py:169
  810.2 0.6 copy-start.2
  822.3 25.9 %copy-start.10 = (bf16[3,2]{0,1:T(2,128)(2,1)S(1)}, bf16[3,2]{0,1:T(2,128)(2,1)}, u32[]{:S(2)}) copy-start(bf16[3,2]{0,1:T(2,128)(2,1)} %param.34) | copy-start | bytes 40
  856.4 18.9 %all-to-all-start.1 = ((bf16[16,1,3]{2,1,0:T(2,128)(2,1)}), bf16[16,1,3]{2,1,0:T(2,128)(2,1)S(1)}, u32[]{:S(2)}, u32[]{:S(2)}) async-start(bf16[16,1,3]{2,1,0:T(2,128)(2,1)} %convert_element_type.105), calls=%async_computation.1 | async-start | bytes 16384 | tf_op jit(solution)/shard_map/all_to_all | solution.py:164
Sparse Core Ops, SparseCore 0:
  11.5 137.3 all-gather.19
  151.1 36.5 all-gather.11
  194.1 253.9 all-reduce.4
  450.4 36.2 all-gather.13
  488.9 31.0 all-gather.15
  539.0 270.0 all-reduce.6
  848.3 44.5 all-gather.17
where the time goes:
time: 916 us; the launch traced here: 915 us
  waiting for transfers between devices  699 us (76%)
  blocking collectives  109 us (12%)
  other arithmetic  38.6 us (4%)
  local copies, waits for them, and re-layouts  26.4 us (3%)
  matrix products  15.7 us (2%)
  between operations  15.7 us (2%)
  starting transfers between devices  9.87 us (1%)
    unnamed x8, waiting for transfers between devices  262 us
    psum x1, waiting for transfers between devices, shards(): lax.psum(jnp.dot(inner_act, w_xproj, preferred_element_type=jnp.float32),...  253 us
    all_gather x1, waiting for transfers between devices, shards(): gathered = lax.all_gather(normed, ('exp', 'hid'), axis=0, tiled=True)  138 us
    all_gather x2, blocking collectives, carried_in(): everything = jax.tree.map(lambda part: lax.all_gather(part, axis), x)  36.3 us
    all_gather x1, waiting for transfers between devices, shards(): lax.all_gather(w_in_x, 'seq', axis=0, tiled=True)  34.4 us
    unnamed x1, blocking collectives  27.9 us
    all_to_all x1, blocking collectives, shards(): lax.all_to_all(send_tok.reshape(n_exp, slot_most, -1), 'exp', split_axis=...  22.8 us
  transfers between devices with their start and end apart: 9, of which 6 were waited for; matrix products, arithmetic and copies ran while one was open for 6% of the time, Pallas kernels for 0%

commit v1 on v0

v1 whole, which is shorter than its diff:
```python
import functools

import jax
import jax.numpy as jnp
from jax import lax
from jax.experimental import pallas as pl
from jax.experimental.pallas import tpu as pltpu
from jax.sharding import PartitionSpec as P

F32 = jnp.float32
BF16 = jnp.bfloat16
MOST = 3


def exchange(x, axis):
    return lax.all_to_all(x, axis, split_axis=0, concat_axis=0, tiled=True)


def spread(x, axis):
    n = lax.axis_size(axis)
    return exchange(jnp.broadcast_to(x[None], (n,) + x.shape), axis)


def normalize(values, gain):
    wide = values.astype(F32)
    scale = lax.rsqrt(jnp.mean(wide * wide, axis=-1, keepdims=True) + 1e-05)
    return (wide * scale * gain).astype(BF16)


def softplus(v):
    return jnp.maximum(v, 0.0) + jnp.log1p(jnp.exp(-jnp.abs(v)))


def scan_kernel(low_ref, wdt_ref, bias_ref, alog_ref, act_ref, b_ref, c_ref, out_ref, cum_ref, state_ref, step_s, drive_s):
    tokens = low_ref.shape[0]
    step = softplus(jnp.dot(low_ref[...], wdt_ref[...], preferred_element_type=F32) + bias_ref[...])
    step_s[...] = step
    drive_s[...] = step * act_ref[...].astype(F32)
    decay = -jnp.exp(alog_ref[...])
    states, channels = decay.shape
    state = jnp.zeros((states, channels), F32)
    total = jnp.zeros((1, channels), F32)
    for t in range(tokens):
        step_t = step_s[t : t + 1, :]
        b_t = jnp.broadcast_to(b_ref[:, t : t + 1], (states, channels))
        c_t = jnp.broadcast_to(c_ref[:, t : t + 1], (states, channels))
        state = jnp.exp(step_t * decay) * state + drive_s[t : t + 1, :] * b_t
        total = total + step_t
        out_ref[t : t + 1, :] = jnp.sum(c_t * state, axis=0, keepdims=True)
        cum_ref[t : t + 1, :] = total
    state_ref[...] = state


def gate_kernel(me_ref, all_ref, alog_ref, c_ref, cum_ref, local_ref, act_ref, skip_ref, z_ref, out_ref, corr_s):
    tokens = cum_ref.shape[0]
    decay = -jnp.exp(alog_ref[...])
    states, channels = decay.shape
    state = jnp.zeros((states, channels), F32)
    me = me_ref[0]
    for k in range(all_ref.shape[0] - 1):
        total = all_ref[k, states : states + 1, :]
        later = jnp.exp(total * decay) * state + all_ref[k, 0:states, :]
        state = jnp.where(k < me, later, state)
    for t in range(tokens):
        c_t = jnp.broadcast_to(c_ref[:, t : t + 1], (states, channels))
        term = c_t * (jnp.exp(cum_ref[t : t + 1, :] * decay) * state)
        corr_s[t : t + 1, :] = jnp.sum(term, axis=0, keepdims=True)
    z = z_ref[...].astype(F32)
    ssm = local_ref[...] + corr_s[...] + skip_ref[...] * act_ref[...].astype(F32)
    out_ref[...] = (ssm * (z / (1.0 + jnp.exp(-z)))).astype(BF16)


def shards(
    x_in,
    norm_gain,
    w_in_x,
    w_in_z,
    conv_weight,
    conv_bias,
    w_xproj,
    w_dt,
    dt_bias,
    a_log,
    d_skip,
    w_out,
    moe_gain,
    route_ids,
    route_weights,
    w_gate,
):
    n_seq, n_exp, n_hid = (lax.axis_size(a) for a in ("seq", "exp", "hid"))
    at_seq, at_exp, at_hid = (lax.axis_index(a) for a in ("seq", "exp", "hid"))
    rows, width = x_in.shape
    tokens = rows * n_exp * n_hid
    channels = w_in_x.shape[1]
    states = a_log.shape[0]
    rank = w_dt.shape[0]
    block = rows * n_hid
    half = width // n_hid // 2

    w_in = lax.all_gather(jnp.concatenate([w_in_x, w_in_z], 1), "seq", axis=0, tiled=True)
    route = []
    for s in range(n_seq):
        for h in range(n_hid):
            per = n_seq // n_hid
            route.append((s * n_hid + h, (h * per + s % per) * n_hid + s // per))
    w_out_here = lax.ppermute(w_out, ("seq", "hid"), route)
    swap = [(i, i ^ 1) for i in range(n_seq)]
    w_mine = w_gate[0].reshape(n_hid, 2, half, -1)
    core = at_seq % 2
    w_keep = lax.dynamic_index_in_dim(w_mine, core, 1, keepdims=False)
    w_other = lax.ppermute(lax.dynamic_index_in_dim(w_mine, 1 - core, 1, keepdims=False), "seq", swap)

    routes = jnp.concatenate([route_ids.astype(BF16), route_weights], 1)
    packed = jnp.concatenate([x_in, jnp.pad(routes, ((0, 0), (0, 124)))], 1)
    over_exp = lax.all_gather(packed, "exp", axis=0, tiled=False)
    everything = spread(over_exp, "hid")
    x_all = everything[..., :width]
    routes_all = everything[..., width : width + 4].transpose(1, 0, 2, 3).reshape(n_exp, block, 4).astype(F32)
    normed = normalize(x_all.reshape(tokens, width), norm_gain)
    both = jnp.dot(normed, w_in, preferred_element_type=F32).astype(BF16)
    both = both.reshape(n_hid, n_exp, rows, 2 * channels).transpose(1, 0, 2, 3).reshape(tokens, 2 * channels)
    stream, gate_in = both[:, :channels], both[:, channels:]

    taps = conv_weight.shape[0]
    before = lax.ppermute(stream[tokens - (taps - 1) :], "seq", [(i, i + 1) for i in range(n_seq - 1)])
    padded = jnp.concatenate([before, stream], 0).astype(F32)
    convolved = conv_bias[None] + conv_weight[0] * padded[0:tokens]
    for offset in range(1, taps):
        convolved = convolved + conv_weight[offset] * padded[offset : offset + tokens]
    inner_act = jax.nn.silu(convolved).astype(BF16)

    low_part = jnp.dot(inner_act, w_xproj[:, :rank], preferred_element_type=F32)
    map_part = lax.dot_general(
        w_xproj[:, rank:], inner_act, (((0,), (1,)), ((), ())), preferred_element_type=F32
    )
    low_tiles = low_part.reshape(tokens // 8, 8, rank // 128, 128).transpose(0, 2, 1, 3).reshape(-1, 8, 128)
    map_wide = jnp.pad(map_part, ((0, 0), (0, -tokens % 128)))
    wide = map_wide.shape[1]
    map_tiles = map_wide.reshape(2 * states // 8, 8, wide // 128, 128).transpose(0, 2, 1, 3).reshape(-1, 8, 128)
    n_low, n_map = low_tiles.shape[0], map_tiles.shape[0]
    tiles = jnp.concatenate(
        [low_tiles, map_tiles, jnp.zeros((n_exp * n_hid - n_low - n_map, 8, 128), F32)], 0
    ).astype(BF16)
    got = exchange(tiles, ("exp", "hid"))
    summed = jnp.sum(got.astype(F32), 0).astype(BF16)
    back = spread(summed, ("exp", "hid"))
    step_low = back[:n_low].reshape(tokens // 8, rank // 128, 8, 128).transpose(0, 2, 1, 3).reshape(tokens, rank)
    maps = (
        back[n_low : n_low + n_map]
        .reshape(2 * states // 8, wide // 128, 8, 128)
        .transpose(0, 2, 1, 3)
        .reshape(2 * states, wide)
        .astype(F32)
    )
    input_mat, output_mat = maps[:states], maps[states:]

    local_out, cum, state = pl.pallas_call(
        scan_kernel,
        out_shape=(
            jax.ShapeDtypeStruct((tokens, channels), F32),
            jax.ShapeDtypeStruct((tokens, channels), F32),
            jax.ShapeDtypeStruct((states, channels), F32),
        ),
        scratch_shapes=[pltpu.VMEM((tokens, channels), F32), pltpu.VMEM((tokens, channels), F32)],
        compiler_params=pltpu.CompilerParams(vmem_limit_bytes=32 * 2**20),
        name="scan",
    )(step_low, w_dt, dt_bias[None], a_log, inner_act, input_mat, output_mat)

    rows_ids = routes_all[:, :, :2].reshape(n_exp, -1)
    rows_wts = routes_all[:, :, 2:].reshape(n_exp, -1)
    n_rows = rows_ids.shape[1]
    upto = (jnp.arange(n_rows)[:, None] <= jnp.arange(n_rows)[None, :]).astype(F32)
    named = (rows_ids == at_exp.astype(F32)).astype(F32)
    place = jnp.dot(named, upto) * named
    slot_wts = jnp.stack(
        [jnp.sum(jnp.where(place == i + 1.0, rows_wts, 0.0), 1) for i in range(MOST)], 1
    ).reshape(1, -1)

    carried = jnp.concatenate(
        [
            state,
            cum[tokens - 1 :],
            jnp.pad(slot_wts, ((0, 0), (0, channels - slot_wts.shape[1]))),
            jnp.zeros((6, channels), F32),
        ],
        0,
    )
    carried_all = lax.all_gather(carried, "seq", axis=0, tiled=False)
    weights = carried_all[:, states + 1, : slot_wts.shape[1]].reshape(-1)

    vmem = pl.BlockSpec(memory_space=pltpu.VMEM)
    gated = pl.pallas_call(
        gate_kernel,
        out_shape=jax.ShapeDtypeStruct((tokens, channels), BF16),
        in_specs=[pl.BlockSpec(memory_space=pltpu.SMEM)] + [vmem] * 8,
        out_specs=vmem,
        scratch_shapes=[pltpu.VMEM((tokens, channels), F32)],
        compiler_params=pltpu.CompilerParams(vmem_limit_bytes=32 * 2**20),
        name="gate",
    )(at_seq.astype(jnp.int32)[None], carried_all, a_log, output_mat, cum, local_out, inner_act, d_skip[None], gate_in)

    per = n_seq // n_hid
    w_out_all = lax.all_gather(w_out_here, "seq", axis=0, tiled=False)
    w_out_all = w_out_all.reshape(n_hid, per, channels, -1).transpose(0, 2, 1, 3).reshape(n_hid * channels, -1)
    gated_all = lax.all_gather(gated, "hid", axis=1, tiled=True)
    mixed = jnp.dot(gated_all, w_out_all, preferred_element_type=F32).astype(BF16)
    cols = mixed.shape[1]
    parts = exchange(mixed.reshape(n_exp, block, cols), "exp")
    x_block = lax.dynamic_slice(
        x_all, (0, at_exp, 0, at_hid * cols), (n_hid, 1, rows, cols)
    ).reshape(block, cols)
    resid_part = (x_block.astype(F32) + jnp.sum(parts.astype(F32), 0)).astype(BF16)
    resid_block = lax.all_gather(resid_part, "hid", axis=1, tiled=True)
    resid = lax.dynamic_slice_in_dim(resid_block, at_hid * rows, rows, 0)
    wide_block = resid_block.astype(F32)
    scale = lax.rsqrt(jnp.mean(wide_block * wide_block, axis=-1, keepdims=True) + 1e-05)
    gain = lax.dynamic_slice_in_dim(moe_gain, at_hid * cols, cols, 0)
    moe_in = (resid_part.astype(F32) * scale * gain).astype(BF16)

    ids = lax.dynamic_index_in_dim(rows_ids, at_exp, 0, keepdims=False)
    onehot = (ids[:, None] == jnp.arange(n_exp, dtype=F32)[None, :]).astype(F32)
    position = jnp.sum(jnp.dot(upto.T, onehot) * onehot, 1) - 1.0
    target = ids * MOST + position
    select = (target[None, :] == jnp.arange(n_exp * MOST, dtype=F32)[:, None]).astype(F32)
    select = jnp.sum(select.reshape(n_exp * MOST, block, -1), 2).astype(BF16)
    send = jnp.dot(select, moe_in, preferred_element_type=F32).astype(BF16)
    slots = exchange(send.reshape(n_exp, MOST, cols), "exp").reshape(n_exp * MOST, 2, half)

    halves = jnp.tile(slots.transpose(1, 0, 2), (n_seq // 2, 1, 1))
    seq_slots = exchange(halves, "seq").reshape(-1, half)
    all_slots = spread(seq_slots, "hid")
    dims = (((2,), (1,)), ((0,), (0,)))
    away = jnp.sum(lax.dot_general(all_slots, w_other, dims, preferred_element_type=F32), 0)
    back_here = lax.ppermute(away, "seq", swap)
    home = jnp.sum(lax.dot_general(all_slots, w_keep, dims, preferred_element_type=F32), 0)
    activated = jax.nn.silu(home + back_here) * weights[:, None]
    return (resid, activated.astype(BF16)[None])


def solution(mesh):
    in_specs = (
        P(("seq", "exp", "hid"), None),
        P(),
        P("seq", ("exp", "hid")),
        P("seq", ("exp", "hid")),
        P(None, ("exp", "hid")),
        P(("exp", "hid")),
        P(("exp", "hid"), None),
        P(None, ("exp", "hid")),
        P(("exp", "hid")),
        P(None, ("exp", "hid")),
        P(("exp", "hid")),
        P(("exp", "hid"), "seq"),
        P(),
        P(("seq", "exp", "hid"), None),
        P(("seq", "exp", "hid"), None),
        P("exp", None, ("seq", "hid")),
    )
    out_specs = (P(("seq", "exp", "hid"), None), P("exp", None, ("seq", "hid")))
    return jax.shard_map(shards, mesh=mesh, in_specs=in_specs, out_specs=out_specs, check_vma=False)
```

time: 916 us -> 301 us (0.33)
  waiting for transfers between devices: 699 us -> 82.4 us
  starting transfers between devices: 9.87 us -> 66.4 us
  blocking collectives: 109 us -> 84.5 us
  other arithmetic: 38.6 us -> 14.3 us
    unnamed x8 -> x2, waiting for transfers between devices: 262 us -> 0.03 us
    psum x1 -> x0, waiting for transfers between devices: 253 us -> none  [shards(): lax.psum(jnp.dot(inner_act, w_xproj, preferred_element_type=jnp.float32),...]
    all_gather x5 -> x2, waiting for transfers between devices: 173 us -> 0.04 us  [the longest x1 0.02 us: shards(): lax.all_gather(jnp.concatenate([w_in_x, w_in_z], 1), 'seq', axis=0, tiled...]
    all_to_all x1 -> x6, waiting for transfers between devices: 9.3 us -> 81.4 us  [exchange(): return lax.all_to_all(x, axis, split_axis=0, concat_axis=0, tiled=True)]
    all_to_all x1 -> x6, starting transfers between devices: 7.67 us -> 41.8 us  [exchange(): return lax.all_to_all(x, axis, split_axis=0, concat_axis=0, tiled=True)]
    unnamed x1 -> x0, blocking collectives: 27.9 us -> none
    ppermute x1 -> x4, starting transfers between devices: 1.92 us -> 24.5 us  [the longest x1 13.1 us: shards(): lax.ppermute(stream[tokens - (taps - 1):], 'seq', [(i, i + 1) for i in ra...]
    another operation x13 -> x1, other arithmetic: 11.2 us -> 0.01 us  [shards(): jnp.stack([jnp.sum(jnp.where(place == i + 1.0, rows_wts, 0.0), 1) for i i...]
  transfers between devices with their start and end apart: 9 -> 12, of which waited for: 6 -> 7; matrix products, arithmetic and copies ran while one was open for 6% -> 13% of each run, Pallas kernels for 0% -> 0%
where the time goes in v1:
time: 301 us; the launch traced here: 300 us
  blocking collectives  84.5 us (28%)
  waiting for transfers between devices  82.4 us (27%)
  starting transfers between devices  66.4 us (22%)
  local copies, waits for them, and re-layouts  25.3 us (8%)
  between operations  14.5 us (5%)
  other arithmetic  14.3 us (5%)
  matrix products  10.5 us (3%)
    all_to_all x6, waiting for transfers between devices, exchange(): return lax.all_to_all(x, axis, split_axis=0, concat_axis=0, tiled=True)  81.4 us
    all_to_all x6, starting transfers between devices, exchange(): return lax.all_to_all(x, axis, split_axis=0, concat_axis=0, tiled=True)  41.8 us
    all_gather x1, blocking collectives, shards(): over_exp = lax.all_gather(packed, 'exp', axis=0, tiled=False)  33.1 us
    all_to_all x1, blocking collectives, exchange(): return lax.all_to_all(x, axis, split_axis=0, concat_axis=0, tiled=True)  17 us
    all_gather x1, blocking collectives, shards(): carried_all = lax.all_gather(carried, 'seq', axis=0, tiled=False)  16.1 us
    ppermute x1, starting transfers between devices, shards(): lax.ppermute(stream[tokens - (taps - 1):], 'seq', [(i, i + 1) for i in ra...  13.1 us
    all_gather x1, blocking collectives, shards(): resid_block = lax.all_gather(resid_part, 'hid', axis=1, tiled=True)  9.51 us
    convert_element_type x2, local copies, waits for them, and re-layouts, normalize(): wide = values.astype(F32)  9.22 us
  transfers between devices with their start and end apart: 12, of which 7 were waited for; matrix products, arithmetic and copies ran while one was open for 13% of the time, Pallas kernels for 0%

profile of v1, /device:TPU:1, one launch (start us, length us, event | category | flops | bytes accessed | tf_op | source)
XLA Modules:
  0.0 300.0 jit_solution(12739644815169187785)
XLA Ops:
  11.3 33.1 %all-gather.3 = bf16[16,3,4224]{2,1,0:T(4,128)(2,1)S(1)} all-gather(bf16[1,3,4224]{2,1,0:T(4,128)(2,1)S(1)} %fusion.20), channel_id=2, replica_groups=mesh['seq'=8,'exp'=16,'hid'=4] {'exp'}, dimensions={0}, use_global_device_ids=true | all-gather | bytes 430848 | tf_op jit(solution)/shard_map/all_gather | solution.py:116
  45.8 4.5 %all-to-all-start = ((bf16[4,16,3,4224]{3,1,2,0:T(8,128)(2,1)}), bf16[4,16,3,4224]{3,1,2,0:T(8,128)(2,1)}, u32[]{:S(2)}, u32[]{:S(2)}) async-start(bf16[4,16,3,4224]{3,1,2,0:T(8,128)(2,1)} %broadcast_in_dim.24), calls=%async_computation | async-start | bytes 3244032 | tf_op jit(solution)/shard_map/all_to_all | solution.py:16
  51.8 12.6 %all-to-all-done = bf16[4,16,3,4224]{3,1,2,0:T(8,128)(2,1)} async-done(((bf16[4,16,3,4224]{3,1,2,0:T(8,128)(2,1)}), bf16[4,16,3,4224]{3,1,2,0:T(8,128)(2,1)}, u32[]{:S(2)}, u32[]{:S(2)}) %all-to-all-start) | async-done | bytes 1622048 | tf_op jit(solution)/shard_map/all_to_all | solution.py:16
  64.4 3.0 %slice_convert_fusion = (f32[4,16,3,4096]{3,1,2,0:T(8,128)S(1)}, bf16[4,16,3,4096]{3,1,2,0:T(8,128)(2,1)}) fusion(bf16[4,16,3,4224]{3,1,2,0:T(8,128)(2,1)} %all-to-all-done), kind=kLoop, calls=%fused_computation.83 | loop fusion | flops 786432 | bytes 6291456 | tf_op jit(solution)/shard_map/convert_element_type | solution.py:25
  67.4 4.1 %copy.90 = f32[4,16,3,4096]{3,2,1,0:T(4,128)} copy(f32[4,16,3,4096]{3,1,2,0:T(8,128)S(1)} %get-tuple-element.11) | data formatting | bytes 6291456 | tf_op jit(solution)/shard_map/convert_element_type | solution.py:25
  71.5 5.1 %reshape.145 = f32[192,4096]{1,0:T(8,128)} reshape(f32[4,16,3,4096]{3,2,1,0:T(4,128)} %copy.90) | data formatting | bytes 6291456 | tf_op jit(solution)/shard_map/convert_element_type | solution.py:25
  78.8 3.2 %fusion.9 = bf16[192,256]{1,0:T(8,128)(2,1)S(1)} fusion(bf16[4096,256]{1,0:T(8,128)(2,1)} %all-gather.7.cloned.1.call-done, f32[192,4096]{1,0:T(8,128)} %reshape.145, f32[4096]{0:T(1024)S(1)} %copy-done.8, f32[192]{0:T(256)S(1)} %rsqrt.20), kind=kOutput, calls=%fused_computation.12 | convolution fusion | flops 405061632 | bytes 5358336 | tf_op jit(solution)/shard_map/dot_general | solution.py:121
  82.1 13.1 %collective-permute-start = (bf16[3,128]{1,0:T(4,128)(2,1)S(1)}, bf16[3,128]{1,0:T(4,128)(2,1)S(1)}, u32[]{:S(2)}, u32[]{:S(2)}) collective-permute-start(bf16[3,128]{1,0:T(4,128)(2,1)S(1)} %slice.102), channel_id=1, source_target_pairs={{0,64},{64,128},{128,192},{192,256},{256,320},{320,384},{384,448},... | collective-permute-start | bytes 2312 | tf_op jit(solution)/shard_map/ppermute | solution.py:126
  97.5 11.8 %all-to-all-start.1 = ((bf16[64,8,128]{2,1,0:T(8,128)(2,1)}), bf16[64,8,128]{2,1,0:T(8,128)(2,1)S(1)}, u32[]{:S(2)}, u32[]{:S(2)}) async-start(bf16[64,8,128]{2,1,0:T(8,128)(2,1)} %maximum_maximum_fusion), calls=%async_computation.1 | async-start | bytes 262144 | tf_op jit(solution)/shard_map/all_to_all | solution.py:16
  109.4 16.5 %all-to-all-done.1 = bf16[64,8,128]{2,1,0:T(8,128)(2,1)S(1)} async-done(((bf16[64,8,128]{2,1,0:T(8,128)(2,1)}), bf16[64,8,128]{2,1,0:T(8,128)(2,1)S(1)}, u32[]{:S(2)}, u32[]{:S(2)}) %all-to-all-start.1) | async-done | bytes 131104 | tf_op jit(solution)/shard_map/all_to_all | solution.py:16
  126.6 5.0 %all-to-all-start.2 = ((bf16[64,8,128]{2,1,0:T(8,128)(2,1)}), bf16[64,8,128]{2,1,0:T(8,128)(2,1)S(1)}, u32[]{:S(2)}, u32[]{:S(2)}) async-start(bf16[64,8,128]{2,1,0:T(8,128)(2,1)} %broadcast_in_dim.27), calls=%async_computation.2 | async-start | bytes 262144 | tf_op jit(solution)/shard_map/all_to_all | solution.py:16
  136.8 9.8 %all-to-all-done.2 = bf16[64,8,128]{2,1,0:T(8,128)(2,1)S(1)} async-done(((bf16[64,8,128]{2,1,0:T(8,128)(2,1)}), bf16[64,8,128]{2,1,0:T(8,128)(2,1)S(1)}, u32[]{:S(2)}, u32[]{:S(2)}) %all-to-all-start.2) | async-done | bytes 131104 | tf_op jit(solution)/shard_map/all_to_all | solution.py:16
  147.9 16.1 %all-gather.1 = f32[192,128]{1,0:T(8,128)S(1)} all-gather(f32[24,128]{1,0:T(8,128)S(1)} %fusion.24), channel_id=3, replica_groups=mesh['seq'=8,'exp'=16,'hid'=4] {'seq'}, dimensions={0}, use_global_device_ids=true | all-gather | bytes 110592 | tf_op jit(solution)/shard_map/all_gather | solution.py:189
  164.8 8.8 %all_gather.32 = bf16[192,512]{1,0:T(8,128)(2,1)S(1)} all-gather(bf16[192,128]{1,0:T(8,128)(2,1)S(1)} %gate.1), channel_id=1, replica_groups=mesh['seq'=8,'exp'=16,'hid'=4] {'hid'}, dimensions={1}, use_global_device_ids=true | all-gather | bytes 245760 | tf_op jit(solution)/shard_map/all_gather | solution.py:206
  176.6 4.2 %all-to-all-start.3 = ((bf16[16,12,1024]{2,1,0:T(8,128)(2,1)}), bf16[16,12,1024]{2,1,0:T(8,128)(2,1)}, u32[]{:S(2)}, u32[]{:S(2)}) async-start(bf16[16,12,1024]{2,1,0:T(8,128)(2,1)} %reshape.141), calls=%async_computation.3 | async-start | bytes 1048576 | tf_op jit(solution)/shard_map/all_to_all | solution.py:16
  183.5 19.1 %all-to-all-done.3 = bf16[16,12,1024]{2,1,0:T(8,128)(2,1)} async-done(((bf16[16,12,1024]{2,1,0:T(8,128)(2,1)}), bf16[16,12,1024]{2,1,0:T(8,128)(2,1)}, u32[]{:S(2)}, u32[]{:S(2)}) %all-to-all-start.3) | async-done | bytes 393248 | tf_op jit(solution)/shard_map/all_to_all | solution.py:16
  203.8 9.5 %all_gather.35 = bf16[12,4096]{1,0:T(8,128)(2,1)S(1)} all-gather(bf16[12,1024]{1,0:T(8,128)(2,1)S(1)} %add_convert_fusion), channel_id=1, replica_groups=mesh['seq'=8,'exp'=16,'hid'=4] {'hid'}, dimensions={1}, use_global_device_ids=true | all-gather | bytes 122880 | tf_op jit(solution)/shard_map/all_gather | solution.py:214
  214.5 12.0 %all-to-all-start.4 = ((bf16[16,3,1024]{2,1,0:T(4,128)(2,1)}), bf16[16,3,1024]{2,1,0:T(4,128)(2,1)S(1)}, u32[]{:S(2)}, u32[]{:S(2)}) async-start(bf16[16,3,1024]{2,1,0:T(4,128)(2,1)} %reshape.142), calls=%async_computation.4 | async-start | bytes 262144 | tf_op jit(solution)/shard_map/all_to_all | solution.py:16
  227.8 7.1 %collective-permute-start.2 = (bf16[4,512,384]{2,1,0:T(8,128)(2,1)}, bf16[4,512,384]{2,1,0:T(8,128)(2,1)}, u32[]{:S(2)}, u32[]{:S(2)}) collective-permute-start(bf16[4,512,384]{2,1,0:T(8,128)(2,1)} %dynamic-slice_bitcast_fusion), channel_id=1, source_target_pairs={{0,64},{64,0},{128,192},{192,128},{256,320},{320,256},{384,448},{4... | collective-permute-start | bytes 4718600 | tf_op jit(solution)/shard_map/ppermute | solution.py:112
  234.9 3.6 %all-to-all-done.4 = bf16[16,3,1024]{2,1,0:T(4,128)(2,1)S(1)} async-done(((bf16[16,3,1024]{2,1,0:T(4,128)(2,1)}), bf16[16,3,1024]{2,1,0:T(4,128)(2,1)S(1)}, u32[]{:S(2)}, u32[]{:S(2)}) %all-to-all-start.4) | async-done | bytes 98336 | tf_op jit(solution)/shard_map/all_to_all | solution.py:16
  240.1 17.0 %all_to_all.35 = bf16[8,48,512]{2,1,0:T(8,128)(2,1)S(1)} all-to-all(bf16[8,48,512]{2,1,0:T(8,128)(2,1)S(1)} %bitcast.94), channel_id=1, replica_groups=mesh['seq'=8,'exp'=16,'hid'=4] {'seq'}, dimensions={0} | all-to-all | bytes 786432 | tf_op jit(solution)/shard_map/all_to_all | solution.py:16
  258.4 4.4 %all-to-all-start.6 = ((bf16[4,384,512]{2,1,0:T(8,128)(2,1)}), bf16[4,384,512]{2,1,0:T(8,128)(2,1)}, u32[]{:S(2)}, u32[]{:S(2)}) async-start(bf16[4,384,512]{2,1,0:T(8,128)(2,1)} %broadcast_in_dim.60), calls=%async_computation.6 | async-start | bytes 3145728 | tf_op jit(solution)/shard_map/all_to_all | solution.py:16
  262.8 19.8 %all-to-all-done.6 = bf16[4,384,512]{2,1,0:T(8,128)(2,1)} async-done(((bf16[4,384,512]{2,1,0:T(8,128)(2,1)}), bf16[4,384,512]{2,1,0:T(8,128)(2,1)}, u32[]{:S(2)}, u32[]{:S(2)}) %all-to-all-start.6) | async-done | bytes 1572896 | tf_op jit(solution)/shard_map/all_to_all | solution.py:16
  285.5 3.7 %collective-permute-start.3 = (f32[384,384]{1,0:T(8,128)S(1)}, f32[384,384]{1,0:T(8,128)S(1)}, u32[]{:S(2)}, u32[]{:S(2)}) collective-permute-start(f32[384,384]{1,0:T(8,128)S(1)} %convolution_bitcast_fusion), channel_id=1, source_target_pairs={{0,64},{64,0},{128,192},{192,128},{256,320},{320,256},{384,448},{4... | collective-permute-start | bytes 1769480 | tf_op jit(solution)/shard_map/ppermute | solution.py:235
  (112 shorter events, 38.5 us)
Async XLA Ops:
  7.2 219.3 %copy-start = (bf16[1,4096,384]{2,1,0:T(8,128)(2,1)S(1)}, bf16[1,4096,384]{2,1,0:T(8,128)(2,1)}, u32[]{:S(2)}) copy-start(bf16[1,4096,384]{2,1,0:T(8,128)(2,1)} %param.31) | copy-start | bytes 9437188
  7.2 71.6 %all-gather.7.cloned.1.call-start = ((), (), s32[]{:S(2)}) async-start(), calls=%async_computation.7 | async-start | bytes 2359296 | tf_op jit(solution)/shard_map/all_gather | solution.py:101
  45.8 4.5 %copy-start.11 = (bf16[128,512]{1,0:T(8,128)(2,1)S(1)}, bf16[128,512]{1,0:T(8,128)(2,1)}, u32[]{:S(2)}) copy-start(bf16[128,512]{1,0:T(8,128)(2,1)} %param.27) | copy-start | bytes 393220
  45.8 5.3 %copy-start.9 = (f32[4,128]{1,0:T(4,128)S(1)}, f32[4,128]{1,0:T(4,128)}, u32[]{:S(2)}) copy-start(f32[4,128]{1,0:T(4,128)} %param.20) | copy-start | bytes 6148
  45.8 18.6 %all-to-all-start = ((bf16[4,16,3,4224]{3,1,2,0:T(8,128)(2,1)}), bf16[4,16,3,4224]{3,1,2,0:T(8,128)(2,1)}, u32[]{:S(2)}, u32[]{:S(2)}) async-start(bf16[4,16,3,4224]{3,1,2,0:T(8,128)(2,1)} %broadcast_in_dim.24), calls=%async_computation | async-start | bytes 3244032 | tf_op jit(solution)/shard_map/all_to_all | solution.py:16
  50.3 82.9 %all-gather.9.cloned.1.call-start = ((), (), s32[]{:S(2)}) async-start(), calls=%async_computation.8 | async-start | bytes 1179648 | tf_op jit(solution)/shard_map/all_gather | solution.py:204
  50.4 0.8 collective-permute-start.1
  51.1 0.6 copy-start.6
  76.6 2.1 copy-start.8
  78.7 17.5 %copy-start.10 = (f32[128]{0:T(128)S(1)}, f32[128]{0:T(128)}, u32[]{:S(2)}) copy-start(f32[128]{0:T(128)} %param.21) | copy-start | bytes 1540
  78.7 17.6 %copy-start.7 = (bf16[128,288]{0,1:T(8,128)(2,1)S(1)}, bf16[128,288]{0,1:T(8,128)(2,1)}, u32[]{:S(2)}) copy-start(bf16[128,288]{0,1:T(8,128)(2,1)} %param.22) | copy-start | bytes 221188
  82.1 14.0 %collective-permute-start = (bf16[3,128]{1,0:T(4,128)(2,1)S(1)}, bf16[3,128]{1,0:T(4,128)(2,1)S(1)}, u32[]{:S(2)}, u32[]{:S(2)}) collective-permute-start(bf16[3,128]{1,0:T(4,128)(2,1)S(1)} %slice.102), channel_id=1, source_target_pairs={{0,64},{64,128},{128,192},{192,256},{256,320},{320,384},{384,448},... | collective-permute-start | bytes 2312 | tf_op jit(solution)/shard_map/ppermute | solution.py:126
  97.5 28.4 %all-to-all-start.1 = ((bf16[64,8,128]{2,1,0:T(8,128)(2,1)}), bf16[64,8,128]{2,1,0:T(8,128)(2,1)S(1)}, u32[]{:S(2)}, u32[]{:S(2)}) async-start(bf16[64,8,128]{2,1,0:T(8,128)(2,1)} %maximum_maximum_fusion), calls=%async_computation.1 | async-start | bytes 262144 | tf_op jit(solution)/shard_map/all_to_all | solution.py:16
  126.6 20.0 %all-to-all-start.2 = ((bf16[64,8,128]{2,1,0:T(8,128)(2,1)}), bf16[64,8,128]{2,1,0:T(8,128)(2,1)S(1)}, u32[]{:S(2)}, u32[]{:S(2)}) async-start(bf16[64,8,128]{2,1,0:T(8,128)(2,1)} %broadcast_in_dim.27), calls=%async_computation.2 | async-start | bytes 262144 | tf_op jit(solution)/shard_map/all_to_all | solution.py:16
  135.5 11.1 %copy-start.1 = (bf16[256,128]{1,0:T(8,128)(2,1)S(1)}, bf16[256,128]{1,0:T(8,128)(2,1)}, u32[]{:S(2)}) copy-start(bf16[256,128]{1,0:T(8,128)(2,1)} %wdt_ref.1) | copy-start | bytes 196612
  135.5 11.1 %copy-start.2 = (f32[16,128]{1,0:T(8,128)S(1)}, f32[16,128]{1,0:T(8,128)}, u32[]{:S(2)}) copy-start(f32[16,128]{1,0:T(8,128)} %alog_ref.3) | copy-start | bytes 24580
  135.5 11.1 %copy-start.3 = (f32[128]{0:T(128)S(1)}, f32[128]{0:T(128)}, u32[]{:S(2)}) copy-start(f32[128]{0:T(128)} %param.24) | copy-start | bytes 1540
  135.5 28.5 %copy-start.4 = (f32[128]{0:T(128)S(1)}, f32[128]{0:T(128)}, u32[]{:S(2)}) copy-start(f32[128]{0:T(128)} %param.26) | copy-start | bytes 1540
  146.6 27.0 %copy-start.5 = (bf16[64,8,2,512]{3,1,2,0:T(8,128)(2,1)S(1)}, bf16[64,8,2,512]{3,1,2,0:T(8,128)(2,1)}, u32[]{:S(2)}) copy-start(bf16[64,8,2,512]{3,1,2,0:T(8,128)(2,1)} %copy.111) | copy-start | bytes 3145732
  176.6 26.1 %all-to-all-start.3 = ((bf16[16,12,1024]{2,1,0:T(8,128)(2,1)}), bf16[16,12,1024]{2,1,0:T(8,128)(2,1)}, u32[]{:S(2)}, u32[]{:S(2)}) async-start(bf16[16,12,1024]{2,1,0:T(8,128)(2,1)} %reshape.141), calls=%async_computation.3 | async-start | bytes 1048576 | tf_op jit(solution)/shard_map/all_to_all | solution.py:16
  214.5 24.0 %all-to-all-start.4 = ((bf16[16,3,1024]{2,1,0:T(4,128)(2,1)}), bf16[16,3,1024]{2,1,0:T(4,128)(2,1)S(1)}, u32[]{:S(2)}, u32[]{:S(2)}) async-start(bf16[16,3,1024]{2,1,0:T(4,128)(2,1)} %reshape.142), calls=%async_computation.4 | async-start | bytes 262144 | tf_op jit(solution)/shard_map/all_to_all | solution.py:16
  227.8 35.1 %collective-permute-start.2 = (bf16[4,512,384]{2,1,0:T(8,128)(2,1)}, bf16[4,512,384]{2,1,0:T(8,128)(2,1)}, u32[]{:S(2)}, u32[]{:S(2)}) collective-permute-start(bf16[4,512,384]{2,1,0:T(8,128)(2,1)} %dynamic-slice_bitcast_fusion), channel_id=1, source_target_pairs={{0,64},{64,0},{128,192},{192,128},{256,320},{320,256},{384,448},{4... | collective-permute-start | bytes 4718600 | tf_op jit(solution)/shard_map/ppermute | solution.py:112
  258.4 24.3 %all-to-all-start.6 = ((bf16[4,384,512]{2,1,0:T(8,128)(2,1)}), bf16[4,384,512]{2,1,0:T(8,128)(2,1)}, u32[]{:S(2)}, u32[]{:S(2)}) async-start(bf16[4,384,512]{2,1,0:T(8,128)(2,1)} %broadcast_in_dim.60), calls=%async_computation.6 | async-start | bytes 3145728 | tf_op jit(solution)/shard_map/all_to_all | solution.py:16
  285.5 6.7 %collective-permute-start.3 = (f32[384,384]{1,0:T(8,128)S(1)}, f32[384,384]{1,0:T(8,128)S(1)}, u32[]{:S(2)}, u32[]{:S(2)}) collective-permute-start(f32[384,384]{1,0:T(8,128)S(1)} %convolution_bitcast_fusion), channel_id=1, source_target_pairs={{0,64},{64,0},{128,192},{192,128},{256,320},{320,256},{384,448},{4... | collective-permute-start | bytes 1769480 | tf_op jit(solution)/shard_map/ppermute | solution.py:235
Sparse Core Ops, SparseCore 0:
  10.7 38.5 all-gather.6
  53.3 49.0 all-gather.8

commit v2 on v1

v2 whole, which is shorter than its diff:
```python
import jax
import jax.numpy as jnp
from jax import lax
from jax.experimental import pallas as pl
from jax.experimental.pallas import tpu as pltpu
from jax.sharding import PartitionSpec as P

F32 = jnp.float32
BF16 = jnp.bfloat16
MOST = 3
STATES = 16
CONV = 4
TAPS, BIAS, STEP, SKIP = 16, 20, 21, 22


def exchange(x, axis):
    return lax.all_to_all(x, axis, split_axis=0, concat_axis=0, tiled=True)


def softplus(v):
    return jnp.maximum(v, 0.0) + jnp.log1p(jnp.exp(-jnp.abs(v)))


def silu(v):
    return v / (1.0 + jnp.exp(-v))


def call(body, name, out_shape, scratch, *args, scalars=0, unread=0, more=(), limit=40):
    vmem, smem = pl.BlockSpec(memory_space=pltpu.VMEM), pl.BlockSpec(memory_space=pltpu.SMEM)
    return pl.pallas_call(
        body,
        out_shape=out_shape,
        in_specs=[smem] * scalars
        + [vmem] * (len(args) - scalars - unread)
        + [pl.BlockSpec(memory_space=pl.ANY)] * unread,
        out_specs=jax.tree.map(lambda _: vmem, out_shape),
        scratch_shapes=[pltpu.VMEM(shape, F32) for shape in scratch] + list(more),
        compiler_params=pltpu.CompilerParams(vmem_limit_bytes=limit * 2**20),
        name=name,
    )(*args)


def like(shape, dtype):
    return jax.ShapeDtypeStruct(shape, dtype)


def rows_kernel(x_ref, out_ref, rows_s):
    groups, rows, wide = x_ref.shape
    width = wide - 128
    for g in range(groups):
        rows_s[g * rows : (g + 1) * rows, :] = x_ref[g].astype(F32)
    x = rows_s[:, 0:width]
    scale = lax.rsqrt(jnp.mean(x * x, axis=-1, keepdims=True) + 1e-05)
    first = scale.astype(BF16).astype(F32)
    second = (scale - first).astype(BF16).astype(F32)
    more = rows_s[:, width:]
    lane = lax.broadcasted_iota(jnp.int32, more.shape, 1)
    for at, value in enumerate((first, second, scale - first - second)):
        more = jnp.where(lane == 4 + at, value, more)
    rows_s[:, width:] = more
    packed = rows_s[...].astype(BF16)
    for h in range(out_ref.shape[0]):
        out_ref[h] = packed


def project_kernel(x_ref, gain_ref, w_ref, both_ref, tail_ref, route_ref, wide_s, w_s, sem):
    copy = pltpu.make_async_copy(w_ref, w_s, sem)
    copy.start()
    quarters, part, wide = x_ref.shape
    width, both = w_s.shape
    channels = both // 2
    rows = MOST
    groups = part // rows
    block = quarters * rows
    normed = []
    for h in range(quarters):
        more = x_ref[h, :, width:].astype(F32)
        scale = more[:, 4:5] + more[:, 5:6] + more[:, 6:7]
        normed.append((x_ref[h, :, 0:width].astype(F32) * scale * gain_ref[...]).astype(BF16))
        wide_s[2, h * part : (h + 1) * part, :] = more
    copy.wait()
    product = jnp.dot(jnp.concatenate(normed, 0), w_s[...], preferred_element_type=F32)
    wide_s[0] = product[:, :channels]
    wide_s[1] = product[:, channels:]
    for h in range(quarters):
        for r in range(rows):
            source, target = pl.ds(h * part + r, groups, stride=rows), pl.ds(h * rows + r, groups, stride=block)
            for k in range(3):
                wide_s[3 + k, target, :] = wide_s[k, source, :]
    both_ref[0] = wide_s[3].astype(BF16)
    both_ref[1] = wide_s[4].astype(BF16)
    tail_ref[...] = wide_s[3, quarters * part - 8 :, :].astype(BF16).astype(F32)
    route_ref[...] = wide_s[5]


def conv_kernel(stream_ref, halo_ref, params_ref, wx_ref, act_ref, tile_ref, pad_s):
    _, tokens, channels = stream_ref.shape
    pad_s[0:8, :] = halo_ref[...]
    pad_s[8:, :] = stream_ref[0].astype(F32)
    conv = params_ref[BIAS : BIAS + 1, :] + jnp.zeros((tokens, channels), F32)
    for k in range(CONV):
        at = 8 - (CONV - 1) + k
        conv = conv + params_ref[TAPS + k : TAPS + k + 1, :] * pad_s[at : at + tokens, :]
    act = silu(conv).astype(BF16)
    act_ref[...] = act
    rank = wx_ref.shape[1] - 2 * STATES
    low = jnp.dot(act, wx_ref[:, :rank], preferred_element_type=F32)
    maps = lax.dot_general(wx_ref[:, rank:], act, (((0,), (1,)), ((), ())), preferred_element_type=F32)
    n = 0
    for t in range(0, tokens, 8):
        for c in range(0, rank, 128):
            tile_ref[n] = low[t : t + 8, c : c + 128].astype(BF16)
            n += 1
    for s in range(0, 32, 8):
        tile_ref[n] = maps[s : s + 8, 0:128].astype(BF16)
        tile_ref[n + 1] = jnp.concatenate(
            [maps[s : s + 8, 128:tokens], jnp.zeros((8, 256 - tokens), F32)], 1
        ).astype(BF16)
        n += 2
    while n < tile_ref.shape[0]:
        tile_ref[n] = jnp.zeros((8, 128), BF16)
        n += 1


def tile_sum_kernel(got_ref, out_ref):
    total = jnp.sum(got_ref[...].astype(F32), axis=0).astype(BF16)
    out_ref[...] = jnp.broadcast_to(total[None], out_ref.shape)


def scan_kernel(
    back_ref, wdt_ref, params_ref, act_ref, wts_ref, out_ref, cum_ref, c_ref, send_ref, low_s, step_s, drive_s
):
    tokens, rank = low_s.shape
    n = 0
    for t in range(0, tokens, 8):
        for c in range(0, rank, 128):
            low_s[t : t + 8, c : c + 128] = back_ref[n].astype(F32)
            n += 1
    maps = []
    for s in range(0, 32, 8):
        maps.append(jnp.concatenate([back_ref[n].astype(F32), back_ref[n + 1].astype(F32)], 1))
        n += 2
    decay = -jnp.exp(params_ref[0:STATES, :])
    states, channels = decay.shape
    b = jnp.concatenate(maps[:2], 0)
    c = jnp.concatenate(maps[2:], 0)
    c_ref[...] = c
    step = softplus(jnp.dot(low_s[...].astype(BF16), wdt_ref[...], preferred_element_type=F32) + params_ref[STEP : STEP + 1, :])
    step_s[...] = step
    drive_s[...] = step * act_ref[...].astype(F32)
    state = jnp.zeros((states, channels), F32)
    total = jnp.zeros((1, channels), F32)
    for t in range(tokens):
        step_t = step_s[t : t + 1, :]
        b_t = jnp.broadcast_to(b[:, t : t + 1], (states, channels))
        c_t = jnp.broadcast_to(c[:, t : t + 1], (states, channels))
        state = jnp.exp(step_t * decay) * state + drive_s[t : t + 1, :] * b_t
        total = total + step_t
        out_ref[t : t + 1, :] = jnp.sum(c_t * state, axis=0, keepdims=True)
        cum_ref[t : t + 1, :] = total
    row = lax.broadcasted_iota(jnp.int32, (8, channels), 0)
    tail = jnp.where(row == 0, total, jnp.where(row == 1, wts_ref[...], 0.0))
    for k in range(send_ref.shape[0]):
        send_ref[k, 0:states, :] = state
        send_ref[k, states:, :] = tail


def gate_kernel(me_ref, all_ref, params_ref, c_ref, cum_ref, local_ref, act_ref, z_ref, out_ref, corr_s):
    tokens = cum_ref.shape[0]
    decay = -jnp.exp(params_ref[0:STATES, :])
    states, channels = decay.shape
    state = jnp.zeros((states, channels), F32)
    me = me_ref[0]
    for k in range(all_ref.shape[0] - 1):
        total = all_ref[k, states : states + 1, :]
        later = jnp.exp(total * decay) * state + all_ref[k, 0:states, :]
        state = jnp.where(k < me, later, state)
    for t in range(tokens):
        c_t = jnp.broadcast_to(c_ref[:, t : t + 1], (states, channels))
        term = c_t * (jnp.exp(cum_ref[t : t + 1, :] * decay) * state)
        corr_s[t : t + 1, :] = jnp.sum(term, axis=0, keepdims=True)
    z = z_ref[1].astype(F32)
    ssm = local_ref[...] + corr_s[...] + params_ref[SKIP : SKIP + 1, :] * act_ref[...].astype(F32)
    gated = (ssm * silu(z)).astype(BF16)
    for h in range(out_ref.shape[0]):
        out_ref[h] = gated


def mix_kernel(gated_ref, w_ref, out_ref, mixed_s):
    quarters = gated_ref.shape[0]
    per = w_ref.shape[0] // quarters
    cols = w_ref.shape[2]
    for b in range(per):
        total = jnp.dot(gated_ref[0], w_ref[b], preferred_element_type=F32)
        for h in range(1, quarters):
            total = total + jnp.dot(gated_ref[h], w_ref[h * per + b], preferred_element_type=F32)
        mixed_s[:, b * cols : (b + 1) * cols] = total
    block = out_ref.shape[1]
    for j in range(out_ref.shape[0]):
        out_ref[j] = mixed_s[j * block : (j + 1) * block, :].astype(BF16)


def resid_kernel(parts_ref, x_ref, select_ref, resid_ref, send_ref, wide_s):
    block = resid_ref.shape[0]
    total = x_ref[...].astype(F32) + jnp.sum(parts_ref[...].astype(F32), axis=0)
    resid = total.astype(BF16)
    resid_ref[...] = resid
    wide_s[...] = jnp.zeros_like(wide_s)
    wide_s[0:block, :] = resid.astype(F32)
    send = jnp.dot(select_ref[...], wide_s[...].astype(BF16), preferred_element_type=F32)
    most = send_ref.shape[1]
    for e in range(send_ref.shape[0]):
        send_ref[e] = send[e * most : (e + 1) * most].astype(BF16)


def expert_kernel(me_ref, tok_ref, gain_ref, resid_ref, w0_ref, w1_ref, w2_ref, w3_ref, out_ref, w_s, sems):
    me = me_ref[0]
    slots, cols = tok_ref.shape
    quarters = out_ref.shape[0]
    hidden = w_s.shape[1] // quarters
    copies = []
    for d, w_ref in enumerate((w0_ref.at[0, pl.ds(pl.multiple_of(me * cols, cols), cols)], w1_ref, w2_ref, w3_ref)):
        copies.append(pltpu.make_async_copy(w_ref, w_s.at[:, pl.ds(d * hidden, hidden)], sems.at[d]))
        copies[d].start()
    tok = tok_ref[...].astype(F32)
    square = tok * tok
    high = square.astype(BF16)
    low = (square - high.astype(F32)).astype(BF16)
    ones = jnp.ones((16, cols), BF16)
    dims = (((1,), (1,)), ((), ()))
    sums = lax.dot_general(ones, high, dims, preferred_element_type=F32)
    sums = sums + lax.dot_general(ones, low, dims, preferred_element_type=F32)
    first = sums.astype(BF16).astype(F32)
    second = (sums - first).astype(BF16).astype(F32)
    third = sums - first - second
    row = lax.broadcasted_iota(jnp.int32, (16, slots), 0)
    scales = jnp.where(row == 0, first, jnp.where(row == 1, second, third)).astype(BF16)
    resid = resid_ref[...].astype(F32)
    rows = resid.shape[0] // quarters
    for h in range(quarters):
        out_ref[h, slots : slots + 16, :] = scales
        pieces = []
        for r in range(rows):
            own = resid[h * rows + r : h * rows + r + 1, :]
            pieces.append(own[:, 0:hidden])
            pieces.append(own[:, hidden : 2 * hidden])
            pieces.append(jnp.concatenate([own[:, 2 * hidden :], jnp.zeros((1, 3 * hidden - cols), F32)], 1))
        pieces.append(jnp.zeros((16 - len(pieces), hidden), F32))
        out_ref[h, slots + 16 :, :] = jnp.concatenate(pieces, 0).astype(BF16)
    tok = (tok * gain_ref[...]).astype(BF16)
    for d in range(0, quarters, 2):
        copies[d].wait()
        copies[d + 1].wait()
        pair = jnp.dot(tok, w_s[:, d * hidden : (d + 2) * hidden], preferred_element_type=F32).astype(BF16)
        for i in range(2):
            out_ref[lax.rem(me - d - i + quarters, quarters), 0:slots, :] = pair[:, i * hidden : (i + 1) * hidden]


def finish_kernel(part_ref, wts_ref, out_ref, resid_ref, resid_s):
    quarters, _, hidden = part_ref.shape
    slots = out_ref.shape[0]
    rows, width = resid_ref.shape
    cols = width // quarters
    total = jnp.zeros((slots, hidden), F32)
    squares = jnp.zeros((1, slots), F32)
    for q in range(quarters):
        total = total + part_ref[q, 0:slots, :].astype(F32)
        parts = part_ref[q, slots : slots + 16, :].astype(F32)
        squares = squares + (parts[0:1] + parts[1:2] + parts[2:3])
        own = part_ref[q, slots + 16 :, :].astype(F32)
        for r in range(rows):
            for m in range(3):
                size = min(hidden, cols - m * hidden)
                at = q * cols + m * hidden
                resid_s[r : r + 1, at : at + size] = own[3 * r + m : 3 * r + m + 1, 0:size]
    resid_ref[...] = resid_s[0:rows, :].astype(BF16)
    row = lax.broadcasted_iota(jnp.int32, (8, slots), 0)
    scale = lax.rsqrt(squares / width + 1e-05)
    both = jnp.where(row == 0, scale, wts_ref[...]).T
    out_ref[...] = (silu(total * both[:, 0:1]) * both[:, 1:2]).astype(BF16)


def shards(
    x_in,
    norm_gain,
    w_in_x,
    w_in_z,
    conv_weight,
    conv_bias,
    w_xproj,
    w_dt,
    dt_bias,
    a_log,
    d_skip,
    w_out,
    moe_gain,
    route_ids,
    route_weights,
    w_gate,
):
    n_seq, n_exp, n_hid = (lax.axis_size(a) for a in ("seq", "exp", "hid"))
    at_seq, at_exp, at_hid = (lax.axis_index(a) for a in ("seq", "exp", "hid"))
    rows, width = x_in.shape
    tokens = rows * n_exp * n_hid
    channels = w_in_x.shape[1]
    states = a_log.shape[0]
    rank = w_dt.shape[0]
    block = rows * n_hid
    cols = width // n_hid
    per = n_seq // n_hid

    w_in = lax.all_gather(jnp.concatenate([w_in_x, w_in_z], 1), "seq", axis=0, tiled=True)

    own_routes = jnp.concatenate([route_ids.astype(BF16), route_weights], 1)
    own = jnp.concatenate([x_in, jnp.pad(own_routes, ((0, 0), (0, 124)))], 1)
    over_exp = lax.all_gather(own, "exp", axis=0, tiled=False)
    quarter_rows = call(
        rows_kernel,
        "rows",
        like((n_hid, n_exp * rows, width + 128), BF16),
        [(n_exp * rows, width + 128)],
        over_exp,
    )
    quarter_rows, w_out = lax.optimization_barrier((quarter_rows, w_out))
    route = [
        (s * n_hid + h, (h * per + s % per) * n_hid + s // per) for s in range(n_seq) for h in range(n_hid)
    ]
    w_out_here = lax.ppermute(w_out, ("seq", "hid"), route)
    w_out_all = lax.all_gather(w_out_here, "seq", axis=0, tiled=False)
    params = jnp.concatenate(
        [a_log, conv_weight, conv_bias[None], dt_bias[None], d_skip[None], jnp.zeros((1, channels), F32)], 0
    )
    all_rows = exchange(quarter_rows, "hid")
    x_block = lax.dynamic_slice(
        all_rows.reshape(n_hid, n_exp, rows, -1), (0, at_exp, 0, at_hid * cols), (n_hid, 1, rows, cols)
    ).reshape(block, cols)
    both, tail, routes = call(
        project_kernel,
        "project",
        (like((2, tokens, channels), BF16), like((8, channels), F32), like((tokens, 128), F32)),
        [(6, tokens, 128)],
        all_rows,
        norm_gain[None],
        w_in,
        unread=1,
        more=[pltpu.VMEM(w_in.shape, BF16), pltpu.SemaphoreType.DMA],
        limit=58,
    )
    halo = lax.ppermute(tail, "seq", [(i, i + 1) for i in range(n_seq - 1)])
    inner_act, tiles = call(
        conv_kernel,
        "conv",
        (like((tokens, channels), BF16), like((n_exp * n_hid, 8, 128), BF16)),
        [(tokens + 8, channels)],
        both,
        halo,
        params,
        w_xproj,
    )

    got = exchange(tiles, ("exp", "hid"))
    back = exchange(call(tile_sum_kernel, "tile_sum", like(got.shape, BF16), [], got), ("exp", "hid"))

    rows_ids = routes[:, :2].reshape(n_exp, -1)
    rows_wts = routes[:, 2:4].reshape(n_exp, -1)
    n_rows = rows_ids.shape[1]
    upto = (jnp.arange(n_rows)[:, None] <= jnp.arange(n_rows)[None, :]).astype(F32)
    named = (rows_ids == at_exp.astype(F32)).astype(F32)
    place = jnp.dot(named, upto) * named
    slot_wts = jnp.stack(
        [jnp.sum(jnp.where(place == i + 1.0, rows_wts, 0.0), 1) for i in range(MOST)], 1
    ).reshape(1, -1)
    n_slots = slot_wts.shape[1]
    ids = lax.dynamic_index_in_dim(rows_ids, at_exp, 0, keepdims=False)
    onehot = (ids[:, None] == jnp.arange(n_exp, dtype=F32)[None, :]).astype(F32)
    position = jnp.sum(jnp.dot(upto.T, onehot) * onehot, 1) - 1.0
    target = ids * MOST + position
    select = (target[None, :] == jnp.arange(n_exp * MOST, dtype=F32)[:, None]).astype(F32)
    select = jnp.sum(select.reshape(n_exp * MOST, block, -1), 2)
    select = jnp.pad(select, ((0, 0), (0, 16 - block))).astype(BF16)

    local_out, cum, output_mat, carried = call(
        scan_kernel,
        "scan",
        (
            like((tokens, channels), F32),
            like((tokens, channels), F32),
            like((states, 256), F32),
            like((n_seq, states + 8, channels), F32),
        ),
        [(tokens, rank), (tokens, channels), (tokens, channels)],
        back,
        w_dt,
        params,
        inner_act,
        jnp.pad(slot_wts, ((0, 0), (0, channels - n_slots))),
    )
    carried_all = exchange(carried, "seq")
    weights = carried_all[:, states + 1, :n_slots].reshape(1, -1)
    gated = call(
        gate_kernel,
        "gate",
        like((n_hid, tokens, channels), BF16),
        [(tokens, channels)],
        at_seq.astype(jnp.int32)[None],
        carried_all,
        params,
        output_mat,
        cum,
        local_out,
        inner_act,
        both,
        scalars=1,
    )

    gated_all = exchange(gated, "hid")
    mixed = call(mix_kernel, "mix", like((n_exp, block, cols), BF16), [(tokens, cols)], gated_all, w_out_all)
    mixed, w_gate = lax.optimization_barrier((mixed, w_gate))
    w_quarters = w_gate[0].reshape(n_hid, cols, -1)

    def shift(d):
        out = lax.dynamic_index_in_dim(w_quarters, (at_hid + d) % n_hid, 0, keepdims=False)
        return lax.ppermute(out, "hid", [(i, (i + d) % n_hid) for i in range(n_hid)])

    w_1, w_2, w_3 = shift(1), shift(2), shift(3)
    sums = exchange(mixed, "exp")
    resid_part, send = call(
        resid_kernel,
        "resid",
        (like((block, cols), BF16), like((n_exp, MOST, cols), BF16)),
        [(16, cols)],
        sums,
        x_block,
        select,
    )

    slots = exchange(send, "exp").reshape(n_exp * MOST, cols)
    all_slots = lax.all_gather(slots, "seq", axis=0, tiled=True)
    n_all, hidden = all_slots.shape[0], w_gate.shape[2]
    away = call(
        expert_kernel,
        "expert",
        like((n_hid, n_all + 32, hidden), BF16),
        [],
        at_hid.astype(jnp.int32)[None],
        all_slots,
        lax.dynamic_slice_in_dim(moe_gain, at_hid * cols, cols, 0)[None],
        resid_part,
        w_gate,
        w_1,
        w_2,
        w_3,
        scalars=1,
        unread=4,
        more=[pltpu.VMEM((cols, n_hid * hidden), BF16), pltpu.SemaphoreType.DMA((n_hid,))],
        limit=58,
    )
    home = exchange(away, "hid")
    activated, resid = call(
        finish_kernel,
        "finish",
        (like((n_all, hidden), BF16), like((rows, width), BF16)),
        [(8, width)],
        home,
        weights,
    )
    return (resid, activated[None])


def solution(mesh):
    in_specs = (
        P(("seq", "exp", "hid"), None),
        P(),
        P("seq", ("exp", "hid")),
        P("seq", ("exp", "hid")),
        P(None, ("exp", "hid")),
        P(("exp", "hid")),
        P(("exp", "hid"), None),
        P(None, ("exp", "hid")),
        P(("exp", "hid")),
        P(None, ("exp", "hid")),
        P(("exp", "hid")),
        P(("exp", "hid"), "seq"),
        P(),
        P(("seq", "exp", "hid"), None),
        P(("seq", "exp", "hid"), None),
        P("exp", None, ("seq", "hid")),
    )
    out_specs = (P(("seq", "exp", "hid"), None), P("exp", None, ("seq", "hid")))
    return jax.shard_map(shards, mesh=mesh, in_specs=in_specs, out_specs=out_specs, check_vma=False)
```

time: 301 us -> 268 us (0.89)
  Pallas kernels: 1.95 us -> 19.1 us
  local copies, waits for them, and re-layouts: 25.3 us -> 13.1 us
  other arithmetic: 14.3 us -> 3.96 us
  matrix products: 10.5 us -> 0.42 us
  waiting for transfers between devices: 82.4 us -> 74.6 us
  starting transfers between devices: 66.4 us -> 61.1 us
  blocking collectives: 84.5 us -> 79.7 us
    pallas_call x2 -> x10, Pallas kernels: 1.95 us -> 19.1 us  [call(): pl.pallas_call(body, out_shape=out_shape, in_specs=[smem] * scalars + [vm...]
    all_gather x4 -> x2, blocking collectives: 67.6 us -> 51 us  [the longest x1 33.1 us: shards(): over_exp = lax.all_gather(own, 'exp', axis=0, tiled=False)]
    all_to_all x1, blocking collectives: 17 us -> 28.7 us  [exchange(): return lax.all_to_all(x, axis, split_axis=0, concat_axis=0, tiled=True)]
    dot_general x7 -> x0, matrix products: 10.1 us -> none  [the longest x1 3.17 us: shards(): both = jnp.dot(normed, w_in, preferred_element_type=F32).astype(BF16)]
    convert_element_type x4 -> x0, local copies, waits for them, and re-layouts: 9.38 us -> none  [the longest x2 9.22 us: normalize(): wide = values.astype(F32)]
    all_to_all x6 -> x7, waiting for transfers between devices: 81.4 us -> 73.7 us  [exchange(): return lax.all_to_all(x, axis, split_axis=0, concat_axis=0, tiled=True)]
    reshape x8 -> x4, local copies, waits for them, and re-layouts: 5.92 us -> 0.28 us  [the longest x1 0.09 us: shards(): rows_wts = routes[:, 2:4].reshape(n_exp, -1)]
    convert_element_type x8 -> x1, other arithmetic: 5.75 us -> 0.68 us  [shards(): own_routes = jnp.concatenate([route_ids.astype(BF16), route_weights], 1)]
  transfers between devices with their start and end apart: 12 -> 14, of which waited for: 7 -> 8; matrix products, arithmetic and copies ran while one was open for 13% -> 4% of each run, Pallas kernels for 0% -> 4%
where the time goes in v2:
time: 268 us; the launch traced here: 266 us
  blocking collectives  79.7 us (30%)
  waiting for transfers between devices  74.6 us (28%)
  starting transfers between devices  61.1 us (23%)
  Pallas kernels  19.1 us (7%)
  between operations  14.4 us (5%)
  local copies, waits for them, and re-layouts  13.1 us (5%)
  other arithmetic  3.96 us (1%)
    all_to_all x7, waiting for transfers between devices, exchange(): return lax.all_to_all(x, axis, split_axis=0, concat_axis=0, tiled=True)  73.7 us
    all_to_all x7, starting transfers between devices, exchange(): return lax.all_to_all(x, axis, split_axis=0, concat_axis=0, tiled=True)  38.4 us
    all_gather x1, blocking collectives, shards(): over_exp = lax.all_gather(own, 'exp', axis=0, tiled=False)  33.1 us
    all_to_all x1, blocking collectives, exchange(): return lax.all_to_all(x, axis, split_axis=0, concat_axis=0, tiled=True)  28.7 us
    pallas_call x10, Pallas kernels, call(): pl.pallas_call(body, out_shape=out_shape, in_specs=[smem] * scalars + [vm...  19.1 us
    all_gather x1, blocking collectives, shards(): all_slots = lax.all_gather(slots, 'seq', axis=0, tiled=True)  17.9 us
    ppermute x1, starting transfers between devices, shards(): halo = lax.ppermute(tail, 'seq', [(i, i + 1) for i in range(n_seq - 1)])  13.5 us
    ppermute x3, starting transfers between devices, shift(): lax.ppermute(out, 'hid', [(i, (i + d) % n_hid) for i in range(n_hid)])  8.43 us
  transfers between devices with their start and end apart: 14, of which 8 were waited for; matrix products, arithmetic and copies ran while one was open for 4% of the time, Pallas kernels for 4%

profile of v2, /device:TPU:1, one launch (start us, length us, event | category | flops | bytes accessed | tf_op | source)
XLA Modules:
  0.0 266.4 jit_solution(14104119348442776723)
XLA Ops:
  11.2 33.1 %all-gather.2.x_ref = bf16[16,3,4224]{2,1,0:T(4,128)(2,1)S(1)} all-gather(bf16[1,3,4224]{2,1,0:T(4,128)(2,1)S(1)} %fusion.3), channel_id=2, replica_groups=mesh['seq'=8,'exp'=16,'hid'=4] {'exp'}, dimensions={0}, use_global_device_ids=true | all-gather | bytes 430848 | tf_op jit(solution)/shard_map/all_gather | solution.py:316
  45.8 4.1 %all-to-all-start = ((bf16[4,48,4224]{2,1,0:T(8,128)(2,1)}), bf16[4,48,4224]{2,1,0:T(8,128)(2,1)S(1)}, u32[]{:S(2)}, u32[]{:S(2)}) async-start(bf16[4,48,4224]{2,1,0:T(8,128)(2,1)} %rows.1), calls=%async_computation | async-start | bytes 3244032 | tf_op jit(solution)/shard_map/all_to_all | solution.py:17
  51.3 12.4 %all-to-all-done.x_ref = bf16[4,48,4224]{2,1,0:T(8,128)(2,1)S(1)} async-done(((bf16[4,48,4224]{2,1,0:T(8,128)(2,1)}), bf16[4,48,4224]{2,1,0:T(8,128)(2,1)S(1)}, u32[]{:S(2)}, u32[]{:S(2)}) %all-to-all-start) | async-done | bytes 1622048 | tf_op jit(solution)/shard_map/all_to_all | solution.py:17
  64.9 4.4 %project.1 = (bf16[2,192,128]{2,1,0:T(8,128)(2,1)}, f32[8,128]{1,0:T(8,128)}, f32[192,128]{1,0:T(8,128)}) custom-call(bf16[4,48,4224]{2,1,0:T(8,128)(2,1)} %copy-done.5, f32[1,4096]{1,0:T(1,128)} %bitcast.34, bf16[4096,256]{1,0:T(8,128)(2,1)} %all-gather.6.cloned.1.call-done.w_ref), custom_call_target="tpu_custom_call" | custom-call | tf_op jit(solution)/shard_map/project/pallas_call | solution.py:30
  69.4 13.5 %collective-permute-start = (f32[8,128]{1,0:T(8,128)}, f32[8,128]{1,0:T(8,128)S(1)}, u32[]{:S(2)}, u32[]{:S(2)}) collective-permute-start(f32[8,128]{1,0:T(8,128)} %get-tuple-element.21), channel_id=1, source_target_pairs={{0,64},{64,128},{128,192},{192,256},{256,320},{320,384},{384,448},... | collective-permute-start | bytes 12296 | tf_op jit(solution)/shard_map/ppermute | solution.py:349
  85.1 28.7 %all_to_all.40.got_ref = bf16[64,8,128]{2,1,0:T(8,128)(2,1)S(1)} all-to-all(bf16[64,8,128]{2,1,0:T(8,128)(2,1)S(1)} %get-tuple-element.22), channel_id=1, replica_groups=mesh['seq'=8,'exp'=16,'hid'=4] {'exp','hid'}, dimensions={0} | all-to-all | bytes 262144 | tf_op jit(solution)/shard_map/all_to_all | solution.py:17
  114.5 4.7 %all-to-all-start.2 = ((bf16[64,8,128]{2,1,0:T(8,128)(2,1)}), bf16[64,8,128]{2,1,0:T(8,128)(2,1)S(1)}, u32[]{:S(2)}, u32[]{:S(2)}) async-start(bf16[64,8,128]{2,1,0:T(8,128)(2,1)} %tile_sum.1), calls=%async_computation.2 | async-start | bytes 262144 | tf_op jit(solution)/shard_map/all_to_all | solution.py:17
  121.0 13.4 %all-to-all-done.2.back_ref = bf16[64,8,128]{2,1,0:T(8,128)(2,1)S(1)} async-done(((bf16[64,8,128]{2,1,0:T(8,128)(2,1)}), bf16[64,8,128]{2,1,0:T(8,128)(2,1)S(1)}, u32[]{:S(2)}, u32[]{:S(2)}) %all-to-all-start.2) | async-done | bytes 131104 | tf_op jit(solution)/shard_map/all_to_all | solution.py:17
  135.9 6.7 %all-to-all-start.3 = ((f32[8,24,128]{2,1,0:T(8,128)}), f32[8,24,128]{2,1,0:T(8,128)S(1)}, u32[]{:S(2)}, u32[]{:S(2)}) async-start(f32[8,24,128]{2,1,0:T(8,128)} %get-tuple-element.25), calls=%async_computation.3 | async-start | bytes 196608 | tf_op jit(solution)/shard_map/all_to_all | solution.py:17
  142.7 5.0 %all-to-all-done.3.all_ref = f32[8,24,128]{2,1,0:T(8,128)S(1)} async-done(((f32[8,24,128]{2,1,0:T(8,128)}), f32[8,24,128]{2,1,0:T(8,128)S(1)}, u32[]{:S(2)}, u32[]{:S(2)}) %all-to-all-start.3) | async-done | bytes 98336 | tf_op jit(solution)/shard_map/all_to_all | solution.py:17
  149.1 3.4 %all-to-all-start.4 = ((bf16[4,192,128]{2,1,0:T(8,128)(2,1)}), bf16[4,192,128]{2,1,0:T(8,128)(2,1)S(1)}, u32[]{:S(2)}, u32[]{:S(2)}) async-start(bf16[4,192,128]{2,1,0:T(8,128)(2,1)} %gate.1), calls=%async_computation.4 | async-start | bytes 393216 | tf_op jit(solution)/shard_map/all_to_all | solution.py:17
  152.5 5.1 %all-to-all-done.4.gated_ref = bf16[4,192,128]{2,1,0:T(8,128)(2,1)S(1)} async-done(((bf16[4,192,128]{2,1,0:T(8,128)(2,1)}), bf16[4,192,128]{2,1,0:T(8,128)(2,1)S(1)}, u32[]{:S(2)}, u32[]{:S(2)}) %all-to-all-start.4) | async-done | bytes 196640 | tf_op jit(solution)/shard_map/all_to_all | solution.py:17
  160.3 3.6 %all-to-all-start.5 = ((bf16[16,12,1024]{2,1,0:T(8,128)(2,1)}), bf16[16,12,1024]{2,1,0:T(8,128)(2,1)S(1)}, u32[]{:S(2)}, u32[]{:S(2)}) async-start(bf16[16,12,1024]{2,1,0:T(8,128)(2,1)} %mix.1), calls=%async_computation.5 | async-start | bytes 1048576 | tf_op jit(solution)/shard_map/all_to_all | solution.py:17
  164.9 3.1 %dynamic-slice_bitcast_fusion = (bf16[1024,384]{1,0:T(8,128)(2,1)}, bf16[1024,384]{1,0:T(8,128)(2,1)}, bf16[1024,384]{1,0:T(8,128)(2,1)}) fusion(bf16[4,1024,384]{2,1,0:T(8,128)(2,1)} %bitcast.31, s32[]{:T(128)S(6)} %select_n.57, s32[]{:T(128)S(6)} %select_n.55, s32[]{:T(128)S(6)} %select_n.53), kind=kLoop, calls=%fused_computation.3 | loop fusion | bytes 4718604 | tf_op jit(solution)/shard_map/jit(dynamic_index_in_dim)/squeeze | solution.py:422
  168.0 2.2 collective-permute-start.2
  170.2 3.7 %collective-permute-start.3 = (bf16[1024,384]{1,0:T(8,128)(2,1)}, bf16[1024,384]{1,0:T(8,128)(2,1)S(1)}, u32[]{:S(2)}, u32[]{:S(2)}) collective-permute-start(bf16[1024,384]{1,0:T(8,128)(2,1)} %get-tuple-element.40), channel_id=1, source_target_pairs={{0,2},{1,3},{2,0},{3,1},{4,6},{5,7},{6,4},{7,5},{8,10},{9,11},{10,... | collective-permute-start | bytes 2359304 | tf_op jit(solution)/shard_map/ppermute | solution.py:423
  173.9 2.6 collective-permute-start.4
  176.7 9.7 %all-to-all-done.5.parts_ref = bf16[16,12,1024]{2,1,0:T(8,128)(2,1)S(1)} async-done(((bf16[16,12,1024]{2,1,0:T(8,128)(2,1)}), bf16[16,12,1024]{2,1,0:T(8,128)(2,1)S(1)}, u32[]{:S(2)}, u32[]{:S(2)}) %all-to-all-start.5) | async-done | bytes 393248 | tf_op jit(solution)/shard_map/all_to_all | solution.py:17
  187.9 12.4 %all-to-all-start.6 = ((bf16[16,3,1024]{2,1,0:T(4,128)(2,1)}), bf16[16,3,1024]{2,1,0:T(4,128)(2,1)S(1)}, u32[]{:S(2)}, u32[]{:S(2)}) async-start(bf16[16,3,1024]{2,1,0:T(4,128)(2,1)} %get-tuple-element.31), calls=%async_computation.6 | async-start | bytes 262144 | tf_op jit(solution)/shard_map/all_to_all | solution.py:17
  201.6 10.7 %all-to-all-done.6 = bf16[16,3,1024]{2,1,0:T(4,128)(2,1)S(1)} async-done(((bf16[16,3,1024]{2,1,0:T(4,128)(2,1)}), bf16[16,3,1024]{2,1,0:T(4,128)(2,1)S(1)}, u32[]{:S(2)}, u32[]{:S(2)}) %all-to-all-start.6) | async-done | bytes 98336 | tf_op jit(solution)/shard_map/all_to_all | solution.py:17
  212.3 17.9 %all_gather.23.tok_ref = bf16[384,1024]{1,0:T(8,128)(2,1)} all-gather(bf16[48,1024]{1,0:T(8,128)(2,1)S(1)} %reshape.47), channel_id=1, replica_groups=mesh['seq'=8,'exp'=16,'hid'=4] {'seq'}, dimensions={0}, use_global_device_ids=true | all-gather | bytes 884736 | tf_op jit(solution)/shard_map/all_gather | solution.py:438
  231.6 5.7 %expert.1 = bf16[4,416,384]{2,1,0:T(8,128)(2,1)} custom-call(s32[1]{0:T(128)} %bitcast.me_ref, bf16[384,1024]{1,0:T(8,128)(2,1)} %all_gather.23.tok_ref, f32[1,1024]{1,0:T(1,128)} %bitcast.33, bf16[12,1024]{1,0:T(8,128)(2,1)} %copy-done.4, bf16[1,4096,384]{2,1,0:T(8,128)(2,1)} %w0_ref, bf16[1024,384]{1,0:T(8,128)(2,1)} %copy-done.7, ...), custom_call_target="tpu_custom_call" | custom-call | tf_op jit(solution)/shard_map/expert/pallas_call | solution.py:30
  237.3 3.5 %all-to-all-start.7 = ((bf16[4,416,384]{2,1,0:T(8,128)(2,1)}), bf16[4,416,384]{2,1,0:T(8,128)(2,1)S(1)}, u32[]{:S(2)}, u32[]{:S(2)}) async-start(bf16[4,416,384]{2,1,0:T(8,128)(2,1)} %expert.1), calls=%async_computation.7 | async-start | bytes 2555904 | tf_op jit(solution)/shard_map/all_to_all | solution.py:17
  240.9 17.4 %all-to-all-done.7.part_ref = bf16[4,416,384]{2,1,0:T(8,128)(2,1)S(1)} async-done(((bf16[4,416,384]{2,1,0:T(8,128)(2,1)}), bf16[4,416,384]{2,1,0:T(8,128)(2,1)S(1)}, u32[]{:S(2)}, u32[]{:S(2)}) %all-to-all-start.7) | async-done | bytes 1277984 | tf_op jit(solution)/shard_map/all_to_all | solution.py:17
  (87 shorter events, 25.0 us)
Async XLA Ops:
  7.2 56.6 %all-gather.6.cloned.1.call-start = ((), (), s32[]{:S(2)}) async-start(), calls=%async_computation.8 | async-start | bytes 2359296 | tf_op jit(solution)/shard_map/all_gather | solution.py:312
  45.8 4.2 %copy-start.17 = (bf16[128,512]{1,0:T(8,128)(2,1)S(1)}, bf16[128,512]{1,0:T(8,128)(2,1)}, u32[]{:S(2)}) copy-start(bf16[128,512]{1,0:T(8,128)(2,1)} %param.27) | copy-start | bytes 393220
  45.8 17.9 %all-to-all-start = ((bf16[4,48,4224]{2,1,0:T(8,128)(2,1)}), bf16[4,48,4224]{2,1,0:T(8,128)(2,1)S(1)}, u32[]{:S(2)}, u32[]{:S(2)}) async-start(bf16[4,48,4224]{2,1,0:T(8,128)(2,1)} %rows.1), calls=%async_computation | async-start | bytes 3244032 | tf_op jit(solution)/shard_map/all_to_all | solution.py:17
  50.0 102.5 %all-gather.8.cloned.1.call-start = ((), (), s32[]{:S(2)}) async-start(), calls=%async_computation.9 | async-start | bytes 1179648 | tf_op jit(solution)/shard_map/all_gather | solution.py:329
  50.0 0.7 collective-permute-start.1
  64.9 18.0 %copy-start.11 = (bf16[128,288]{0,1:T(8,128)(2,1)S(1)}, bf16[128,288]{0,1:T(8,128)(2,1)}, u32[]{:S(2)}) copy-start(bf16[128,288]{0,1:T(8,128)(2,1)} %param.22) | copy-start | bytes 221188
  64.9 18.2 %copy-start.12 = (f32[16,128]{1,0:T(8,128)S(1)}, f32[16,128]{1,0:T(8,128)}, u32[]{:S(2)}) copy-start(f32[16,128]{1,0:T(8,128)} %param.25) | copy-start | bytes 24580
  64.9 18.2 %copy-start.13 = (f32[4,128]{1,0:T(4,128)S(1)}, f32[4,128]{1,0:T(4,128)}, u32[]{:S(2)}) copy-start(f32[4,128]{1,0:T(4,128)} %param.20) | copy-start | bytes 6148
  64.9 18.2 %copy-start.14 = (f32[128]{0:T(128)S(1)}, f32[128]{0:T(128)}, u32[]{:S(2)}) copy-start(f32[128]{0:T(128)} %param.21) | copy-start | bytes 1540
  64.9 18.2 %copy-start.15 = (f32[128]{0:T(128)S(1)}, f32[128]{0:T(128)}, u32[]{:S(2)}) copy-start(f32[128]{0:T(128)} %param.24) | copy-start | bytes 1540
  64.9 18.2 %copy-start.16 = (f32[128]{0:T(128)S(1)}, f32[128]{0:T(128)}, u32[]{:S(2)}) copy-start(f32[128]{0:T(128)} %param.26) | copy-start | bytes 1540
  69.4 65.0 %copy-start.3 = (bf16[256,128]{1,0:T(8,128)(2,1)S(1)}, bf16[256,128]{1,0:T(8,128)(2,1)}, u32[]{:S(2)}) copy-start(bf16[256,128]{1,0:T(8,128)(2,1)} %wdt_ref.1) | copy-start | bytes 196612
  69.4 78.3 %copy-start.2 = (bf16[2,192,128]{2,1,0:T(8,128)(2,1)S(1)}, bf16[2,192,128]{2,1,0:T(8,128)(2,1)}, u32[]{:S(2)}) copy-start(bf16[2,192,128]{2,1,0:T(8,128)(2,1)} %get-tuple-element.20.stream_ref.z_ref) | copy-start | bytes 294916
  69.4 14.6 %collective-permute-start = (f32[8,128]{1,0:T(8,128)}, f32[8,128]{1,0:T(8,128)S(1)}, u32[]{:S(2)}, u32[]{:S(2)}) collective-permute-start(f32[8,128]{1,0:T(8,128)} %get-tuple-element.21), channel_id=1, source_target_pairs={{0,64},{64,128},{128,192},{192,256},{256,320},{320,384},{384,448},... | collective-permute-start | bytes 12296 | tf_op jit(solution)/shard_map/ppermute | solution.py:349
  114.5 19.8 %all-to-all-start.2 = ((bf16[64,8,128]{2,1,0:T(8,128)(2,1)}), bf16[64,8,128]{2,1,0:T(8,128)(2,1)S(1)}, u32[]{:S(2)}, u32[]{:S(2)}) async-start(bf16[64,8,128]{2,1,0:T(8,128)(2,1)} %tile_sum.1), calls=%async_computation.2 | async-start | bytes 262144 | tf_op jit(solution)/shard_map/all_to_all | solution.py:17
  135.9 11.7 %all-to-all-start.3 = ((f32[8,24,128]{2,1,0:T(8,128)}), f32[8,24,128]{2,1,0:T(8,128)S(1)}, u32[]{:S(2)}, u32[]{:S(2)}) async-start(f32[8,24,128]{2,1,0:T(8,128)} %get-tuple-element.25), calls=%async_computation.3 | async-start | bytes 196608 | tf_op jit(solution)/shard_map/all_to_all | solution.py:17
  149.1 8.5 %all-to-all-start.4 = ((bf16[4,192,128]{2,1,0:T(8,128)(2,1)}), bf16[4,192,128]{2,1,0:T(8,128)(2,1)S(1)}, u32[]{:S(2)}, u32[]{:S(2)}) async-start(bf16[4,192,128]{2,1,0:T(8,128)(2,1)} %gate.1), calls=%async_computation.4 | async-start | bytes 393216 | tf_op jit(solution)/shard_map/all_to_all | solution.py:17
  158.8 5.1 %copy-start.6 = (bf16[4,48,4224]{2,1,0:T(8,128)(2,1)S(1)}, bf16[4,48,4224]{2,1,0:T(8,128)(2,1)}, u32[]{:S(2)}) copy-start(bf16[4,48,4224]{2,1,0:T(8,128)(2,1)} %copy-done.5) | copy-start | bytes 4866052
  160.3 26.1 %all-to-all-start.5 = ((bf16[16,12,1024]{2,1,0:T(8,128)(2,1)}), bf16[16,12,1024]{2,1,0:T(8,128)(2,1)S(1)}, u32[]{:S(2)}, u32[]{:S(2)}) async-start(bf16[16,12,1024]{2,1,0:T(8,128)(2,1)} %mix.1), calls=%async_computation.5 | async-start | bytes 1048576 | tf_op jit(solution)/shard_map/all_to_all | solution.py:17
  168.0 62.2 %collective-permute-start.2 = (bf16[1024,384]{1,0:T(8,128)(2,1)}, bf16[1024,384]{1,0:T(8,128)(2,1)S(1)}, u32[]{:S(2)}, u32[]{:S(2)}) collective-permute-start(bf16[1024,384]{1,0:T(8,128)(2,1)} %get-tuple-element.41), channel_id=1, source_target_pairs={{0,1},{1,2},{2,3},{3,0},{4,5},{5,6},{6,7},{7,4},{8,9},{9,10},{10,1... | collective-permute-start | bytes 2359304 | tf_op jit(solution)/shard_map/ppermute | solution.py:423
  170.2 60.0 %collective-permute-start.3 = (bf16[1024,384]{1,0:T(8,128)(2,1)}, bf16[1024,384]{1,0:T(8,128)(2,1)S(1)}, u32[]{:S(2)}, u32[]{:S(2)}) collective-permute-start(bf16[1024,384]{1,0:T(8,128)(2,1)} %get-tuple-element.40), channel_id=1, source_target_pairs={{0,2},{1,3},{2,0},{3,1},{4,6},{5,7},{6,4},{7,5},{8,10},{9,11},{10,... | collective-permute-start | bytes 2359304 | tf_op jit(solution)/shard_map/ppermute | solution.py:423
  173.9 56.3 %collective-permute-start.4 = (bf16[1024,384]{1,0:T(8,128)(2,1)}, bf16[1024,384]{1,0:T(8,128)(2,1)S(1)}, u32[]{:S(2)}, u32[]{:S(2)}) collective-permute-start(bf16[1024,384]{1,0:T(8,128)(2,1)} %get-tuple-element.39), channel_id=1, source_target_pairs={{0,3},{1,0},{2,1},{3,2},{4,7},{5,4},{6,5},{7,6},{8,11},{9,8},{10,9... | collective-permute-start | bytes 2359304 | tf_op jit(solution)/shard_map/ppermute | solution.py:423
  187.9 24.3 %all-to-all-start.6 = ((bf16[16,3,1024]{2,1,0:T(4,128)(2,1)}), bf16[16,3,1024]{2,1,0:T(4,128)(2,1)S(1)}, u32[]{:S(2)}, u32[]{:S(2)}) async-start(bf16[16,3,1024]{2,1,0:T(4,128)(2,1)} %get-tuple-element.31), calls=%async_computation.6 | async-start | bytes 262144 | tf_op jit(solution)/shard_map/all_to_all | solution.py:17
  237.3 21.1 %all-to-all-start.7 = ((bf16[4,416,384]{2,1,0:T(8,128)(2,1)}), bf16[4,416,384]{2,1,0:T(8,128)(2,1)S(1)}, u32[]{:S(2)}, u32[]{:S(2)}) async-start(bf16[4,416,384]{2,1,0:T(8,128)(2,1)} %expert.1), calls=%async_computation.7 | async-start | bytes 2555904 | tf_op jit(solution)/shard_map/all_to_all | solution.py:17
  (8 other events, 7.9 us)
Sparse Core Ops, SparseCore 0:
  10.7 38.5 all-gather.5
  53.0 49.0 all-gather.7

commit v3 on v2

--- a/solution.py
+++ b/solution.py
@@ -63,40 +63,48 @@
         out_ref[h] = packed
 
 
-def project_kernel(x_ref, gain_ref, w_ref, both_ref, tail_ref, route_ref, wide_s, w_s, sem):
-    copy = pltpu.make_async_copy(w_ref, w_s, sem)
-    copy.start()
-    quarters, part, wide = x_ref.shape
-    width, both = w_s.shape
-    channels = both // 2
-    rows = MOST
-    groups = part // rows
-    block = quarters * rows
-    normed = []
-    for h in range(quarters):
+def normed_rows(x_ref, gain_ref, width):
+    normed, extras = [], []
+    for h in range(x_ref.shape[0]):
         more = x_ref[h, :, width:].astype(F32)
         scale = more[:, 4:5] + more[:, 5:6] + more[:, 6:7]
         normed.append((x_ref[h, :, 0:width].astype(F32) * scale * gain_ref[...]).astype(BF16))
-        wide_s[2, h * part : (h + 1) * part, :] = more
-    copy.wait()
-    product = jnp.dot(jnp.concatenate(normed, 0), w_s[...], preferred_element_type=F32)
-    wide_s[0] = product[:, :channels]
-    wide_s[1] = product[:, channels:]
+        extras.append(more)
+    return jnp.concatenate(normed, 0), extras
+
+
+def in_order(source, target, quarters):
+    part = source.shape[0] // quarters
+    groups = part // MOST
     for h in range(quarters):
-        for r in range(rows):
-            source, target = pl.ds(h * part + r, groups, stride=rows), pl.ds(h * rows + r, groups, stride=block)
-            for k in range(3):
-                wide_s[3 + k, target, :] = wide_s[k, source, :]
-    both_ref[0] = wide_s[3].astype(BF16)
-    both_ref[1] = wide_s[4].astype(BF16)
-    tail_ref[...] = wide_s[3, quarters * part - 8 :, :].astype(BF16).astype(F32)
-    route_ref[...] = wide_s[5]
+        for r in range(MOST):
+            own = source[pl.ds(h * part + r, groups, stride=MOST), :]
+            target[pl.ds(h * MOST + r, groups, stride=quarters * MOST), :] = own
+
+
+def project_kernel(x_ref, gain_ref, w_ref, stream_ref, tail_ref, route_ref, mixed_s, more_s, stream_s):
+    quarters, part, _ = x_ref.shape
+    normed, extras = normed_rows(x_ref, gain_ref, w_ref.shape[0])
+    for h in range(quarters):
+        more_s[h * part : (h + 1) * part, :] = extras[h]
+    mixed_s[...] = jnp.dot(normed, w_ref[...], preferred_element_type=F32)
+    in_order(mixed_s, stream_s, quarters)
+    in_order(more_s, route_ref, quarters)
+    stream_ref[...] = stream_s[...].astype(BF16)
+    tail_ref[...] = stream_s[quarters * part - 8 :, :].astype(BF16).astype(F32)
+
+
+def project_gate_kernel(x_ref, gain_ref, w_ref, gate_ref, mixed_s, gate_s):
+    normed, _ = normed_rows(x_ref, gain_ref, w_ref.shape[0])
+    mixed_s[...] = jnp.dot(normed, w_ref[...], preferred_element_type=F32)
+    in_order(mixed_s, gate_s, x_ref.shape[0])
+    gate_ref[...] = gate_s[...].astype(BF16)
 
 
 def conv_kernel(stream_ref, halo_ref, params_ref, wx_ref, act_ref, tile_ref, pad_s):
-    _, tokens, channels = stream_ref.shape
+    tokens, channels = stream_ref.shape
     pad_s[0:8, :] = halo_ref[...]
-    pad_s[8:, :] = stream_ref[0].astype(F32)
+    pad_s[8:, :] = stream_ref[...].astype(F32)
     conv = params_ref[BIAS : BIAS + 1, :] + jnp.zeros((tokens, channels), F32)
     for k in range(CONV):
         at = 8 - (CONV - 1) + k
@@ -128,7 +136,7 @@
 
 
 def scan_kernel(
-    back_ref, wdt_ref, params_ref, act_ref, wts_ref, out_ref, cum_ref, c_ref, send_ref, low_s, step_s, drive_s
+    back_ref, wdt_ref, params_ref, act_ref, wts_ref, out_ref, send_ref, low_s, step_s, drive_s
 ):
     tokens, rank = low_s.shape
     n = 0
@@ -144,10 +152,12 @@
     states, channels = decay.shape
     b = jnp.concatenate(maps[:2], 0)
     c = jnp.concatenate(maps[2:], 0)
-    c_ref[...] = c
+    out_ref[2 * tokens : 2 * tokens + states, :] = c[:, :channels]
+    out_ref[2 * tokens + states :, :] = c[:, channels:]
     step = softplus(jnp.dot(low_s[...].astype(BF16), wdt_ref[...], preferred_element_type=F32) + params_ref[STEP : STEP + 1, :])
     step_s[...] = step
-    drive_s[...] = step * act_ref[...].astype(F32)
+    act = act_ref[...].astype(F32)
+    drive_s[...] = step * act
     state = jnp.zeros((states, channels), F32)
     total = jnp.zeros((1, channels), F32)
     for t in range(tokens):
@@ -157,7 +167,8 @@
         state = jnp.exp(step_t * decay) * state + drive_s[t : t + 1, :] * b_t
         total = total + step_t
         out_ref[t : t + 1, :] = jnp.sum(c_t * state, axis=0, keepdims=True)
-        cum_ref[t : t + 1, :] = total
+        out_ref[tokens + t : tokens + t + 1, :] = total
+    out_ref[0:tokens, :] = out_ref[0:tokens, :] + params_ref[SKIP : SKIP + 1, :] * act
     row = lax.broadcasted_iota(jnp.int32, (8, channels), 0)
     tail = jnp.where(row == 0, total, jnp.where(row == 1, wts_ref[...], 0.0))
     for k in range(send_ref.shape[0]):
@@ -165,8 +176,8 @@
         send_ref[k, states:, :] = tail
 
 
-def gate_kernel(me_ref, all_ref, params_ref, c_ref, cum_ref, local_ref, act_ref, z_ref, out_ref, corr_s):
-    tokens = cum_ref.shape[0]
+def gate_kernel(me_ref, all_ref, params_ref, local_ref, z_ref, out_ref, corr_s):
+    tokens = z_ref.shape[0]
     decay = -jnp.exp(params_ref[0:STATES, :])
     states, channels = decay.shape
     state = jnp.zeros((states, channels), F32)
@@ -175,18 +186,19 @@
         total = all_ref[k, states : states + 1, :]
         later = jnp.exp(total * decay) * state + all_ref[k, 0:states, :]
         state = jnp.where(k < me, later, state)
+    c = [local_ref[at : at + states, :] for at in (2 * tokens, 2 * tokens + states)]
     for t in range(tokens):
-        c_t = jnp.broadcast_to(c_ref[:, t : t + 1], (states, channels))
-        term = c_t * (jnp.exp(cum_ref[t : t + 1, :] * decay) * state)
+        c_t = jnp.broadcast_to(c[t // channels][:, t % channels : t % channels + 1], (states, channels))
+        term = c_t * (jnp.exp(local_ref[tokens + t : tokens + t + 1, :] * decay) * state)
         corr_s[t : t + 1, :] = jnp.sum(term, axis=0, keepdims=True)
-    z = z_ref[1].astype(F32)
-    ssm = local_ref[...] + corr_s[...] + params_ref[SKIP : SKIP + 1, :] * act_ref[...].astype(F32)
+    z = z_ref[...].astype(F32)
+    ssm = local_ref[0:tokens, :] + corr_s[...]
     gated = (ssm * silu(z)).astype(BF16)
     for h in range(out_ref.shape[0]):
         out_ref[h] = gated
 
 
-def mix_kernel(gated_ref, w_ref, out_ref, mixed_s):
+def mix_kernel(gated_ref, w_ref, _0, _1, out_ref, mixed_s):
     quarters = gated_ref.shape[0]
     per = w_ref.shape[0] // quarters
     cols = w_ref.shape[2]
@@ -195,63 +207,83 @@
         for h in range(1, quarters):
             total = total + jnp.dot(gated_ref[h], w_ref[h * per + b], preferred_element_type=F32)
         mixed_s[:, b * cols : (b + 1) * cols] = total
-    block = out_ref.shape[1]
+    block = mixed_s.shape[0] // out_ref.shape[0]
+    wide = mixed_s.shape[1]
     for j in range(out_ref.shape[0]):
-        out_ref[j] = mixed_s[j * block : (j + 1) * block, :].astype(BF16)
+        own = mixed_s[j * block : (j + 1) * block, :]
+        rest = jnp.concatenate([own[8:, : wide // 2], own[8:, wide // 2 :]], 0)
+        out_ref[j] = jnp.concatenate([own[:8], rest], 1).astype(BF16)
 
 
 def resid_kernel(parts_ref, x_ref, select_ref, resid_ref, send_ref, wide_s):
-    block = resid_ref.shape[0]
-    total = x_ref[...].astype(F32) + jnp.sum(parts_ref[...].astype(F32), axis=0)
+    block, cols = resid_ref.shape
+    sums = jnp.sum(parts_ref[...].astype(F32), axis=0)
+    rest = jnp.concatenate([sums[: block - 8, cols:], sums[block - 8 :, cols:]], 1)
+    total = x_ref[...].astype(F32) + jnp.concatenate([sums[:, :cols], rest], 0)
     resid = total.astype(BF16)
     resid_ref[...] = resid
     wide_s[...] = jnp.zeros_like(wide_s)
     wide_s[0:block, :] = resid.astype(F32)
     send = jnp.dot(select_ref[...], wide_s[...].astype(BF16), preferred_element_type=F32)
-    most = send_ref.shape[1]
     for e in range(send_ref.shape[0]):
-        send_ref[e] = send[e * most : (e + 1) * most].astype(BF16)
-
-
-def expert_kernel(me_ref, tok_ref, gain_ref, resid_ref, w0_ref, w1_ref, w2_ref, w3_ref, out_ref, w_s, sems):
+        own = send[e * MOST : (e + 1) * MOST]
+        rows = [own[:, 0:384], own[:, 384:768]]
+        rows.append(jnp.concatenate([own[0:1, 768:], own[2:3, 768:896]], 1))
+        rows.append(jnp.concatenate([own[1:2, 768:], own[2:3, 896:]], 1))
+        send_ref[e] = jnp.concatenate(rows, 0).astype(BF16)
+
+
+def slots_kernel(got_ref, _0, out_ref, slots_s):
+    for j in range(got_ref.shape[0]):
+        own = got_ref[j].astype(F32)
+        at = j * MOST
+        slots_s[at : at + 3, 0:384] = own[0:3]
+        slots_s[at : at + 3, 384:768] = own[3:6]
+        slots_s[at : at + 1, 768:] = own[6:7, 0:256]
+        slots_s[at + 1 : at + 2, 768:] = own[7:8, 0:256]
+        slots_s[at + 2 : at + 3, 768:] = jnp.concatenate([own[6:7, 256:], own[7:8, 256:]], 1)
+    out_ref[...] = slots_s[...].astype(BF16)
+
+
+def stage_kernel(me_ref, w0_ref, w1_ref, w2_ref, w3_ref, out_ref, sems):
+    cols = out_ref.shape[0]
+    hidden = w1_ref.shape[1]
+    sources = [w0_ref.at[0, pl.ds(pl.multiple_of(me_ref[0] * cols, cols), cols)], w1_ref, w2_ref, w3_ref]
+    copies = []
+    for d, w_ref in enumerate(sources):
+        copies.append(pltpu.make_async_copy(w_ref, out_ref.at[:, pl.ds(d * hidden, hidden)], sems.at[d]))
+        copies[d].start()
+    for copy in copies:
+        copy.wait()
+
+
+def expert_kernel(me_ref, tok_ref, gain_ref, resid_ref, w_ref, out_ref):
     me = me_ref[0]
     slots, cols = tok_ref.shape
     quarters = out_ref.shape[0]
-    hidden = w_s.shape[1] // quarters
-    copies = []
-    for d, w_ref in enumerate((w0_ref.at[0, pl.ds(pl.multiple_of(me * cols, cols), cols)], w1_ref, w2_ref, w3_ref)):
-        copies.append(pltpu.make_async_copy(w_ref, w_s.at[:, pl.ds(d * hidden, hidden)], sems.at[d]))
-        copies[d].start()
+    hidden = w_ref.shape[1] // quarters
     tok = tok_ref[...].astype(F32)
-    square = tok * tok
-    high = square.astype(BF16)
-    low = (square - high.astype(F32)).astype(BF16)
-    ones = jnp.ones((16, cols), BF16)
-    dims = (((1,), (1,)), ((), ()))
-    sums = lax.dot_general(ones, high, dims, preferred_element_type=F32)
-    sums = sums + lax.dot_general(ones, low, dims, preferred_element_type=F32)
+    sums = jnp.sum(tok * tok, axis=-1, keepdims=True)
+    sums = jnp.broadcast_to(sums, (slots, 128)).T[0:MOST]
     first = sums.astype(BF16).astype(F32)
     second = (sums - first).astype(BF16).astype(F32)
     third = sums - first - second
-    row = lax.broadcasted_iota(jnp.int32, (16, slots), 0)
-    scales = jnp.where(row == 0, first, jnp.where(row == 1, second, third)).astype(BF16)
+    row = lax.broadcasted_iota(jnp.int32, (MOST, slots), 0)
+    scales = jnp.where(row == 0, first, jnp.where(row == 1, second, third))
     resid = resid_ref[...].astype(F32)
     rows = resid.shape[0] // quarters
     for h in range(quarters):
-        out_ref[h, slots : slots + 16, :] = scales
-        pieces = []
+        pieces = [scales]
         for r in range(rows):
             own = resid[h * rows + r : h * rows + r + 1, :]
             pieces.append(own[:, 0:hidden])
             pieces.append(own[:, hidden : 2 * hidden])
             pieces.append(jnp.concatenate([own[:, 2 * hidden :], jnp.zeros((1, 3 * hidden - cols), F32)], 1))
-        pieces.append(jnp.zeros((16 - len(pieces), hidden), F32))
-        out_ref[h, slots + 16 :, :] = jnp.concatenate(pieces, 0).astype(BF16)
+        pieces.append(jnp.zeros((16 - 4 * MOST, hidden), F32))
+        out_ref[h, slots:, :] = jnp.concatenate(pieces, 0).astype(BF16)
     tok = (tok * gain_ref[...]).astype(BF16)
     for d in range(0, quarters, 2):
-        copies[d].wait()
-        copies[d + 1].wait()
-        pair = jnp.dot(tok, w_s[:, d * hidden : (d + 2) * hidden], preferred_element_type=F32).astype(BF16)
+        pair = jnp.dot(tok, w_ref[:, d * hidden : (d + 2) * hidden], preferred_element_type=F32).astype(BF16)
         for i in range(2):
             out_ref[lax.rem(me - d - i + quarters, quarters), 0:slots, :] = pair[:, i * hidden : (i + 1) * hidden]
 
@@ -265,14 +297,13 @@
     squares = jnp.zeros((1, slots), F32)
     for q in range(quarters):
         total = total + part_ref[q, 0:slots, :].astype(F32)
-        parts = part_ref[q, slots : slots + 16, :].astype(F32)
-        squares = squares + (parts[0:1] + parts[1:2] + parts[2:3])
-        own = part_ref[q, slots + 16 :, :].astype(F32)
+        own = part_ref[q, slots:, :].astype(F32)
+        squares = squares + (own[0:1] + own[1:2] + own[2:3])
         for r in range(rows):
             for m in range(3):
                 size = min(hidden, cols - m * hidden)
                 at = q * cols + m * hidden
-                resid_s[r : r + 1, at : at + size] = own[3 * r + m : 3 * r + m + 1, 0:size]
+                resid_s[r : r + 1, at : at + size] = own[3 + 3 * r + m : 4 + 3 * r + m, 0:size]
     resid_ref[...] = resid_s[0:rows, :].astype(BF16)
     row = lax.broadcasted_iota(jnp.int32, (8, slots), 0)
     scale = lax.rsqrt(squares / width + 1e-05)
@@ -309,7 +340,7 @@
     cols = width // n_hid
     per = n_seq // n_hid
 
-    w_in = lax.all_gather(jnp.concatenate([w_in_x, w_in_z], 1), "seq", axis=0, tiled=True)
+    w_x = lax.all_gather(w_in_x, "seq", axis=0, tiled=True)
 
     own_routes = jnp.concatenate([route_ids.astype(BF16), route_weights], 1)
     own = jnp.concatenate([x_in, jnp.pad(own_routes, ((0, 0), (0, 124)))], 1)
@@ -321,7 +352,8 @@
         [(n_exp * rows, width + 128)],
         over_exp,
     )
-    quarter_rows, w_out = lax.optimization_barrier((quarter_rows, w_out))
+    quarter_rows, w_out, w_in_z = lax.optimization_barrier((quarter_rows, w_out, w_in_z))
+    w_z = lax.all_gather(w_in_z, "seq", axis=0, tiled=True)
     route = [
         (s * n_hid + h, (h * per + s % per) * n_hid + s // per) for s in range(n_seq) for h in range(n_hid)
     ]
@@ -334,17 +366,23 @@
     x_block = lax.dynamic_slice(
         all_rows.reshape(n_hid, n_exp, rows, -1), (0, at_exp, 0, at_hid * cols), (n_hid, 1, rows, cols)
     ).reshape(block, cols)
-    both, tail, routes = call(
+    stream, tail, routes = call(
         project_kernel,
         "project",
-        (like((2, tokens, channels), BF16), like((8, channels), F32), like((tokens, 128), F32)),
-        [(6, tokens, 128)],
+        (like((tokens, channels), BF16), like((8, channels), F32), like((tokens, 128), F32)),
+        [(tokens, channels), (tokens, 128), (tokens, channels)],
         all_rows,
         norm_gain[None],
-        w_in,
-        unread=1,
-        more=[pltpu.VMEM(w_in.shape, BF16), pltpu.SemaphoreType.DMA],
-        limit=58,
+        w_x,
+    )
+    gate_in = call(
+        project_gate_kernel,
+        "project_gate",
+        like((tokens, channels), BF16),
+        [(tokens, channels), (tokens, channels)],
+        all_rows,
+        norm_gain[None],
+        w_z,
     )
     halo = lax.ppermute(tail, "seq", [(i, i + 1) for i in range(n_seq - 1)])
     inner_act, tiles = call(
@@ -352,7 +390,7 @@
         "conv",
         (like((tokens, channels), BF16), like((n_exp * n_hid, 8, 128), BF16)),
         [(tokens + 8, channels)],
-        both,
+        stream,
         halo,
         params,
         w_xproj,
@@ -379,13 +417,17 @@
     select = jnp.sum(select.reshape(n_exp * MOST, block, -1), 2)
     select = jnp.pad(select, ((0, 0), (0, 16 - block))).astype(BF16)
 
-    local_out, cum, output_mat, carried = call(
+    def shift(w, d):
+        out = lax.dynamic_index_in_dim(w[0].reshape(n_hid, cols, -1), (at_hid + d) % n_hid, 0, keepdims=False)
+        return lax.ppermute(out, "hid", [(i, (i + d) % n_hid) for i in range(n_hid)])
+
+    slot_wts, w_first = lax.optimization_barrier((slot_wts, w_gate))
+    w_1, w_3 = shift(w_first, 1), shift(w_first, 3)
+    local, carried = call(
         scan_kernel,
         "scan",
         (
-            like((tokens, channels), F32),
-            like((tokens, channels), F32),
-            like((states, 256), F32),
+            like((2 * tokens + 2 * states, channels), F32),
             like((n_seq, states + 8, channels), F32),
         ),
         [(tokens, rank), (tokens, channels), (tokens, channels)],
@@ -405,55 +447,73 @@
         at_seq.astype(jnp.int32)[None],
         carried_all,
         params,
-        output_mat,
-        cum,
-        local_out,
-        inner_act,
-        both,
+        local,
+        gate_in,
         scalars=1,
     )
 
     gated_all = exchange(gated, "hid")
-    mixed = call(mix_kernel, "mix", like((n_exp, block, cols), BF16), [(tokens, cols)], gated_all, w_out_all)
-    mixed, w_gate = lax.optimization_barrier((mixed, w_gate))
-    w_quarters = w_gate[0].reshape(n_hid, cols, -1)
-
-    def shift(d):
-        out = lax.dynamic_index_in_dim(w_quarters, (at_hid + d) % n_hid, 0, keepdims=False)
-        return lax.ppermute(out, "hid", [(i, (i + d) % n_hid) for i in range(n_hid)])
-
-    w_1, w_2, w_3 = shift(1), shift(2), shift(3)
+    mixed = call(
+        mix_kernel,
+        "mix",
+        like((n_exp, 8, block * cols // 8), BF16),
+        [(tokens, cols)],
+        gated_all,
+        w_out_all,
+        w_1,
+        w_3,
+        unread=2,
+    )
+    mixed, w_second = lax.optimization_barrier((mixed, w_gate))
+    w_2 = shift(w_second, 2)
     sums = exchange(mixed, "exp")
     resid_part, send = call(
         resid_kernel,
         "resid",
-        (like((block, cols), BF16), like((n_exp, MOST, cols), BF16)),
+        (like((block, cols), BF16), like((n_exp, 8, MOST * cols // 8), BF16)),
         [(16, cols)],
         sums,
         x_block,
         select,
     )
 
-    slots = exchange(send, "exp").reshape(n_exp * MOST, cols)
-    all_slots = lax.all_gather(slots, "seq", axis=0, tiled=True)
-    n_all, hidden = all_slots.shape[0], w_gate.shape[2]
-    away = call(
-        expert_kernel,
-        "expert",
-        like((n_hid, n_all + 32, hidden), BF16),
+    hidden = w_gate.shape[2]
+    w_side = call(
+        stage_kernel,
+        "stage",
+        like((cols, n_hid * hidden), BF16),
         [],
         at_hid.astype(jnp.int32)[None],
-        all_slots,
-        lax.dynamic_slice_in_dim(moe_gain, at_hid * cols, cols, 0)[None],
-        resid_part,
         w_gate,
         w_1,
         w_2,
         w_3,
         scalars=1,
         unread=4,
-        more=[pltpu.VMEM((cols, n_hid * hidden), BF16), pltpu.SemaphoreType.DMA((n_hid,))],
-        limit=58,
+        more=[pltpu.SemaphoreType.DMA((n_hid,))],
+    )
+    slots = call(
+        slots_kernel,
+        "slots",
+        like((n_exp * MOST, cols), BF16),
+        [(n_exp * MOST, cols)],
+        exchange(send, "exp"),
+        w_side,
+        unread=1,
+    )
+    all_slots = lax.all_gather(slots, "seq", axis=0, tiled=True)
+    n_all = all_slots.shape[0]
+    away = call(
+        expert_kernel,
+        "expert",
+        like((n_hid, n_all + 16, hidden), BF16),
+        [],
+        at_hid.astype(jnp.int32)[None],
+        all_slots,
+        lax.dynamic_slice_in_dim(moe_gain, at_hid * cols, cols, 0)[None],
+        resid_part,
+        w_side,
+        scalars=1,
     )
     home = exchange(away, "hid")
     activated, resid = call(

time: 268 us -> 255 us (0.951)
  blocking collectives: 79.7 us -> 49.2 us
  starting transfers between devices: 61.1 us -> 77.7 us
  local copies, waits for them, and re-layouts: 13.1 us -> 21.6 us
  Pallas kernels: 19.1 us -> 11.9 us
    all_to_all x1 -> x0, blocking collectives: 28.7 us -> none  [exchange(): return lax.all_to_all(x, axis, split_axis=0, concat_axis=0, tiled=True)]
    all_to_all x7 -> x8, starting transfers between devices: 38.4 us -> 54.7 us  [exchange(): return lax.all_to_all(x, axis, split_axis=0, concat_axis=0, tiled=True)]
    unnamed x38 -> x54, local copies, waits for them, and re-layouts: 6.16 us -> 15.5 us
    pallas_call x10 -> x13, Pallas kernels: 19.1 us -> 11.9 us  [call(): pl.pallas_call(body, out_shape=out_shape, in_specs=[smem] * scalars + [vm...]
    all_to_all x7 -> x8, waiting for transfers between devices: 73.7 us -> 75.1 us  [exchange(): return lax.all_to_all(x, axis, split_axis=0, concat_axis=0, tiled=True)]
  transfers between devices with their start and end apart: 14 -> 16, of which waited for: 8 -> 9; matrix products, arithmetic and copies ran while one was open for 4% -> 4% of each run, Pallas kernels for 4% -> 3%
where the time goes in v3:
time: 255 us; the launch traced here: 254 us
  starting transfers between devices  77.7 us (30%)
  waiting for transfers between devices  76.4 us (30%)
  blocking collectives  49.2 us (19%)
  local copies, waits for them, and re-layouts  21.6 us (8%)
  between operations  14.2 us (6%)
  Pallas kernels  11.9 us (5%)
    all_to_all x8, waiting for transfers between devices, exchange(): return lax.all_to_all(x, axis, split_axis=0, concat_axis=0, tiled=True)  75.1 us
    all_to_all x8, starting transfers between devices, exchange(): return lax.all_to_all(x, axis, split_axis=0, concat_axis=0, tiled=True)  54.7 us
    all_gather x1, blocking collectives, shards(): over_exp = lax.all_gather(own, 'exp', axis=0, tiled=False)  32.9 us
    all_gather x1, blocking collectives, shards(): all_slots = lax.all_gather(slots, 'seq', axis=0, tiled=True)  16.3 us
    unnamed x54, local copies, waits for them, and re-layouts  15.5 us
    ppermute x1, starting transfers between devices, shards(): halo = lax.ppermute(tail, 'seq', [(i, i + 1) for i in range(n_seq - 1)])  14 us
    pallas_call x13, Pallas kernels, call(): pl.pallas_call(body, out_shape=out_shape, in_specs=[smem] * scalars + [vm...  11.9 us
    ppermute x3, starting transfers between devices, shift(): lax.ppermute(out, 'hid', [(i, (i + d) % n_hid) for i in range(n_hid)])  8.3 us
  transfers between devices with their start and end apart: 16, of which 9 were waited for; matrix products, arithmetic and copies ran while one was open for 4% of the time, Pallas kernels for 3%

profile of v3, /device:TPU:1, one launch (start us, length us, event | category | flops | bytes accessed | tf_op | source)
XLA Modules:
  0.0 253.8 jit_solution(12505475130629731185)
XLA Ops:
  10.2 32.9 %all-gather.2.x_ref = bf16[16,3,4224]{2,1,0:T(4,128)(2,1)S(1)} all-gather(bf16[1,3,4224]{2,1,0:T(4,128)(2,1)S(1)} %fusion.3), channel_id=2, replica_groups=mesh['seq'=8,'exp'=16,'hid'=4] {'exp'}, dimensions={0}, use_global_device_ids=true | all-gather | bytes 430848 | tf_op jit(solution)/shard_map/all_gather | solution.py:347
  44.7 4.1 %all-to-all-start = ((bf16[4,48,4224]{2,1,0:T(8,128)(2,1)}), bf16[4,48,4224]{2,1,0:T(8,128)(2,1)S(1)}, u32[]{:S(2)}, u32[]{:S(2)}) async-start(bf16[4,48,4224]{2,1,0:T(8,128)(2,1)} %rows.1), calls=%async_computation | async-start | bytes 3244032 | tf_op jit(solution)/shard_map/all_to_all | solution.py:17
  50.3 11.8 %all-to-all-done.x_ref = bf16[4,48,4224]{2,1,0:T(8,128)(2,1)S(1)} async-done(((bf16[4,48,4224]{2,1,0:T(8,128)(2,1)}), bf16[4,48,4224]{2,1,0:T(8,128)(2,1)S(1)}, u32[]{:S(2)}, u32[]{:S(2)}) %all-to-all-start) | async-done | bytes 1622048 | tf_op jit(solution)/shard_map/all_to_all | solution.py:17
  64.1 14.0 %collective-permute-start = (f32[8,128]{1,0:T(8,128)S(1)}, f32[8,128]{1,0:T(8,128)S(1)}, u32[]{:S(2)}, u32[]{:S(2)}) collective-permute-start(f32[8,128]{1,0:T(8,128)S(1)} %get-tuple-element.22), channel_id=1, source_target_pairs={{0,64},{64,128},{128,192},{192,256},{256,320},{320,384},{384,448},... | collective-permute-start | bytes 12296 | tf_op jit(solution)/shard_map/ppermute | solution.py:387
  79.7 12.3 %all-to-all-start.1 = ((bf16[64,8,128]{2,1,0:T(8,128)(2,1)}), bf16[64,8,128]{2,1,0:T(8,128)(2,1)S(1)}, u32[]{:S(2)}, u32[]{:S(2)}) async-start(bf16[64,8,128]{2,1,0:T(8,128)(2,1)} %get-tuple-element.23), calls=%async_computation.1 | async-start | bytes 262144 | tf_op jit(solution)/shard_map/all_to_all | solution.py:17
  92.8 2.7 %dynamic-slice_bitcast_fusion.1 = (bf16[1024,384]{1,0:T(8,128)(2,1)}, bf16[1024,384]{1,0:T(8,128)(2,1)}) fusion(bf16[4,1024,384]{2,1,0:T(8,128)(2,1)} %bitcast.31, s32[]{:T(128)S(6)} %select_n.52, s32[]{:T(128)S(6)} %select_n.50), kind=kLoop, calls=%fused_computation.4 | loop fusion | bytes 3145736 | tf_op jit(solution)/shard_map/jit(dynamic_index_in_dim)/squeeze | solution.py:421
  95.6 4.1 %collective-permute-start.3 = (bf16[1024,384]{1,0:T(8,128)(2,1)}, bf16[1024,384]{1,0:T(8,128)(2,1)S(1)}, u32[]{:S(2)}, u32[]{:S(2)}) collective-permute-start(bf16[1024,384]{1,0:T(8,128)(2,1)} %get-tuple-element.41), channel_id=1, source_target_pairs={{0,3},{1,0},{2,1},{3,2},{4,7},{5,4},{6,5},{7,6},{8,11},{9,8},{10,9... | collective-permute-start | bytes 2359304 | tf_op jit(solution)/shard_map/ppermute | solution.py:422
  99.7 1.9 collective-permute-start.2
  101.6 7.3 %all-to-all-done.1.got_ref = bf16[64,8,128]{2,1,0:T(8,128)(2,1)S(1)} async-done(((bf16[64,8,128]{2,1,0:T(8,128)(2,1)}), bf16[64,8,128]{2,1,0:T(8,128)(2,1)S(1)}, u32[]{:S(2)}, u32[]{:S(2)}) %all-to-all-start.1) | async-done | bytes 131104 | tf_op jit(solution)/shard_map/all_to_all | solution.py:17
  109.7 7.4 %all-to-all-start.2 = ((bf16[64,8,128]{2,1,0:T(8,128)(2,1)}), bf16[64,8,128]{2,1,0:T(8,128)(2,1)S(1)}, u32[]{:S(2)}, u32[]{:S(2)}) async-start(bf16[64,8,128]{2,1,0:T(8,128)(2,1)} %tile_sum.1), calls=%async_computation.2 | async-start | bytes 262144 | tf_op jit(solution)/shard_map/all_to_all | solution.py:17
  117.1 14.9 %all-to-all-done.2.back_ref = bf16[64,8,128]{2,1,0:T(8,128)(2,1)S(1)} async-done(((bf16[64,8,128]{2,1,0:T(8,128)(2,1)}), bf16[64,8,128]{2,1,0:T(8,128)(2,1)S(1)}, u32[]{:S(2)}, u32[]{:S(2)}) %all-to-all-start.2) | async-done | bytes 131104 | tf_op jit(solution)/shard_map/all_to_all | solution.py:17
  134.3 6.9 %all-to-all-start.3 = ((f32[8,24,128]{2,1,0:T(8,128)}), f32[8,24,128]{2,1,0:T(8,128)S(1)}, u32[]{:S(2)}, u32[]{:S(2)}) async-start(f32[8,24,128]{2,1,0:T(8,128)} %copy-done.15), calls=%async_computation.3 | async-start | bytes 196608 | tf_op jit(solution)/shard_map/all_to_all | solution.py:17
  143.3 3.0 %all-to-all-done.3.all_ref = f32[8,24,128]{2,1,0:T(8,128)S(1)} async-done(((f32[8,24,128]{2,1,0:T(8,128)}), f32[8,24,128]{2,1,0:T(8,128)S(1)}, u32[]{:S(2)}, u32[]{:S(2)}) %all-to-all-start.3) | async-done | bytes 98336 | tf_op jit(solution)/shard_map/all_to_all | solution.py:17
  148.6 3.4 %all-to-all-start.4 = ((bf16[4,192,128]{2,1,0:T(8,128)(2,1)}), bf16[4,192,128]{2,1,0:T(8,128)(2,1)S(1)}, u32[]{:S(2)}, u32[]{:S(2)}) async-start(bf16[4,192,128]{2,1,0:T(8,128)(2,1)} %copy-done.12), calls=%async_computation.4 | async-start | bytes 393216 | tf_op jit(solution)/shard_map/all_to_all | solution.py:17
  152.0 5.1 %all-to-all-done.4.gated_ref = bf16[4,192,128]{2,1,0:T(8,128)(2,1)S(1)} async-done(((bf16[4,192,128]{2,1,0:T(8,128)(2,1)}), bf16[4,192,128]{2,1,0:T(8,128)(2,1)S(1)}, u32[]{:S(2)}, u32[]{:S(2)}) %all-to-all-start.4) | async-done | bytes 196640 | tf_op jit(solution)/shard_map/all_to_all | solution.py:17
  159.7 4.2 %all-to-all-start.5 = ((bf16[16,8,1536]{2,1,0:T(8,128)(2,1)}), bf16[16,8,1536]{2,1,0:T(8,128)(2,1)}, u32[]{:S(2)}, u32[]{:S(2)}) async-start(bf16[16,8,1536]{2,1,0:T(8,128)(2,1)} %copy-done.6), calls=%async_computation.5 | async-start | bytes 786432 | tf_op jit(solution)/shard_map/all_to_all | solution.py:17
  165.9 2.3 collective-permute-start.4
  168.7 11.5 %all-to-all-done.5.parts_ref = bf16[16,8,1536]{2,1,0:T(8,128)(2,1)} async-done(((bf16[16,8,1536]{2,1,0:T(8,128)(2,1)}), bf16[16,8,1536]{2,1,0:T(8,128)(2,1)}, u32[]{:S(2)}, u32[]{:S(2)}) %all-to-all-start.5) | async-done | bytes 393248 | tf_op jit(solution)/shard_map/all_to_all | solution.py:17
  182.0 12.8 %all-to-all-start.6 = ((bf16[16,8,384]{2,1,0:T(8,128)(2,1)}), bf16[16,8,384]{2,1,0:T(8,128)(2,1)S(1)}, u32[]{:S(2)}, u32[]{:S(2)}) async-start(bf16[16,8,384]{2,1,0:T(8,128)(2,1)} %get-tuple-element.33), calls=%async_computation.6 | async-start | bytes 196608 | tf_op jit(solution)/shard_map/all_to_all | solution.py:17
  196.4 1.9 copy-done
  202.1 4.6 %all-to-all-done.6.got_ref = bf16[16,8,384]{2,1,0:T(8,128)(2,1)S(1)} async-done(((bf16[16,8,384]{2,1,0:T(8,128)(2,1)}), bf16[16,8,384]{2,1,0:T(8,128)(2,1)S(1)}, u32[]{:S(2)}, u32[]{:S(2)}) %all-to-all-start.6) | async-done | bytes 98336 | tf_op jit(solution)/shard_map/all_to_all | solution.py:17
  206.8 16.3 %all_gather.27.tok_ref = bf16[384,1024]{1,0:T(8,128)(2,1)S(1)} all-gather(bf16[48,1024]{1,0:T(8,128)(2,1)S(1)} %slots.1), channel_id=1, replica_groups=mesh['seq'=8,'exp'=16,'hid'=4] {'seq'}, dimensions={0}, use_global_device_ids=true | all-gather | bytes 884736 | tf_op jit(solution)/shard_map/all_gather | solution.py:504
  225.5 3.5 %all-to-all-start.7 = ((bf16[4,400,384]{2,1,0:T(8,128)(2,1)}), bf16[4,400,384]{2,1,0:T(8,128)(2,1)S(1)}, u32[]{:S(2)}, u32[]{:S(2)}) async-start(bf16[4,400,384]{2,1,0:T(8,128)(2,1)} %copy-done.1), calls=%async_computation.7 | async-start | bytes 2457600 | tf_op jit(solution)/shard_map/all_to_all | solution.py:17
  229.2 16.9 %all-to-all-done.7.part_ref = bf16[4,400,384]{2,1,0:T(8,128)(2,1)S(1)} async-done(((bf16[4,400,384]{2,1,0:T(8,128)(2,1)}), bf16[4,400,384]{2,1,0:T(8,128)(2,1)S(1)}, u32[]{:S(2)}, u32[]{:S(2)}) %all-to-all-start.7) | async-done | bytes 1228832 | tf_op jit(solution)/shard_map/all_to_all | solution.py:17
  (109 shorter events, 33.7 us)
Async XLA Ops:
  7.2 54.9 %all-gather.7.cloned.1.call-start = ((), (), s32[]{:S(2)}) async-start(), calls=%async_computation.8 | async-start | bytes 1179648 | tf_op jit(solution)/shard_map/all_gather | solution.py:343
  7.9 133.3 %all-gather.9.cloned.1.call-start = ((), (), s32[]{:S(2)}) async-start(), calls=%async_computation.9 | async-start | bytes 1179648 | tf_op jit(solution)/shard_map/all_gather | solution.py:356
  44.7 17.4 %copy-start.16 = (f32[4096]{0:T(1024)S(1)}, f32[4096]{0:T(1024)}, u32[]{:S(2)}) copy-start(f32[4096]{0:T(1024)} %param.17) | copy-start | bytes 49156
  44.7 17.4 %all-to-all-start = ((bf16[4,48,4224]{2,1,0:T(8,128)(2,1)}), bf16[4,48,4224]{2,1,0:T(8,128)(2,1)S(1)}, u32[]{:S(2)}, u32[]{:S(2)}) async-start(bf16[4,48,4224]{2,1,0:T(8,128)(2,1)} %rows.1), calls=%async_computation | async-start | bytes 3244032 | tf_op jit(solution)/shard_map/all_to_all | solution.py:17
  48.8 29.3 %copy-start.19 = (bf16[128,288]{0,1:T(8,128)(2,1)S(1)}, bf16[128,288]{0,1:T(8,128)(2,1)}, u32[]{:S(2)}) copy-start(bf16[128,288]{0,1:T(8,128)(2,1)} %param.22) | copy-start | bytes 221188
  48.8 29.4 %copy-start.20 = (f32[16,128]{1,0:T(8,128)S(1)}, f32[16,128]{1,0:T(8,128)}, u32[]{:S(2)}) copy-start(f32[16,128]{1,0:T(8,128)} %param.25) | copy-start | bytes 24580
  48.8 29.4 %copy-start.21 = (f32[4,128]{1,0:T(4,128)S(1)}, f32[4,128]{1,0:T(4,128)}, u32[]{:S(2)}) copy-start(f32[4,128]{1,0:T(4,128)} %param.20) | copy-start | bytes 6148
  48.8 29.5 %copy-start.22 = (f32[128]{0:T(128)S(1)}, f32[128]{0:T(128)}, u32[]{:S(2)}) copy-start(f32[128]{0:T(128)} %param.21) | copy-start | bytes 1540
  48.8 29.5 %copy-start.23 = (f32[128]{0:T(128)S(1)}, f32[128]{0:T(128)}, u32[]{:S(2)}) copy-start(f32[128]{0:T(128)} %param.24) | copy-start | bytes 1540
  48.8 29.4 %copy-start.24 = (f32[128]{0:T(128)S(1)}, f32[128]{0:T(128)}, u32[]{:S(2)}) copy-start(f32[128]{0:T(128)} %param.26) | copy-start | bytes 1540
  48.8 103.2 %all-gather.11.cloned.1.call-start = ((), (), s32[]{:S(2)}) async-start(), calls=%async_computation.10 | async-start | bytes 1179648 | tf_op jit(solution)/shard_map/all_gather | solution.py:361
  48.9 0.7 collective-permute-start.1
  64.1 14.8 %collective-permute-start = (f32[8,128]{1,0:T(8,128)S(1)}, f32[8,128]{1,0:T(8,128)S(1)}, u32[]{:S(2)}, u32[]{:S(2)}) collective-permute-start(f32[8,128]{1,0:T(8,128)S(1)} %get-tuple-element.22), channel_id=1, source_target_pairs={{0,64},{64,128},{128,192},{192,256},{256,320},{320,384},{384,448},... | collective-permute-start | bytes 12296 | tf_op jit(solution)/shard_map/ppermute | solution.py:387
  79.7 29.2 %all-to-all-start.1 = ((bf16[64,8,128]{2,1,0:T(8,128)(2,1)}), bf16[64,8,128]{2,1,0:T(8,128)(2,1)S(1)}, u32[]{:S(2)}, u32[]{:S(2)}) async-start(bf16[64,8,128]{2,1,0:T(8,128)(2,1)} %get-tuple-element.23), calls=%async_computation.1 | async-start | bytes 262144 | tf_op jit(solution)/shard_map/all_to_all | solution.py:17
  92.8 39.2 %copy-start.17 = (bf16[256,128]{1,0:T(8,128)(2,1)S(1)}, bf16[256,128]{1,0:T(8,128)(2,1)}, u32[]{:S(2)}) copy-start(bf16[256,128]{1,0:T(8,128)(2,1)} %wdt_ref.1) | copy-start | bytes 196612
  95.6 56.4 %collective-permute-start.3 = (bf16[1024,384]{1,0:T(8,128)(2,1)}, bf16[1024,384]{1,0:T(8,128)(2,1)S(1)}, u32[]{:S(2)}, u32[]{:S(2)}) collective-permute-start(bf16[1024,384]{1,0:T(8,128)(2,1)} %get-tuple-element.41), channel_id=1, source_target_pairs={{0,3},{1,0},{2,1},{3,2},{4,7},{5,4},{6,5},{7,6},{8,11},{9,8},{10,9... | collective-permute-start | bytes 2359304 | tf_op jit(solution)/shard_map/ppermute | solution.py:422
  99.7 52.3 %collective-permute-start.2 = (bf16[1024,384]{1,0:T(8,128)(2,1)}, bf16[1024,384]{1,0:T(8,128)(2,1)S(1)}, u32[]{:S(2)}, u32[]{:S(2)}) collective-permute-start(bf16[1024,384]{1,0:T(8,128)(2,1)} %get-tuple-element.42), channel_id=1, source_target_pairs={{0,1},{1,2},{2,3},{3,0},{4,5},{5,6},{6,7},{7,4},{8,9},{9,10},{10,1... | collective-permute-start | bytes 2359304 | tf_op jit(solution)/shard_map/ppermute | solution.py:422
  109.7 22.3 %all-to-all-start.2 = ((bf16[64,8,128]{2,1,0:T(8,128)(2,1)}), bf16[64,8,128]{2,1,0:T(8,128)(2,1)S(1)}, u32[]{:S(2)}, u32[]{:S(2)}) async-start(bf16[64,8,128]{2,1,0:T(8,128)(2,1)} %tile_sum.1), calls=%async_computation.2 | async-start | bytes 262144 | tf_op jit(solution)/shard_map/all_to_all | solution.py:17
  134.3 11.9 %all-to-all-start.3 = ((f32[8,24,128]{2,1,0:T(8,128)}), f32[8,24,128]{2,1,0:T(8,128)S(1)}, u32[]{:S(2)}, u32[]{:S(2)}) async-start(f32[8,24,128]{2,1,0:T(8,128)} %copy-done.15), calls=%async_computation.3 | async-start | bytes 196608 | tf_op jit(solution)/shard_map/all_to_all | solution.py:17
  148.6 8.5 %all-to-all-start.4 = ((bf16[4,192,128]{2,1,0:T(8,128)(2,1)}), bf16[4,192,128]{2,1,0:T(8,128)(2,1)S(1)}, u32[]{:S(2)}, u32[]{:S(2)}) async-start(bf16[4,192,128]{2,1,0:T(8,128)(2,1)} %copy-done.12), calls=%async_computation.4 | async-start | bytes 393216 | tf_op jit(solution)/shard_map/all_to_all | solution.py:17
  159.7 20.4 %all-to-all-start.5 = ((bf16[16,8,1536]{2,1,0:T(8,128)(2,1)}), bf16[16,8,1536]{2,1,0:T(8,128)(2,1)}, u32[]{:S(2)}, u32[]{:S(2)}) async-start(bf16[16,8,1536]{2,1,0:T(8,128)(2,1)} %copy-done.6), calls=%async_computation.5 | async-start | bytes 786432 | tf_op jit(solution)/shard_map/all_to_all | solution.py:17
  165.9 29.6 %collective-permute-start.4 = (bf16[1024,384]{1,0:T(8,128)(2,1)S(1)}, bf16[1024,384]{1,0:T(8,128)(2,1)S(1)}, u32[]{:S(2)}, u32[]{:S(2)}) collective-permute-start(bf16[1024,384]{1,0:T(8,128)(2,1)S(1)} %dynamic-slice_bitcast_fusion), channel_id=1, source_target_pairs={{0,2},{1,3},{2,0},{3,1},{4,6},{5,7},{6,4},{7,5},{8,10},{9,11},{10,... | collective-permute-start | bytes 2359304 | tf_op jit(solution)/shard_map/ppermute | solution.py:422
  182.0 24.7 %all-to-all-start.6 = ((bf16[16,8,384]{2,1,0:T(8,128)(2,1)}), bf16[16,8,384]{2,1,0:T(8,128)(2,1)S(1)}, u32[]{:S(2)}, u32[]{:S(2)}) async-start(bf16[16,8,384]{2,1,0:T(8,128)(2,1)} %get-tuple-element.33), calls=%async_computation.6 | async-start | bytes 196608 | tf_op jit(solution)/shard_map/all_to_all | solution.py:17
  225.5 20.5 %all-to-all-start.7 = ((bf16[4,400,384]{2,1,0:T(8,128)(2,1)}), bf16[4,400,384]{2,1,0:T(8,128)(2,1)S(1)}, u32[]{:S(2)}, u32[]{:S(2)}) async-start(bf16[4,400,384]{2,1,0:T(8,128)(2,1)} %copy-done.1), calls=%async_computation.7 | async-start | bytes 2457600 | tf_op jit(solution)/shard_map/all_to_all | solution.py:17
  (18 other events, 34.8 us)
Sparse Core Ops, SparseCore 0:
  10.1 36.7 all-gather.6
  49.1 30.9 all-gather.8
  82.3 31.2 all-gather.10

commit v4 on v3

--- a/solution.py
+++ b/solution.py
@@ -38,6 +38,16 @@
         compiler_params=pltpu.CompilerParams(vmem_limit_bytes=limit * 2**20),
         name=name,
     )(*args)
+
+
+def near_kernel(x_ref, out_ref, sem):
+    copy = pltpu.make_async_copy(x_ref, out_ref, sem)
+    copy.start()
+    copy.wait()
+
+
+def near(x, name):
+    return call(near_kernel, name, like(x.shape, x.dtype), [], x, unread=1, more=[pltpu.SemaphoreType.DMA])
 
 
 def like(shape, dtype):
@@ -198,7 +208,7 @@
         out_ref[h] = gated
 
 
-def mix_kernel(gated_ref, w_ref, _0, _1, out_ref, mixed_s):
+def mix_kernel(gated_ref, w_ref, _0, out_ref, mixed_s):
     quarters = gated_ref.shape[0]
     per = w_ref.shape[0] // quarters
     cols = w_ref.shape[2]
@@ -245,12 +255,10 @@
     out_ref[...] = slots_s[...].astype(BF16)
 
 
-def stage_kernel(me_ref, w0_ref, w1_ref, w2_ref, w3_ref, out_ref, sems):
-    cols = out_ref.shape[0]
+def stage_kernel(w0_ref, w1_ref, w2_ref, w3_ref, out_ref, sems):
     hidden = w1_ref.shape[1]
-    sources = [w0_ref.at[0, pl.ds(pl.multiple_of(me_ref[0] * cols, cols), cols)], w1_ref, w2_ref, w3_ref]
     copies = []
-    for d, w_ref in enumerate(sources):
+    for d, w_ref in enumerate((w0_ref, w1_ref, w2_ref, w3_ref)):
         copies.append(pltpu.make_async_copy(w_ref, out_ref.at[:, pl.ds(d * hidden, hidden)], sems.at[d]))
         copies[d].start()
     for copy in copies:
@@ -373,7 +381,7 @@
         [(tokens, channels), (tokens, 128), (tokens, channels)],
         all_rows,
         norm_gain[None],
-        w_x,
+        near(w_x, "near_x"),
     )
     gate_in = call(
         project_gate_kernel,
@@ -417,12 +425,14 @@
     select = jnp.sum(select.reshape(n_exp * MOST, block, -1), 2)
     select = jnp.pad(select, ((0, 0), (0, 16 - block))).astype(BF16)
 
+    def pick(w, d):
+        return lax.dynamic_index_in_dim(w[0].reshape(n_hid, cols, -1), (at_hid + d) % n_hid, 0, keepdims=False)
+
     def shift(w, d):
-        out = lax.dynamic_index_in_dim(w[0].reshape(n_hid, cols, -1), (at_hid + d) % n_hid, 0, keepdims=False)
-        return lax.ppermute(out, "hid", [(i, (i + d) % n_hid) for i in range(n_hid)])
+        return lax.ppermute(pick(w, d), "hid", [(i, (i + d) % n_hid) for i in range(n_hid)])
 
     slot_wts, w_first = lax.optimization_barrier((slot_wts, w_gate))
-    w_1, w_3 = shift(w_first, 1), shift(w_first, 3)
+    w_2 = shift(w_first, 2)
     local, carried = call(
         scan_kernel,
         "scan",
@@ -459,13 +469,12 @@
         like((n_exp, 8, block * cols // 8), BF16),
         [(tokens, cols)],
         gated_all,
-        w_out_all,
-        w_1,
-        w_3,
-        unread=2,
+        near(w_out_all, "near_out"),
+        w_2,
+        unread=1,
     )
     mixed, w_second = lax.optimization_barrier((mixed, w_gate))
-    w_2 = shift(w_second, 2)
+    w_own, w_1, w_3 = pick(w_second, 0), shift(w_second, 1), shift(w_second, 3)
     sums = exchange(mixed, "exp")
     resid_part, send = call(
         resid_kernel,
@@ -483,12 +492,10 @@
         "stage",
         like((cols, n_hid * hidden), BF16),
         [],
-        at_hid.astype(jnp.int32)[None],
-        w_gate,
+        w_own,
         w_1,
         w_2,
         w_3,
-        scalars=1,
         unread=4,
         more=[pltpu.SemaphoreType.DMA((n_hid,))],
     )

time: 255 us -> 250 us (0.980)
  waiting for transfers between devices: 76.4 us -> 69.9 us
    all_to_all x8, waiting for transfers between devices: 75.1 us -> 68.6 us  [exchange(): return lax.all_to_all(x, axis, split_axis=0, concat_axis=0, tiled=True)]
    unnamed x54 -> x50, local copies, waits for them, and re-layouts: 15.5 us -> 12.7 us
    all_to_all x8, starting transfers between devices: 54.7 us -> 51.9 us  [exchange(): return lax.all_to_all(x, axis, split_axis=0, concat_axis=0, tiled=True)]
    pallas_call x13 -> x15, Pallas kernels: 11.9 us -> 13.3 us  [call(): pl.pallas_call(body, out_shape=out_shape, in_specs=[smem] * scalars + [vm...]
  transfers between devices with their start and end apart: 16 -> 16, of which waited for: 9 -> 9; matrix products, arithmetic and copies ran while one was open for 4% -> 5% of each run, Pallas kernels for 3% -> 4%
where the time goes in v4:
time: 250 us; the launch traced here: 248 us
  starting transfers between devices  77.7 us (31%)
  waiting for transfers between devices  69.9 us (28%)
  blocking collectives  49.2 us (20%)
  local copies, waits for them, and re-layouts  20.7 us (8%)
  between operations  14.3 us (6%)
  Pallas kernels  13.3 us (5%)
  other arithmetic  2.95 us (1%)
    all_to_all x8, waiting for transfers between devices, exchange(): return lax.all_to_all(x, axis, split_axis=0, concat_axis=0, tiled=True)  68.6 us
    all_to_all x8, starting transfers between devices, exchange(): return lax.all_to_all(x, axis, split_axis=0, concat_axis=0, tiled=True)  51.9 us
    all_gather x1, blocking collectives, shards(): over_exp = lax.all_gather(own, 'exp', axis=0, tiled=False)  32.9 us
    all_gather x1, blocking collectives, shards(): all_slots = lax.all_gather(slots, 'seq', axis=0, tiled=True)  16.3 us
    ppermute x1, starting transfers between devices, shards(): halo = lax.ppermute(tail, 'seq', [(i, i + 1) for i in range(n_seq - 1)])  15.3 us
    pallas_call x15, Pallas kernels, call(): pl.pallas_call(body, out_shape=out_shape, in_specs=[smem] * scalars + [vm...  13.3 us
    unnamed x50, local copies, waits for them, and re-layouts  12.7 us
    ppermute x3, starting transfers between devices, shift(): lax.ppermute(pick(w, d), 'hid', [(i, (i + d) % n_hid) for i in range(n_hi...  9.68 us
  transfers between devices with their start and end apart: 16, of which 9 were waited for; matrix products, arithmetic and copies ran while one was open for 5% of the time, Pallas kernels for 4%

profile of v4, /device:TPU:1, one launch (start us, length us, event | category | flops | bytes accessed | tf_op | source)
XLA Modules:
  0.0 248.4 jit_solution(2964861976234928569)
XLA Ops:
  10.2 32.9 %all-gather.2.x_ref = bf16[16,3,4224]{2,1,0:T(4,128)(2,1)S(1)} all-gather(bf16[1,3,4224]{2,1,0:T(4,128)(2,1)S(1)} %fusion.3), channel_id=2, replica_groups=mesh['seq'=8,'exp'=16,'hid'=4] {'exp'}, dimensions={0}, use_global_device_ids=true | all-gather | bytes 430848 | tf_op jit(solution)/shard_map/all_gather | solution.py:355
  44.7 4.1 %all-to-all-start = ((bf16[4,48,4224]{2,1,0:T(8,128)(2,1)}), bf16[4,48,4224]{2,1,0:T(8,128)(2,1)S(1)}, u32[]{:S(2)}, u32[]{:S(2)}) async-start(bf16[4,48,4224]{2,1,0:T(8,128)(2,1)} %rows.1), calls=%async_computation | async-start | bytes 3244032 | tf_op jit(solution)/shard_map/all_to_all | solution.py:17
  51.5 10.5 %all-to-all-done.x_ref = bf16[4,48,4224]{2,1,0:T(8,128)(2,1)S(1)} async-done(((bf16[4,48,4224]{2,1,0:T(8,128)(2,1)}), bf16[4,48,4224]{2,1,0:T(8,128)(2,1)S(1)}, u32[]{:S(2)}, u32[]{:S(2)}) %all-to-all-start) | async-done | bytes 1622048 | tf_op jit(solution)/shard_map/all_to_all | solution.py:17
  62.8 15.3 %collective-permute-start = (f32[8,128]{1,0:T(8,128)S(1)}, f32[8,128]{1,0:T(8,128)S(1)}, u32[]{:S(2)}, u32[]{:S(2)}) collective-permute-start(f32[8,128]{1,0:T(8,128)S(1)} %get-tuple-element.22), channel_id=1, source_target_pairs={{0,64},{64,128},{128,192},{192,256},{256,320},{320,384},{384,448},... | collective-permute-start | bytes 12296 | tf_op jit(solution)/shard_map/ppermute | solution.py:395
  79.8 12.4 %all-to-all-start.1 = ((bf16[64,8,128]{2,1,0:T(8,128)(2,1)}), bf16[64,8,128]{2,1,0:T(8,128)(2,1)S(1)}, u32[]{:S(2)}, u32[]{:S(2)}) async-start(bf16[64,8,128]{2,1,0:T(8,128)(2,1)} %get-tuple-element.23), calls=%async_computation.1 | async-start | bytes 262144 | tf_op jit(solution)/shard_map/all_to_all | solution.py:17
  92.9 2.1 dynamic-slice_bitcast_fusion.3
  95.1 4.4 %collective-permute-start.2 = (bf16[1024,384]{1,0:T(8,128)(2,1)}, bf16[1024,384]{1,0:T(8,128)(2,1)S(1)}, u32[]{:S(2)}, u32[]{:S(2)}) collective-permute-start(bf16[1024,384]{1,0:T(8,128)(2,1)} %dynamic-slice_bitcast_fusion.3), channel_id=1, source_target_pairs={{0,2},{1,3},{2,0},{3,1},{4,6},{5,7},{6,4},{7,5},{8,10},{9,11},{10,... | collective-permute-start | bytes 2359304 | tf_op jit(solution)/shard_map/ppermute | solution.py:432
  99.5 9.6 %all-to-all-done.1.got_ref = bf16[64,8,128]{2,1,0:T(8,128)(2,1)S(1)} async-done(((bf16[64,8,128]{2,1,0:T(8,128)(2,1)}), bf16[64,8,128]{2,1,0:T(8,128)(2,1)S(1)}, u32[]{:S(2)}, u32[]{:S(2)}) %all-to-all-start.1) | async-done | bytes 131104 | tf_op jit(solution)/shard_map/all_to_all | solution.py:17
  109.8 4.8 %all-to-all-start.2 = ((bf16[64,8,128]{2,1,0:T(8,128)(2,1)}), bf16[64,8,128]{2,1,0:T(8,128)(2,1)S(1)}, u32[]{:S(2)}, u32[]{:S(2)}) async-start(bf16[64,8,128]{2,1,0:T(8,128)(2,1)} %tile_sum.1), calls=%async_computation.2 | async-start | bytes 262144 | tf_op jit(solution)/shard_map/all_to_all | solution.py:17
  114.6 15.1 %all-to-all-done.2.back_ref = bf16[64,8,128]{2,1,0:T(8,128)(2,1)S(1)} async-done(((bf16[64,8,128]{2,1,0:T(8,128)(2,1)}), bf16[64,8,128]{2,1,0:T(8,128)(2,1)S(1)}, u32[]{:S(2)}, u32[]{:S(2)}) %all-to-all-start.2) | async-done | bytes 131104 | tf_op jit(solution)/shard_map/all_to_all | solution.py:17
  131.3 6.7 %all-to-all-start.3 = ((f32[8,24,128]{2,1,0:T(8,128)}), f32[8,24,128]{2,1,0:T(8,128)S(1)}, u32[]{:S(2)}, u32[]{:S(2)}) async-start(f32[8,24,128]{2,1,0:T(8,128)} %get-tuple-element.27), calls=%async_computation.3 | async-start | bytes 196608 | tf_op jit(solution)/shard_map/all_to_all | solution.py:17
  140.1 3.0 %all-to-all-done.3.all_ref = f32[8,24,128]{2,1,0:T(8,128)S(1)} async-done(((f32[8,24,128]{2,1,0:T(8,128)}), f32[8,24,128]{2,1,0:T(8,128)S(1)}, u32[]{:S(2)}, u32[]{:S(2)}) %all-to-all-start.3) | async-done | bytes 98336 | tf_op jit(solution)/shard_map/all_to_all | solution.py:17
  144.5 4.0 %all-to-all-start.4 = ((bf16[4,192,128]{2,1,0:T(8,128)(2,1)}), bf16[4,192,128]{2,1,0:T(8,128)(2,1)}, u32[]{:S(2)}, u32[]{:S(2)}) async-start(bf16[4,192,128]{2,1,0:T(8,128)(2,1)} %gate.1), calls=%async_computation.4 | async-start | bytes 393216 | tf_op jit(solution)/shard_map/all_to_all | solution.py:17
  149.9 3.9 %all-to-all-done.4.gated_ref = bf16[4,192,128]{2,1,0:T(8,128)(2,1)} async-done(((bf16[4,192,128]{2,1,0:T(8,128)(2,1)}), bf16[4,192,128]{2,1,0:T(8,128)(2,1)}, u32[]{:S(2)}, u32[]{:S(2)}) %all-to-all-start.4) | async-done | bytes 196640 | tf_op jit(solution)/shard_map/all_to_all | solution.py:17
  156.0 3.6 %all-to-all-start.5 = ((bf16[16,8,1536]{2,1,0:T(8,128)(2,1)}), bf16[16,8,1536]{2,1,0:T(8,128)(2,1)S(1)}, u32[]{:S(2)}, u32[]{:S(2)}) async-start(bf16[16,8,1536]{2,1,0:T(8,128)(2,1)} %copy-done.4), calls=%async_computation.5 | async-start | bytes 786432 | tf_op jit(solution)/shard_map/all_to_all | solution.py:17
  160.4 3.0 %dynamic-slice_bitcast_fusion = (bf16[1024,384]{1,0:T(8,128)(2,1)}, bf16[1024,384]{1,0:T(8,128)(2,1)S(1)}, bf16[1024,384]{1,0:T(8,128)(2,1)}) fusion(bf16[4,1024,384]{2,1,0:T(8,128)(2,1)} %bitcast.38, s32[]{:T(128)S(6)} %select_n.65, s32[]{:T(128)S(6)} %select_n.63, s32[]{:T(128)S(6)} %select_n.61), kind=kLoop, calls=%fused_computation.3 | loop fusion | bytes 4718604 | tf_op jit(solution)/shard_map/jit(dynamic_index_in_dim)/squeeze | solution.py:429
  163.4 2.8 %collective-permute-start.4 = (bf16[1024,384]{1,0:T(8,128)(2,1)}, bf16[1024,384]{1,0:T(8,128)(2,1)S(1)}, u32[]{:S(2)}, u32[]{:S(2)}) collective-permute-start(bf16[1024,384]{1,0:T(8,128)(2,1)} %get-tuple-element.41), channel_id=1, source_target_pairs={{0,3},{1,0},{2,1},{3,2},{4,7},{5,4},{6,5},{7,6},{8,11},{9,8},{10,9... | collective-permute-start | bytes 2359304 | tf_op jit(solution)/shard_map/ppermute | solution.py:432
  166.2 2.5 %collective-permute-start.3 = (bf16[1024,384]{1,0:T(8,128)(2,1)S(1)}, bf16[1024,384]{1,0:T(8,128)(2,1)S(1)}, u32[]{:S(2)}, u32[]{:S(2)}) collective-permute-start(bf16[1024,384]{1,0:T(8,128)(2,1)S(1)} %get-tuple-element.42), channel_id=1, source_target_pairs={{0,1},{1,2},{2,3},{3,0},{4,5},{5,6},{6,7},{7,4},{8,9},{9,10},{10,1... | collective-permute-start | bytes 2359304 | tf_op jit(solution)/shard_map/ppermute | solution.py:432
  170.5 5.2 %all-to-all-done.5.parts_ref = bf16[16,8,1536]{2,1,0:T(8,128)(2,1)S(1)} async-done(((bf16[16,8,1536]{2,1,0:T(8,128)(2,1)}), bf16[16,8,1536]{2,1,0:T(8,128)(2,1)S(1)}, u32[]{:S(2)}, u32[]{:S(2)}) %all-to-all-start.5) | async-done | bytes 393248 | tf_op jit(solution)/shard_map/all_to_all | solution.py:17
  176.6 12.8 %all-to-all-start.6 = ((bf16[16,8,384]{2,1,0:T(8,128)(2,1)}), bf16[16,8,384]{2,1,0:T(8,128)(2,1)S(1)}, u32[]{:S(2)}, u32[]{:S(2)}) async-start(bf16[16,8,384]{2,1,0:T(8,128)(2,1)} %get-tuple-element.33), calls=%async_computation.6 | async-start | bytes 196608 | tf_op jit(solution)/shard_map/all_to_all | solution.py:17
  196.8 4.5 %all-to-all-done.6.got_ref = bf16[16,8,384]{2,1,0:T(8,128)(2,1)S(1)} async-done(((bf16[16,8,384]{2,1,0:T(8,128)(2,1)}), bf16[16,8,384]{2,1,0:T(8,128)(2,1)S(1)}, u32[]{:S(2)}, u32[]{:S(2)}) %all-to-all-start.6) | async-done | bytes 98336 | tf_op jit(solution)/shard_map/all_to_all | solution.py:17
  201.4 16.3 %all_gather.27.tok_ref = bf16[384,1024]{1,0:T(8,128)(2,1)S(1)} all-gather(bf16[48,1024]{1,0:T(8,128)(2,1)S(1)} %slots.1), channel_id=1, replica_groups=mesh['seq'=8,'exp'=16,'hid'=4] {'seq'}, dimensions={0}, use_global_device_ids=true | all-gather | bytes 884736 | tf_op jit(solution)/shard_map/all_gather | solution.py:511
  220.1 3.5 %all-to-all-start.7 = ((bf16[4,400,384]{2,1,0:T(8,128)(2,1)}), bf16[4,400,384]{2,1,0:T(8,128)(2,1)S(1)}, u32[]{:S(2)}, u32[]{:S(2)}) async-start(bf16[4,400,384]{2,1,0:T(8,128)(2,1)} %copy-done), calls=%async_computation.7 | async-start | bytes 2457600 | tf_op jit(solution)/shard_map/all_to_all | solution.py:17
  223.8 16.9 %all-to-all-done.7.part_ref = bf16[4,400,384]{2,1,0:T(8,128)(2,1)S(1)} async-done(((bf16[4,400,384]{2,1,0:T(8,128)(2,1)}), bf16[4,400,384]{2,1,0:T(8,128)(2,1)S(1)}, u32[]{:S(2)}, u32[]{:S(2)}) %all-to-all-start.7) | async-done | bytes 1228832 | tf_op jit(solution)/shard_map/all_to_all | solution.py:17
  (107 shorter events, 34.2 us)
Async XLA Ops:
  7.2 43.0 %all-gather.7.cloned.1.call-start = ((), (), s32[]{:S(2)}) async-start(), calls=%async_computation.8 | async-start | bytes 1179648 | tf_op jit(solution)/shard_map/all_gather | solution.py:351
  7.9 130.2 %all-gather.9.cloned.1.call-start = ((), (), s32[]{:S(2)}) async-start(), calls=%async_computation.9 | async-start | bytes 1179648 | tf_op jit(solution)/shard_map/all_gather | solution.py:364
  44.7 17.4 %all-to-all-start = ((bf16[4,48,4224]{2,1,0:T(8,128)(2,1)}), bf16[4,48,4224]{2,1,0:T(8,128)(2,1)S(1)}, u32[]{:S(2)}, u32[]{:S(2)}) async-start(bf16[4,48,4224]{2,1,0:T(8,128)(2,1)} %rows.1), calls=%async_computation | async-start | bytes 3244032 | tf_op jit(solution)/shard_map/all_to_all | solution.py:17
  48.8 99.8 %all-gather.11.cloned.1.call-start = ((), (), s32[]{:S(2)}) async-start(), calls=%async_computation.10 | async-start | bytes 1179648 | tf_op jit(solution)/shard_map/all_gather | solution.py:369
  48.8 0.7 collective-permute-start.1
  51.5 26.9 %copy-start.18 = (f32[16,128]{1,0:T(8,128)S(1)}, f32[16,128]{1,0:T(8,128)}, u32[]{:S(2)}) copy-start(f32[16,128]{1,0:T(8,128)} %param.25) | copy-start | bytes 24580
  51.5 26.9 %copy-start.19 = (f32[4,128]{1,0:T(4,128)S(1)}, f32[4,128]{1,0:T(4,128)}, u32[]{:S(2)}) copy-start(f32[4,128]{1,0:T(4,128)} %param.20) | copy-start | bytes 6148
  51.5 26.9 %copy-start.20 = (f32[128]{0:T(128)S(1)}, f32[128]{0:T(128)}, u32[]{:S(2)}) copy-start(f32[128]{0:T(128)} %param.21) | copy-start | bytes 1540
  51.5 26.8 %copy-start.21 = (f32[128]{0:T(128)S(1)}, f32[128]{0:T(128)}, u32[]{:S(2)}) copy-start(f32[128]{0:T(128)} %param.24) | copy-start | bytes 1540
  51.5 26.8 %copy-start.22 = (f32[128]{0:T(128)S(1)}, f32[128]{0:T(128)}, u32[]{:S(2)}) copy-start(f32[128]{0:T(128)} %param.26) | copy-start | bytes 1540
  62.8 16.1 %collective-permute-start = (f32[8,128]{1,0:T(8,128)S(1)}, f32[8,128]{1,0:T(8,128)S(1)}, u32[]{:S(2)}, u32[]{:S(2)}) collective-permute-start(f32[8,128]{1,0:T(8,128)S(1)} %get-tuple-element.22), channel_id=1, source_target_pairs={{0,64},{64,128},{128,192},{192,256},{256,320},{320,384},{384,448},... | collective-permute-start | bytes 12296 | tf_op jit(solution)/shard_map/ppermute | solution.py:395
  78.3 51.4 %copy-start.14 = (bf16[256,128]{1,0:T(8,128)(2,1)S(1)}, bf16[256,128]{1,0:T(8,128)(2,1)}, u32[]{:S(2)}) copy-start(bf16[256,128]{1,0:T(8,128)(2,1)} %wdt_ref.1) | copy-start | bytes 196612
  79.8 29.3 %all-to-all-start.1 = ((bf16[64,8,128]{2,1,0:T(8,128)(2,1)}), bf16[64,8,128]{2,1,0:T(8,128)(2,1)S(1)}, u32[]{:S(2)}, u32[]{:S(2)}) async-start(bf16[64,8,128]{2,1,0:T(8,128)(2,1)} %get-tuple-element.23), calls=%async_computation.1 | async-start | bytes 262144 | tf_op jit(solution)/shard_map/all_to_all | solution.py:17
  92.2 45.9 %copy-start.13 = (f32[4096]{0:T(1024)S(1)}, f32[4096]{0:T(1024)}, u32[]{:S(2)}) copy-start(f32[4096]{0:T(1024)} %param.17) | copy-start | bytes 49156
  92.4 37.3 %copy-start.17 = (f32[16,24]{1,0:T(8,128)}, f32[16,24]{1,0:T(8,128)S(1)}, u32[]{:S(2)}) copy-start(f32[16,24]{1,0:T(8,128)S(1)} %reshape.39) | copy-start | bytes 4612
  95.1 54.8 %collective-permute-start.2 = (bf16[1024,384]{1,0:T(8,128)(2,1)}, bf16[1024,384]{1,0:T(8,128)(2,1)S(1)}, u32[]{:S(2)}, u32[]{:S(2)}) collective-permute-start(bf16[1024,384]{1,0:T(8,128)(2,1)} %dynamic-slice_bitcast_fusion.3), channel_id=1, source_target_pairs={{0,2},{1,3},{2,0},{3,1},{4,6},{5,7},{6,4},{7,5},{8,10},{9,11},{10,... | collective-permute-start | bytes 2359304 | tf_op jit(solution)/shard_map/ppermute | solution.py:432
  109.8 19.9 %all-to-all-start.2 = ((bf16[64,8,128]{2,1,0:T(8,128)(2,1)}), bf16[64,8,128]{2,1,0:T(8,128)(2,1)S(1)}, u32[]{:S(2)}, u32[]{:S(2)}) async-start(bf16[64,8,128]{2,1,0:T(8,128)(2,1)} %tile_sum.1), calls=%async_computation.2 | async-start | bytes 262144 | tf_op jit(solution)/shard_map/all_to_all | solution.py:17
  131.3 11.7 %all-to-all-start.3 = ((f32[8,24,128]{2,1,0:T(8,128)}), f32[8,24,128]{2,1,0:T(8,128)S(1)}, u32[]{:S(2)}, u32[]{:S(2)}) async-start(f32[8,24,128]{2,1,0:T(8,128)} %get-tuple-element.27), calls=%async_computation.3 | async-start | bytes 196608 | tf_op jit(solution)/shard_map/all_to_all | solution.py:17
  144.5 9.2 %all-to-all-start.4 = ((bf16[4,192,128]{2,1,0:T(8,128)(2,1)}), bf16[4,192,128]{2,1,0:T(8,128)(2,1)}, u32[]{:S(2)}, u32[]{:S(2)}) async-start(bf16[4,192,128]{2,1,0:T(8,128)(2,1)} %gate.1), calls=%async_computation.4 | async-start | bytes 393216 | tf_op jit(solution)/shard_map/all_to_all | solution.py:17
  156.0 19.7 %all-to-all-start.5 = ((bf16[16,8,1536]{2,1,0:T(8,128)(2,1)}), bf16[16,8,1536]{2,1,0:T(8,128)(2,1)S(1)}, u32[]{:S(2)}, u32[]{:S(2)}) async-start(bf16[16,8,1536]{2,1,0:T(8,128)(2,1)} %copy-done.4), calls=%async_computation.5 | async-start | bytes 786432 | tf_op jit(solution)/shard_map/all_to_all | solution.py:17
  163.4 26.7 %collective-permute-start.4 = (bf16[1024,384]{1,0:T(8,128)(2,1)}, bf16[1024,384]{1,0:T(8,128)(2,1)S(1)}, u32[]{:S(2)}, u32[]{:S(2)}) collective-permute-start(bf16[1024,384]{1,0:T(8,128)(2,1)} %get-tuple-element.41), channel_id=1, source_target_pairs={{0,3},{1,0},{2,1},{3,2},{4,7},{5,4},{6,5},{7,6},{8,11},{9,8},{10,9... | collective-permute-start | bytes 2359304 | tf_op jit(solution)/shard_map/ppermute | solution.py:432
  166.2 24.8 %collective-permute-start.3 = (bf16[1024,384]{1,0:T(8,128)(2,1)S(1)}, bf16[1024,384]{1,0:T(8,128)(2,1)S(1)}, u32[]{:S(2)}, u32[]{:S(2)}) collective-permute-start(bf16[1024,384]{1,0:T(8,128)(2,1)S(1)} %get-tuple-element.42), channel_id=1, source_target_pairs={{0,1},{1,2},{2,3},{3,0},{4,5},{5,6},{6,7},{7,4},{8,9},{9,10},{10,1... | collective-permute-start | bytes 2359304 | tf_op jit(solution)/shard_map/ppermute | solution.py:432
  176.6 24.7 %all-to-all-start.6 = ((bf16[16,8,384]{2,1,0:T(8,128)(2,1)}), bf16[16,8,384]{2,1,0:T(8,128)(2,1)S(1)}, u32[]{:S(2)}, u32[]{:S(2)}) async-start(bf16[16,8,384]{2,1,0:T(8,128)(2,1)} %get-tuple-element.33), calls=%async_computation.6 | async-start | bytes 196608 | tf_op jit(solution)/shard_map/all_to_all | solution.py:17
  220.1 20.5 %all-to-all-start.7 = ((bf16[4,400,384]{2,1,0:T(8,128)(2,1)}), bf16[4,400,384]{2,1,0:T(8,128)(2,1)S(1)}, u32[]{:S(2)}, u32[]{:S(2)}) async-start(bf16[4,400,384]{2,1,0:T(8,128)(2,1)} %copy-done), calls=%async_computation.7 | async-start | bytes 2457600 | tf_op jit(solution)/shard_map/all_to_all | solution.py:17
  (16 other events, 66.3 us)
Sparse Core Ops, SparseCore 0:
  10.1 36.7 all-gather.6
  49.1 30.9 all-gather.8
  82.3 31.2 all-gather.10

commit v5 on v4

--- a/solution.py
+++ b/solution.py
@@ -55,32 +55,29 @@
 
 
 def rows_kernel(x_ref, out_ref, rows_s):
-    groups, rows, wide = x_ref.shape
-    width = wide - 128
+    groups, rows, width = x_ref.shape
     for g in range(groups):
         rows_s[g * rows : (g + 1) * rows, :] = x_ref[g].astype(F32)
-    x = rows_s[:, 0:width]
+    x = rows_s[...]
     scale = lax.rsqrt(jnp.mean(x * x, axis=-1, keepdims=True) + 1e-05)
     first = scale.astype(BF16).astype(F32)
     second = (scale - first).astype(BF16).astype(F32)
-    more = rows_s[:, width:]
-    lane = lax.broadcasted_iota(jnp.int32, more.shape, 1)
+    lane = lax.broadcasted_iota(jnp.int32, (groups * rows, 128), 1)
+    more = jnp.zeros((groups * rows, 128), F32)
     for at, value in enumerate((first, second, scale - first - second)):
-        more = jnp.where(lane == 4 + at, value, more)
-    rows_s[:, width:] = more
-    packed = rows_s[...].astype(BF16)
+        more = jnp.where(lane == at, value, more)
     for h in range(out_ref.shape[0]):
-        out_ref[h] = packed
+        out_ref[h, :, 0:width] = x.astype(BF16)
+        out_ref[h, :, width:] = more.astype(BF16)
 
 
 def normed_rows(x_ref, gain_ref, width):
-    normed, extras = [], []
+    normed = []
     for h in range(x_ref.shape[0]):
         more = x_ref[h, :, width:].astype(F32)
-        scale = more[:, 4:5] + more[:, 5:6] + more[:, 6:7]
+        scale = more[:, 0:1] + more[:, 1:2] + more[:, 2:3]
         normed.append((x_ref[h, :, 0:width].astype(F32) * scale * gain_ref[...]).astype(BF16))
-        extras.append(more)
-    return jnp.concatenate(normed, 0), extras
+    return jnp.concatenate(normed, 0)
 
 
 def in_order(source, target, quarters):
@@ -92,26 +89,23 @@
             target[pl.ds(h * MOST + r, groups, stride=quarters * MOST), :] = own
 
 
-def project_kernel(x_ref, gain_ref, w_ref, stream_ref, tail_ref, route_ref, mixed_s, more_s, stream_s):
+def project_kernel(x_ref, gain_ref, w_ref, stream_ref, tail_ref, mixed_s, stream_s):
     quarters, part, _ = x_ref.shape
-    normed, extras = normed_rows(x_ref, gain_ref, w_ref.shape[0])
-    for h in range(quarters):
-        more_s[h * part : (h + 1) * part, :] = extras[h]
+    normed = normed_rows(x_ref, gain_ref, w_ref.shape[0])
     mixed_s[...] = jnp.dot(normed, w_ref[...], preferred_element_type=F32)
     in_order(mixed_s, stream_s, quarters)
-    in_order(more_s, route_ref, quarters)
     stream_ref[...] = stream_s[...].astype(BF16)
     tail_ref[...] = stream_s[quarters * part - 8 :, :].astype(BF16).astype(F32)
 
 
 def project_gate_kernel(x_ref, gain_ref, w_ref, gate_ref, mixed_s, gate_s):
-    normed, _ = normed_rows(x_ref, gain_ref, w_ref.shape[0])
+    normed = normed_rows(x_ref, gain_ref, w_ref.shape[0])
     mixed_s[...] = jnp.dot(normed, w_ref[...], preferred_element_type=F32)
     in_order(mixed_s, gate_s, x_ref.shape[0])
     gate_ref[...] = gate_s[...].astype(BF16)
 
 
-def conv_kernel(stream_ref, halo_ref, params_ref, wx_ref, act_ref, tile_ref, pad_s):
+def conv_kernel(stream_ref, halo_ref, params_ref, wx_ref, act_ref, tile_ref, pad_s, wide_s, tile_s):
     tokens, channels = stream_ref.shape
     pad_s[0:8, :] = halo_ref[...]
     pad_s[8:, :] = stream_ref[...].astype(F32)
@@ -121,66 +115,62 @@
         conv = conv + params_ref[TAPS + k : TAPS + k + 1, :] * pad_s[at : at + tokens, :]
     act = silu(conv).astype(BF16)
     act_ref[...] = act
-    rank = wx_ref.shape[1] - 2 * STATES
-    low = jnp.dot(act, wx_ref[:, :rank], preferred_element_type=F32)
-    maps = lax.dot_general(wx_ref[:, rank:], act, (((0,), (1,)), ((), ())), preferred_element_type=F32)
-    n = 0
-    for t in range(0, tokens, 8):
-        for c in range(0, rank, 128):
-            tile_ref[n] = low[t : t + 8, c : c + 128].astype(BF16)
-            n += 1
-    for s in range(0, 32, 8):
-        tile_ref[n] = maps[s : s + 8, 0:128].astype(BF16)
-        tile_ref[n + 1] = jnp.concatenate(
-            [maps[s : s + 8, 128:tokens], jnp.zeros((8, 256 - tokens), F32)], 1
-        ).astype(BF16)
-        n += 2
-    while n < tile_ref.shape[0]:
-        tile_ref[n] = jnp.zeros((8, 128), BF16)
-        n += 1
-
-
-def tile_sum_kernel(got_ref, out_ref):
-    total = jnp.sum(got_ref[...].astype(F32), axis=0).astype(BF16)
+    wide = jnp.dot(act, wx_ref[...], preferred_element_type=F32)
+    blocks = wide_s.shape[0]
+    for i in range(blocks):
+        wide_s[i] = wide[:, i * 128 : i * 128 + 128]
+    groups = tile_ref.shape[0]
+    maps = jnp.zeros((groups, 128), F32)
+    for r in range(MOST):
+        own = pl.ds(r, groups, stride=MOST)
+        for c in range(2):
+            tile_s[pl.ds(2 * r + c, groups, stride=8), :] = wide_s[c, own, :]
+        maps = maps + wide_s[2 + r, own, :]
+    tile_s[pl.ds(6, groups, stride=8), :] = maps
+    tile_s[pl.ds(7, groups, stride=8), :] = jnp.zeros((groups, 128), F32)
+    tile_ref[...] = tile_s[...].reshape(groups, 8, 128).astype(BF16)
+
+
+def tile_sum_kernel(got_ref, route_ref, _0, out_ref):
+    total = jnp.sum(got_ref[...].astype(F32), axis=0)
+    row = lax.broadcasted_iota(jnp.int32, total.shape, 0)
+    total = jnp.where(row == 7, route_ref[...], total).astype(BF16)
     out_ref[...] = jnp.broadcast_to(total[None], out_ref.shape)
 
 
-def scan_kernel(
-    back_ref, wdt_ref, params_ref, act_ref, wts_ref, out_ref, send_ref, low_s, step_s, drive_s
-):
-    tokens, rank = low_s.shape
-    n = 0
-    for t in range(0, tokens, 8):
-        for c in range(0, rank, 128):
-            low_s[t : t + 8, c : c + 128] = back_ref[n].astype(F32)
-            n += 1
-    maps = []
-    for s in range(0, 32, 8):
-        maps.append(jnp.concatenate([back_ref[n].astype(F32), back_ref[n + 1].astype(F32)], 1))
-        n += 2
+def scan_kernel(back_ref, wdt_ref, params_ref, act_ref, out_ref, send_ref, tile_s, low_s, step_s, drive_s):
+    _, tokens, half = low_s.shape
+    groups = back_ref.shape[0]
+    tile_s[...] = back_ref[...].astype(F32).reshape(groups * 8, 128)
+    for r in range(MOST):
+        for c in range(2):
+            low_s[c, pl.ds(r, groups, stride=MOST), :] = tile_s[pl.ds(2 * r + c, groups, stride=8), :]
+    blank = jnp.zeros((128 - groups, 128), F32)
+    maps = jnp.concatenate([tile_s[pl.ds(6, groups, stride=8), :], blank], 0).T
+    routes = jnp.concatenate([tile_s[pl.ds(7, groups, stride=8), :], blank], 0).T
+    out_ref[2 * tokens :, :] = maps
     decay = -jnp.exp(params_ref[0:STATES, :])
     states, channels = decay.shape
-    b = jnp.concatenate(maps[:2], 0)
-    c = jnp.concatenate(maps[2:], 0)
-    out_ref[2 * tokens : 2 * tokens + states, :] = c[:, :channels]
-    out_ref[2 * tokens + states :, :] = c[:, channels:]
-    step = softplus(jnp.dot(low_s[...].astype(BF16), wdt_ref[...], preferred_element_type=F32) + params_ref[STEP : STEP + 1, :])
+    step = jnp.dot(low_s[0].astype(BF16), wdt_ref[0:half, :], preferred_element_type=F32)
+    step = step + jnp.dot(low_s[1].astype(BF16), wdt_ref[half:, :], preferred_element_type=F32)
+    step = softplus(step + params_ref[STEP : STEP + 1, :])
     step_s[...] = step
     act = act_ref[...].astype(F32)
     drive_s[...] = step * act
     state = jnp.zeros((states, channels), F32)
     total = jnp.zeros((1, channels), F32)
     for t in range(tokens):
+        at, own = t % MOST * 32, t // MOST
         step_t = step_s[t : t + 1, :]
-        b_t = jnp.broadcast_to(b[:, t : t + 1], (states, channels))
-        c_t = jnp.broadcast_to(c[:, t : t + 1], (states, channels))
+        b_t = jnp.broadcast_to(maps[at : at + 16, own : own + 1], (states, channels))
+        c_t = jnp.broadcast_to(maps[at + 16 : at + 32, own : own + 1], (states, channels))
         state = jnp.exp(step_t * decay) * state + drive_s[t : t + 1, :] * b_t
         total = total + step_t
         out_ref[t : t + 1, :] = jnp.sum(c_t * state, axis=0, keepdims=True)
         out_ref[tokens + t : tokens + t + 1, :] = total
     out_ref[0:tokens, :] = out_ref[0:tokens, :] + params_ref[SKIP : SKIP + 1, :] * act
-    row = lax.broadcasted_iota(jnp.int32, (8, channels), 0)
-    tail = jnp.where(row == 0, total, jnp.where(row == 1, wts_ref[...], 0.0))
+    routes = jnp.concatenate([routes[0:6, 0:groups], routes[6:12, 0:groups]], 1)
+    tail = jnp.concatenate([total, routes, jnp.zeros((1, channels), F32)], 0)
     for k in range(send_ref.shape[0]):
         send_ref[k, 0:states, :] = state
         send_ref[k, states:, :] = tail
@@ -196,9 +186,10 @@
         total = all_ref[k, states : states + 1, :]
         later = jnp.exp(total * decay) * state + all_ref[k, 0:states, :]
         state = jnp.where(k < me, later, state)
-    c = [local_ref[at : at + states, :] for at in (2 * tokens, 2 * tokens + states)]
+    maps = local_ref[2 * tokens :, :]
     for t in range(tokens):
-        c_t = jnp.broadcast_to(c[t // channels][:, t % channels : t % channels + 1], (states, channels))
+        at, own = t % MOST * 32 + 16, t // MOST
+        c_t = jnp.broadcast_to(maps[at : at + 16, own : own + 1], (states, channels))
         term = c_t * (jnp.exp(local_ref[tokens + t : tokens + t + 1, :] * decay) * state)
         corr_s[t : t + 1, :] = jnp.sum(term, axis=0, keepdims=True)
     z = z_ref[...].astype(F32)
@@ -350,14 +341,12 @@
 
     w_x = lax.all_gather(w_in_x, "seq", axis=0, tiled=True)
 
-    own_routes = jnp.concatenate([route_ids.astype(BF16), route_weights], 1)
-    own = jnp.concatenate([x_in, jnp.pad(own_routes, ((0, 0), (0, 124)))], 1)
-    over_exp = lax.all_gather(own, "exp", axis=0, tiled=False)
+    over_exp = lax.all_gather(x_in, "exp", axis=0, tiled=False)
     quarter_rows = call(
         rows_kernel,
         "rows",
         like((n_hid, n_exp * rows, width + 128), BF16),
-        [(n_exp * rows, width + 128)],
+        [(n_exp * rows, width)],
         over_exp,
     )
     quarter_rows, w_out, w_in_z = lax.optimization_barrier((quarter_rows, w_out, w_in_z))
@@ -367,6 +356,12 @@
     ]
     w_out_here = lax.ppermute(w_out, ("seq", "hid"), route)
     w_out_all = lax.all_gather(w_out_here, "seq", axis=0, tiled=False)
+    w_maps = w_xproj[:, rank:]
+    w_maps = jnp.concatenate(
+        [w_xproj[:, :rank]] + [jnp.pad(w_maps, ((0, 0), (32 * r, 96 - 32 * r))) for r in range(rows)], 1
+    )
+    routes = jnp.concatenate([route_ids.astype(F32), route_weights.astype(F32)], 1).T.reshape(1, -1)
+    routes = jnp.pad(routes, ((0, 0), (0, 128 - routes.shape[1])))
     params = jnp.concatenate(
         [a_log, conv_weight, conv_bias[None], dt_bias[None], d_skip[None], jnp.zeros((1, channels), F32)], 0
     )
@@ -374,11 +369,11 @@
     x_block = lax.dynamic_slice(
         all_rows.reshape(n_hid, n_exp, rows, -1), (0, at_exp, 0, at_hid * cols), (n_hid, 1, rows, cols)
     ).reshape(block, cols)
-    stream, tail, routes = call(
+    stream, tail = call(
         project_kernel,
         "project",
-        (like((tokens, channels), BF16), like((8, channels), F32), like((tokens, 128), F32)),
-        [(tokens, channels), (tokens, 128), (tokens, channels)],
+        (like((tokens, channels), BF16), like((8, channels), F32)),
+        [(tokens, channels), (tokens, channels)],
         all_rows,
         norm_gain[None],
         near(w_x, "near_x"),
@@ -397,58 +392,57 @@
         conv_kernel,
         "conv",
         (like((tokens, channels), BF16), like((n_exp * n_hid, 8, 128), BF16)),
-        [(tokens + 8, channels)],
+        [(tokens + 8, channels), (5, tokens, 128), (n_exp * n_hid * 8, 128)],
         stream,
         halo,
         params,
-        w_xproj,
+        w_maps,
     )
 
     got = exchange(tiles, ("exp", "hid"))
-    back = exchange(call(tile_sum_kernel, "tile_sum", like(got.shape, BF16), [], got), ("exp", "hid"))
-
-    rows_ids = routes[:, :2].reshape(n_exp, -1)
-    rows_wts = routes[:, 2:4].reshape(n_exp, -1)
+    back = exchange(call(tile_sum_kernel, "tile_sum", like(got.shape, BF16), [], got, routes, gate_in, unread=1), ("exp", "hid"))
+
+    def pick(w, d):
+        return lax.dynamic_index_in_dim(w[0].reshape(n_hid, cols, -1), (at_hid + d) % n_hid, 0, keepdims=False)
+
+    def shift(w, d):
+        return lax.ppermute(pick(w, d), "hid", [(i, (i + d) % n_hid) for i in range(n_hid)])
+
+    gate_in, w_first = lax.optimization_barrier((gate_in, w_gate))
+    w_2 = shift(w_first, 2)
+    local, carried = call(
+        scan_kernel,
+        "scan",
+        (
+            like((2 * tokens + 128, channels), F32),
+            like((n_seq, states + 8, channels), F32),
+        ),
+        [(n_exp * n_hid * 8, 128), (2, tokens, 128), (tokens, channels), (tokens, channels)],
+        back,
+        w_dt,
+        params,
+        inner_act,
+    )
+    carried_all = exchange(carried, "seq")
+
+    routed = carried_all[:, states + 1 : states + 7].reshape(n_seq, 6, 2, -1).transpose(0, 2, 1, 3)
+    routed = routed.reshape(n_seq, 4, rows, -1).transpose(0, 3, 2, 1).reshape(n_seq * n_exp, block, 4)
+    rows_ids = routed[:, :, :2].reshape(n_seq * n_exp, -1)
+    rows_wts = routed[:, :, 2:].reshape(n_seq * n_exp, -1)
     n_rows = rows_ids.shape[1]
     upto = (jnp.arange(n_rows)[:, None] <= jnp.arange(n_rows)[None, :]).astype(F32)
     named = (rows_ids == at_exp.astype(F32)).astype(F32)
     place = jnp.dot(named, upto) * named
-    slot_wts = jnp.stack(
+    weights = jnp.stack(
         [jnp.sum(jnp.where(place == i + 1.0, rows_wts, 0.0), 1) for i in range(MOST)], 1
     ).reshape(1, -1)
-    n_slots = slot_wts.shape[1]
-    ids = lax.dynamic_index_in_dim(rows_ids, at_exp, 0, keepdims=False)
+    ids = lax.dynamic_index_in_dim(rows_ids, at_seq * n_exp + at_exp, 0, keepdims=False)
     onehot = (ids[:, None] == jnp.arange(n_exp, dtype=F32)[None, :]).astype(F32)
     position = jnp.sum(jnp.dot(upto.T, onehot) * onehot, 1) - 1.0
     target = ids * MOST + position
     select = (target[None, :] == jnp.arange(n_exp * MOST, dtype=F32)[:, None]).astype(F32)
     select = jnp.sum(select.reshape(n_exp * MOST, block, -1), 2)
     select = jnp.pad(select, ((0, 0), (0, 16 - block))).astype(BF16)
-
-    def pick(w, d):
-        return lax.dynamic_index_in_dim(w[0].reshape(n_hid, cols, -1), (at_hid + d) % n_hid, 0, keepdims=False)
-
-    def shift(w, d):
-        return lax.ppermute(pick(w, d), "hid", [(i, (i + d) % n_hid) for i in range(n_hid)])
-
-    slot_wts, w_first = lax.optimization_barrier((slot_wts, w_gate))
-    w_2 = shift(w_first, 2)
-    local, carried = call(
-        scan_kernel,
-        "scan",
-        (
-            like((2 * tokens + 2 * states, channels), F32),
-            like((n_seq, states + 8, channels), F32),
-        ),
-        [(tokens, rank), (tokens, channels), (tokens, channels)],
-        back,
-        w_dt,
-        params,
-        inner_act,
-        jnp.pad(slot_wts, ((0, 0), (0, channels - n_slots))),
-    )
-    carried_all = exchange(carried, "seq")
-    weights = carried_all[:, states + 1, :n_slots].reshape(1, -1)
     gated = call(
         gate_kernel,
         "gate",

time: 250 us -> 247 us (0.988)
  blocking collectives: 49.2 us -> 68.5 us
  waiting for transfers between devices: 69.9 us -> 54.3 us
  starting transfers between devices: 77.7 us -> 74.2 us
  other arithmetic: 2.95 us -> 0.42 us
    all_to_all x0 -> x1, blocking collectives: none -> 19.5 us  [exchange(): return lax.all_to_all(x, axis, split_axis=0, concat_axis=0, tiled=True)]
    all_to_all x8 -> x7, waiting for transfers between devices: 68.6 us -> 53 us  [exchange(): return lax.all_to_all(x, axis, split_axis=0, concat_axis=0, tiled=True)]
    all_to_all x8 -> x7, starting transfers between devices: 51.9 us -> 47.8 us  [exchange(): return lax.all_to_all(x, axis, split_axis=0, concat_axis=0, tiled=True)]
    unnamed x50 -> x48, local copies, waits for them, and re-layouts: 12.7 us -> 12.7 us
  transfers between devices with their start and end apart: 16 -> 15, of which waited for: 9 -> 8; matrix products, arithmetic and copies ran while one was open for 5% -> 4% of each run, Pallas kernels for 4% -> 3%
where the time goes in v5:
time: 247 us; the launch traced here: 246 us
  starting transfers between devices  74.2 us (30%)
  blocking collectives  68.5 us (28%)
  waiting for transfers between devices  54.3 us (22%)
  local copies, waits for them, and re-layouts  21.1 us (9%)
  between operations  14.4 us (6%)
  Pallas kernels  12.8 us (5%)
    all_to_all x7, waiting for transfers between devices, exchange(): return lax.all_to_all(x, axis, split_axis=0, concat_axis=0, tiled=True)  53 us
    all_to_all x7, starting transfers between devices, exchange(): return lax.all_to_all(x, axis, split_axis=0, concat_axis=0, tiled=True)  47.8 us
    all_gather x1, blocking collectives, shards(): over_exp = lax.all_gather(x_in, 'exp', axis=0, tiled=False)  32.5 us
    all_to_all x1, blocking collectives, exchange(): return lax.all_to_all(x, axis, split_axis=0, concat_axis=0, tiled=True)  19.5 us
    all_gather x1, blocking collectives, shards(): all_slots = lax.all_gather(slots, 'seq', axis=0, tiled=True)  16.5 us
    ppermute x1, starting transfers between devices, shards(): halo = lax.ppermute(tail, 'seq', [(i, i + 1) for i in range(n_seq - 1)])  16 us
    pallas_call x15, Pallas kernels, call(): pl.pallas_call(body, out_shape=out_shape, in_specs=[smem] * scalars + [vm...  12.8 us
    unnamed x48, local copies, waits for them, and re-layouts  12.7 us
  transfers between devices with their start and end apart: 15, of which 8 were waited for; matrix products, arithmetic and copies ran while one was open for 4% of the time, Pallas kernels for 3%

profile of v5, /device:TPU:1, one launch (start us, length us, event | category | flops | bytes accessed | tf_op | source)
XLA Modules:
  0.0 246.1 jit_solution(13826425490146938693)
XLA Ops:
  7.9 32.5 %all-gather.2.x_ref = bf16[16,3,4096]{2,1,0:T(4,128)(2,1)S(1)} all-gather(bf16[1,3,4096]{2,1,0:T(4,128)(2,1)} %bitcast.54), channel_id=2, replica_groups=mesh['seq'=8,'exp'=16,'hid'=4] {'exp'}, dimensions={0}, use_global_device_ids=true | all-gather | bytes 417792 | tf_op jit(solution)/shard_map/all_gather | solution.py:344
  42.0 4.2 %all-to-all-start = ((bf16[4,48,4224]{2,1,0:T(8,128)(2,1)}), bf16[4,48,4224]{2,1,0:T(8,128)(2,1)S(1)}, u32[]{:S(2)}, u32[]{:S(2)}) async-start(bf16[4,48,4224]{2,1,0:T(8,128)(2,1)} %rows.1), calls=%async_computation | async-start | bytes 3244032 | tf_op jit(solution)/shard_map/all_to_all | solution.py:17
  49.2 9.9 %all-to-all-done.x_ref = bf16[4,48,4224]{2,1,0:T(8,128)(2,1)S(1)} async-done(((bf16[4,48,4224]{2,1,0:T(8,128)(2,1)}), bf16[4,48,4224]{2,1,0:T(8,128)(2,1)S(1)}, u32[]{:S(2)}, u32[]{:S(2)}) %all-to-all-start) | async-done | bytes 1622048 | tf_op jit(solution)/shard_map/all_to_all | solution.py:17
  59.9 16.0 %collective-permute-start = (f32[8,128]{1,0:T(8,128)S(1)}, f32[8,128]{1,0:T(8,128)S(1)}, u32[]{:S(2)}, u32[]{:S(2)}) collective-permute-start(f32[8,128]{1,0:T(8,128)S(1)} %get-tuple-element.21), channel_id=1, source_target_pairs={{0,64},{64,128},{128,192},{192,256},{256,320},{320,384},{384,448},... | collective-permute-start | bytes 12296 | tf_op jit(solution)/shard_map/ppermute | solution.py:390
  77.6 12.8 %all-to-all-start.1 = ((bf16[64,8,128]{2,1,0:T(8,128)(2,1)}), bf16[64,8,128]{2,1,0:T(8,128)(2,1)S(1)}, u32[]{:S(2)}, u32[]{:S(2)}) async-start(bf16[64,8,128]{2,1,0:T(8,128)(2,1)} %get-tuple-element.22), calls=%async_computation.1 | async-start | bytes 262144 | tf_op jit(solution)/shard_map/all_to_all | solution.py:17
  92.6 2.2 dynamic-slice_bitcast_fusion.3
  94.7 4.4 %collective-permute-start.2 = (bf16[1024,384]{1,0:T(8,128)(2,1)}, bf16[1024,384]{1,0:T(8,128)(2,1)S(1)}, u32[]{:S(2)}, u32[]{:S(2)}) collective-permute-start(bf16[1024,384]{1,0:T(8,128)(2,1)} %dynamic-slice_bitcast_fusion.3), channel_id=1, source_target_pairs={{0,2},{1,3},{2,0},{3,1},{4,6},{5,7},{6,4},{7,5},{8,10},{9,11},{10,... | collective-permute-start | bytes 2359304 | tf_op jit(solution)/shard_map/ppermute | solution.py:409
  99.2 8.2 %all-to-all-done.1.got_ref = bf16[64,8,128]{2,1,0:T(8,128)(2,1)S(1)} async-done(((bf16[64,8,128]{2,1,0:T(8,128)(2,1)}), bf16[64,8,128]{2,1,0:T(8,128)(2,1)S(1)}, u32[]{:S(2)}, u32[]{:S(2)}) %all-to-all-start.1) | async-done | bytes 131104 | tf_op jit(solution)/shard_map/all_to_all | solution.py:17
  107.5 19.5 %all_to_all.40.back_ref = bf16[64,8,128]{2,1,0:T(8,128)(2,1)S(1)} all-to-all(bf16[64,8,128]{2,1,0:T(8,128)(2,1)S(1)} %tile_sum.1), channel_id=1, replica_groups=mesh['seq'=8,'exp'=16,'hid'=4] {'exp','hid'}, dimensions={0} | all-to-all | bytes 262144 | tf_op jit(solution)/shard_map/all_to_all | solution.py:17
  127.0 1.8 scan.1
  128.8 6.9 %all-to-all-start.3 = ((f32[8,24,128]{2,1,0:T(8,128)}), f32[8,24,128]{2,1,0:T(8,128)S(1)}, u32[]{:S(2)}, u32[]{:S(2)}) async-start(f32[8,24,128]{2,1,0:T(8,128)} %get-tuple-element.25), calls=%async_computation.3 | async-start | bytes 196608 | tf_op jit(solution)/shard_map/all_to_all | solution.py:17
  135.7 5.0 %all-to-all-done.3.all_ref = f32[8,24,128]{2,1,0:T(8,128)S(1)} async-done(((f32[8,24,128]{2,1,0:T(8,128)}), f32[8,24,128]{2,1,0:T(8,128)S(1)}, u32[]{:S(2)}, u32[]{:S(2)}) %all-to-all-start.3) | async-done | bytes 98336 | tf_op jit(solution)/shard_map/all_to_all | solution.py:17
  142.0 4.0 %all-to-all-start.4 = ((bf16[4,192,128]{2,1,0:T(8,128)(2,1)}), bf16[4,192,128]{2,1,0:T(8,128)(2,1)}, u32[]{:S(2)}, u32[]{:S(2)}) async-start(bf16[4,192,128]{2,1,0:T(8,128)(2,1)} %gate.1), calls=%async_computation.4 | async-start | bytes 393216 | tf_op jit(solution)/shard_map/all_to_all | solution.py:17
  147.4 3.9 %all-to-all-done.4.gated_ref = bf16[4,192,128]{2,1,0:T(8,128)(2,1)} async-done(((bf16[4,192,128]{2,1,0:T(8,128)(2,1)}), bf16[4,192,128]{2,1,0:T(8,128)(2,1)}, u32[]{:S(2)}, u32[]{:S(2)}) %all-to-all-start.4) | async-done | bytes 196640 | tf_op jit(solution)/shard_map/all_to_all | solution.py:17
  153.5 3.6 %all-to-all-start.5 = ((bf16[16,8,1536]{2,1,0:T(8,128)(2,1)}), bf16[16,8,1536]{2,1,0:T(8,128)(2,1)S(1)}, u32[]{:S(2)}, u32[]{:S(2)}) async-start(bf16[16,8,1536]{2,1,0:T(8,128)(2,1)} %copy-done.4), calls=%async_computation.5 | async-start | bytes 786432 | tf_op jit(solution)/shard_map/all_to_all | solution.py:17
  159.2 3.0 %dynamic-slice_bitcast_fusion = (bf16[1024,384]{1,0:T(8,128)(2,1)}, bf16[1024,384]{1,0:T(8,128)(2,1)S(1)}, bf16[1024,384]{1,0:T(8,128)(2,1)}) fusion(bf16[4,1024,384]{2,1,0:T(8,128)(2,1)} %bitcast.47, s32[]{:T(128)S(6)} %select_n.65, s32[]{:T(128)S(6)} %select_n.63, s32[]{:T(128)S(6)} %select_n.61), kind=kLoop, calls=%fused_computation.3 | loop fusion | bytes 4718604 | tf_op jit(solution)/shard_map/jit(dynamic_index_in_dim)/squeeze | solution.py:406
  162.2 2.8 %collective-permute-start.4 = (bf16[1024,384]{1,0:T(8,128)(2,1)}, bf16[1024,384]{1,0:T(8,128)(2,1)S(1)}, u32[]{:S(2)}, u32[]{:S(2)}) collective-permute-start(bf16[1024,384]{1,0:T(8,128)(2,1)} %get-tuple-element.39), channel_id=1, source_target_pairs={{0,3},{1,0},{2,1},{3,2},{4,7},{5,4},{6,5},{7,6},{8,11},{9,8},{10,9... | collective-permute-start | bytes 2359304 | tf_op jit(solution)/shard_map/ppermute | solution.py:409
  165.0 2.5 %collective-permute-start.3 = (bf16[1024,384]{1,0:T(8,128)(2,1)S(1)}, bf16[1024,384]{1,0:T(8,128)(2,1)S(1)}, u32[]{:S(2)}, u32[]{:S(2)}) collective-permute-start(bf16[1024,384]{1,0:T(8,128)(2,1)S(1)} %get-tuple-element.40), channel_id=1, source_target_pairs={{0,1},{1,2},{2,3},{3,0},{4,5},{5,6},{6,7},{7,4},{8,9},{9,10},{10,1... | collective-permute-start | bytes 2359304 | tf_op jit(solution)/shard_map/ppermute | solution.py:409
  168.1 5.2 %all-to-all-done.5.parts_ref = bf16[16,8,1536]{2,1,0:T(8,128)(2,1)S(1)} async-done(((bf16[16,8,1536]{2,1,0:T(8,128)(2,1)}), bf16[16,8,1536]{2,1,0:T(8,128)(2,1)S(1)}, u32[]{:S(2)}, u32[]{:S(2)}) %all-to-all-start.5) | async-done | bytes 393248 | tf_op jit(solution)/shard_map/all_to_all | solution.py:17
  174.1 12.8 %all-to-all-start.6 = ((bf16[16,8,384]{2,1,0:T(8,128)(2,1)}), bf16[16,8,384]{2,1,0:T(8,128)(2,1)S(1)}, u32[]{:S(2)}, u32[]{:S(2)}) async-start(bf16[16,8,384]{2,1,0:T(8,128)(2,1)} %get-tuple-element.31), calls=%async_computation.6 | async-start | bytes 196608 | tf_op jit(solution)/shard_map/all_to_all | solution.py:17
  194.3 4.5 %all-to-all-done.6.got_ref = bf16[16,8,384]{2,1,0:T(8,128)(2,1)S(1)} async-done(((bf16[16,8,384]{2,1,0:T(8,128)(2,1)}), bf16[16,8,384]{2,1,0:T(8,128)(2,1)S(1)}, u32[]{:S(2)}, u32[]{:S(2)}) %all-to-all-start.6) | async-done | bytes 98336 | tf_op jit(solution)/shard_map/all_to_all | solution.py:17
  198.9 16.5 %all_gather.27.tok_ref = bf16[384,1024]{1,0:T(8,128)(2,1)S(1)} all-gather(bf16[48,1024]{1,0:T(8,128)(2,1)S(1)} %slots.1), channel_id=1, replica_groups=mesh['seq'=8,'exp'=16,'hid'=4] {'seq'}, dimensions={0}, use_global_device_ids=true | all-gather | bytes 884736 | tf_op jit(solution)/shard_map/all_gather | solution.py:505
  217.8 3.5 %all-to-all-start.7 = ((bf16[4,400,384]{2,1,0:T(8,128)(2,1)}), bf16[4,400,384]{2,1,0:T(8,128)(2,1)S(1)}, u32[]{:S(2)}, u32[]{:S(2)}) async-start(bf16[4,400,384]{2,1,0:T(8,128)(2,1)} %copy-done), calls=%async_computation.7 | async-start | bytes 2457600 | tf_op jit(solution)/shard_map/all_to_all | solution.py:17
  222.0 16.3 %all-to-all-done.7.part_ref = bf16[4,400,384]{2,1,0:T(8,128)(2,1)S(1)} async-done(((bf16[4,400,384]{2,1,0:T(8,128)(2,1)}), bf16[4,400,384]{2,1,0:T(8,128)(2,1)S(1)}, u32[]{:S(2)}, u32[]{:S(2)}) %all-to-all-start.7) | async-done | bytes 1228832 | tf_op jit(solution)/shard_map/all_to_all | solution.py:17
  (116 shorter events, 29.8 us)
Async XLA Ops:
  7.2 40.7 %all-gather.7.cloned.1.call-start = ((), (), s32[]{:S(2)}) async-start(), calls=%async_computation.8 | async-start | bytes 1179648 | tf_op jit(solution)/shard_map/all_gather | solution.py:342
  7.9 82.6 %all-gather.9.cloned.1.call-start = ((), (), s32[]{:S(2)}) async-start(), calls=%async_computation.9 | async-start | bytes 1179648 | tf_op jit(solution)/shard_map/all_gather | solution.py:353
  42.0 17.1 %all-to-all-start = ((bf16[4,48,4224]{2,1,0:T(8,128)(2,1)}), bf16[4,48,4224]{2,1,0:T(8,128)(2,1)S(1)}, u32[]{:S(2)}, u32[]{:S(2)}) async-start(bf16[4,48,4224]{2,1,0:T(8,128)(2,1)} %rows.1), calls=%async_computation | async-start | bytes 3244032 | tf_op jit(solution)/shard_map/all_to_all | solution.py:17
  46.2 12.9 %copy-start.12 = (f32[4096]{0:T(1024)S(1)}, f32[4096]{0:T(1024)}, u32[]{:S(2)}) copy-start(f32[4096]{0:T(1024)} %param.17) | copy-start | bytes 49156
  46.2 99.9 %all-gather.11.cloned.1.call-start = ((), (), s32[]{:S(2)}) async-start(), calls=%async_computation.10 | async-start | bytes 1179648 | tf_op jit(solution)/shard_map/all_gather | solution.py:358
  46.2 0.7 collective-permute-start.1
  49.1 26.9 %copy-start.15 = (f32[16,128]{1,0:T(8,128)S(1)}, f32[16,128]{1,0:T(8,128)}, u32[]{:S(2)}) copy-start(f32[16,128]{1,0:T(8,128)} %param.25) | copy-start | bytes 24580
  49.2 26.9 %copy-start.16 = (f32[4,128]{1,0:T(4,128)S(1)}, f32[4,128]{1,0:T(4,128)}, u32[]{:S(2)}) copy-start(f32[4,128]{1,0:T(4,128)} %param.20) | copy-start | bytes 6148
  49.2 26.9 %copy-start.18 = (f32[128]{0:T(128)S(1)}, f32[128]{0:T(128)}, u32[]{:S(2)}) copy-start(f32[128]{0:T(128)} %param.21) | copy-start | bytes 1540
  49.2 26.9 %copy-start.19 = (f32[128]{0:T(128)S(1)}, f32[128]{0:T(128)}, u32[]{:S(2)}) copy-start(f32[128]{0:T(128)} %param.24) | copy-start | bytes 1540
  49.2 26.9 %copy-start.20 = (f32[128]{0:T(128)S(1)}, f32[128]{0:T(128)}, u32[]{:S(2)}) copy-start(f32[128]{0:T(128)} %param.26) | copy-start | bytes 1540
  59.1 31.3 %copy-start.17 = (s32[3,2]{0,1:T(2,128)S(1)}, s32[3,2]{0,1:T(2,128)}, u32[]{:S(2)}) copy-start(s32[3,2]{0,1:T(2,128)} %param.29) | copy-start | bytes 76
  59.1 31.4 %copy-start.22 = (bf16[3,2]{0,1:T(2,128)(2,1)S(1)}, bf16[3,2]{0,1:T(2,128)(2,1)}, u32[]{:S(2)}) copy-start(bf16[3,2]{0,1:T(2,128)(2,1)} %param.30) | copy-start | bytes 40
  59.9 16.8 %collective-permute-start = (f32[8,128]{1,0:T(8,128)S(1)}, f32[8,128]{1,0:T(8,128)S(1)}, u32[]{:S(2)}, u32[]{:S(2)}) collective-permute-start(f32[8,128]{1,0:T(8,128)S(1)} %get-tuple-element.21), channel_id=1, source_target_pairs={{0,64},{64,128},{128,192},{192,256},{256,320},{320,384},{384,448},... | collective-permute-start | bytes 12296 | tf_op jit(solution)/shard_map/ppermute | solution.py:390
  77.6 29.8 %all-to-all-start.1 = ((bf16[64,8,128]{2,1,0:T(8,128)(2,1)}), bf16[64,8,128]{2,1,0:T(8,128)(2,1)S(1)}, u32[]{:S(2)}, u32[]{:S(2)}) async-start(bf16[64,8,128]{2,1,0:T(8,128)(2,1)} %get-tuple-element.22), calls=%async_computation.1 | async-start | bytes 262144 | tf_op jit(solution)/shard_map/all_to_all | solution.py:17
  92.5 34.5 %copy-start.13 = (bf16[256,128]{1,0:T(8,128)(2,1)S(1)}, bf16[256,128]{1,0:T(8,128)(2,1)}, u32[]{:S(2)}) copy-start(bf16[256,128]{1,0:T(8,128)(2,1)} %wdt_ref.1) | copy-start | bytes 196612
  94.7 52.6 %collective-permute-start.2 = (bf16[1024,384]{1,0:T(8,128)(2,1)}, bf16[1024,384]{1,0:T(8,128)(2,1)S(1)}, u32[]{:S(2)}, u32[]{:S(2)}) collective-permute-start(bf16[1024,384]{1,0:T(8,128)(2,1)} %dynamic-slice_bitcast_fusion.3), channel_id=1, source_target_pairs={{0,2},{1,3},{2,0},{3,1},{4,6},{5,7},{6,4},{7,5},{8,10},{9,11},{10,... | collective-permute-start | bytes 2359304 | tf_op jit(solution)/shard_map/ppermute | solution.py:409
  128.8 11.9 %all-to-all-start.3 = ((f32[8,24,128]{2,1,0:T(8,128)}), f32[8,24,128]{2,1,0:T(8,128)S(1)}, u32[]{:S(2)}, u32[]{:S(2)}) async-start(f32[8,24,128]{2,1,0:T(8,128)} %get-tuple-element.25), calls=%async_computation.3 | async-start | bytes 196608 | tf_op jit(solution)/shard_map/all_to_all | solution.py:17
  142.0 9.2 %all-to-all-start.4 = ((bf16[4,192,128]{2,1,0:T(8,128)(2,1)}), bf16[4,192,128]{2,1,0:T(8,128)(2,1)}, u32[]{:S(2)}, u32[]{:S(2)}) async-start(bf16[4,192,128]{2,1,0:T(8,128)(2,1)} %gate.1), calls=%async_computation.4 | async-start | bytes 393216 | tf_op jit(solution)/shard_map/all_to_all | solution.py:17
  153.5 19.7 %all-to-all-start.5 = ((bf16[16,8,1536]{2,1,0:T(8,128)(2,1)}), bf16[16,8,1536]{2,1,0:T(8,128)(2,1)S(1)}, u32[]{:S(2)}, u32[]{:S(2)}) async-start(bf16[16,8,1536]{2,1,0:T(8,128)(2,1)} %copy-done.4), calls=%async_computation.5 | async-start | bytes 786432 | tf_op jit(solution)/shard_map/all_to_all | solution.py:17
  162.2 25.5 %collective-permute-start.4 = (bf16[1024,384]{1,0:T(8,128)(2,1)}, bf16[1024,384]{1,0:T(8,128)(2,1)S(1)}, u32[]{:S(2)}, u32[]{:S(2)}) collective-permute-start(bf16[1024,384]{1,0:T(8,128)(2,1)} %get-tuple-element.39), channel_id=1, source_target_pairs={{0,3},{1,0},{2,1},{3,2},{4,7},{5,4},{6,5},{7,6},{8,11},{9,8},{10,9... | collective-permute-start | bytes 2359304 | tf_op jit(solution)/shard_map/ppermute | solution.py:409
  165.0 23.6 %collective-permute-start.3 = (bf16[1024,384]{1,0:T(8,128)(2,1)S(1)}, bf16[1024,384]{1,0:T(8,128)(2,1)S(1)}, u32[]{:S(2)}, u32[]{:S(2)}) collective-permute-start(bf16[1024,384]{1,0:T(8,128)(2,1)S(1)} %get-tuple-element.40), channel_id=1, source_target_pairs={{0,1},{1,2},{2,3},{3,0},{4,5},{5,6},{6,7},{7,4},{8,9},{9,10},{10,1... | collective-permute-start | bytes 2359304 | tf_op jit(solution)/shard_map/ppermute | solution.py:409
  174.1 24.7 %all-to-all-start.6 = ((bf16[16,8,384]{2,1,0:T(8,128)(2,1)}), bf16[16,8,384]{2,1,0:T(8,128)(2,1)S(1)}, u32[]{:S(2)}, u32[]{:S(2)}) async-start(bf16[16,8,384]{2,1,0:T(8,128)(2,1)} %get-tuple-element.31), calls=%async_computation.6 | async-start | bytes 196608 | tf_op jit(solution)/shard_map/all_to_all | solution.py:17
  217.8 20.5 %all-to-all-start.7 = ((bf16[4,400,384]{2,1,0:T(8,128)(2,1)}), bf16[4,400,384]{2,1,0:T(8,128)(2,1)S(1)}, u32[]{:S(2)}, u32[]{:S(2)}) async-start(bf16[4,400,384]{2,1,0:T(8,128)(2,1)} %copy-done), calls=%async_computation.7 | async-start | bytes 2457600 | tf_op jit(solution)/shard_map/all_to_all | solution.py:17
  (16 other events, 37.6 us)
Sparse Core Ops, SparseCore 0:
  10.1 36.9 all-gather.6
  49.3 31.7 all-gather.8
  83.2 30.0 all-gather.10

commit v6 on v5

--- a/solution.py
+++ b/solution.py
@@ -355,7 +355,6 @@
         (s * n_hid + h, (h * per + s % per) * n_hid + s // per) for s in range(n_seq) for h in range(n_hid)
     ]
     w_out_here = lax.ppermute(w_out, ("seq", "hid"), route)
-    w_out_all = lax.all_gather(w_out_here, "seq", axis=0, tiled=False)
     w_maps = w_xproj[:, rank:]
     w_maps = jnp.concatenate(
         [w_xproj[:, :rank]] + [jnp.pad(w_maps, ((0, 0), (32 * r, 96 - 32 * r))) for r in range(rows)], 1
@@ -399,6 +398,8 @@
         w_maps,
     )
 
+    tiles, w_out_here = lax.optimization_barrier((tiles, w_out_here))
+    w_out_all = lax.all_gather(w_out_here, "seq", axis=0, tiled=False)
     got = exchange(tiles, ("exp", "hid"))
     back = exchange(call(tile_sum_kernel, "tile_sum", like(got.shape, BF16), [], got, routes, gate_in, unread=1), ("exp", "hid"))
 

time: 247 us -> 244 us (0.988)
  starting transfers between devices: 74.2 us -> 67.5 us
  waiting for transfers between devices: 54.3 us -> 58.1 us
    ppermute x1, starting transfers between devices: 16 us -> 12.2 us  [shards(): halo = lax.ppermute(tail, 'seq', [(i, i + 1) for i in range(n_seq - 1)])]
    all_to_all x7, starting transfers between devices: 47.8 us -> 44.8 us  [exchange(): return lax.all_to_all(x, axis, split_axis=0, concat_axis=0, tiled=True)]
  transfers between devices with their start and end apart: 15 -> 15, of which waited for: 8 -> 8; matrix products, arithmetic and copies ran while one was open for 4% -> 4% of each run, Pallas kernels for 3% -> 4%
where the time goes in v6:
time: 244 us; the launch traced here: 243 us
  blocking collectives  68.4 us (28%)
  starting transfers between devices  67.5 us (28%)
  waiting for transfers between devices  58.1 us (24%)
  local copies, waits for them, and re-layouts  21.1 us (9%)
  between operations  14.3 us (6%)
  Pallas kernels  12.8 us (5%)
    all_to_all x7, waiting for transfers between devices, exchange(): return lax.all_to_all(x, axis, split_axis=0, concat_axis=0, tiled=True)  54.3 us
    all_to_all x7, starting transfers between devices, exchange(): return lax.all_to_all(x, axis, split_axis=0, concat_axis=0, tiled=True)  44.8 us
    all_gather x1, blocking collectives, shards(): over_exp = lax.all_gather(x_in, 'exp', axis=0, tiled=False)  32.5 us
    all_to_all x1, blocking collectives, exchange(): return lax.all_to_all(x, axis, split_axis=0, concat_axis=0, tiled=True)  19.5 us
    all_gather x1, blocking collectives, shards(): all_slots = lax.all_gather(slots, 'seq', axis=0, tiled=True)  16.5 us
    pallas_call x15, Pallas kernels, call(): pl.pallas_call(body, out_shape=out_shape, in_specs=[smem] * scalars + [vm...  12.8 us
    unnamed x48, local copies, waits for them, and re-layouts  12.7 us
    ppermute x1, starting transfers between devices, shards(): halo = lax.ppermute(tail, 'seq', [(i, i + 1) for i in range(n_seq - 1)])  12.2 us
  transfers between devices with their start and end apart: 15, of which 8 were waited for; matrix products, arithmetic and copies ran while one was open for 4% of the time, Pallas kernels for 4%

profile of v6, /device:TPU:1, one launch (start us, length us, event | category | flops | bytes accessed | tf_op | source)
XLA Modules:
  0.0 243.0 jit_solution(14225608305248918159)
XLA Ops:
  7.9 32.5 %all-gather.2.x_ref = bf16[16,3,4096]{2,1,0:T(4,128)(2,1)S(1)} all-gather(bf16[1,3,4096]{2,1,0:T(4,128)(2,1)} %bitcast.54), channel_id=2, replica_groups=mesh['seq'=8,'exp'=16,'hid'=4] {'exp'}, dimensions={0}, use_global_device_ids=true | all-gather | bytes 417792 | tf_op jit(solution)/shard_map/all_gather | solution.py:344
  42.0 4.2 %all-to-all-start = ((bf16[4,48,4224]{2,1,0:T(8,128)(2,1)}), bf16[4,48,4224]{2,1,0:T(8,128)(2,1)S(1)}, u32[]{:S(2)}, u32[]{:S(2)}) async-start(bf16[4,48,4224]{2,1,0:T(8,128)(2,1)} %rows.1), calls=%async_computation | async-start | bytes 3244032 | tf_op jit(solution)/shard_map/all_to_all | solution.py:17
  48.5 10.6 %all-to-all-done.x_ref = bf16[4,48,4224]{2,1,0:T(8,128)(2,1)S(1)} async-done(((bf16[4,48,4224]{2,1,0:T(8,128)(2,1)}), bf16[4,48,4224]{2,1,0:T(8,128)(2,1)S(1)}, u32[]{:S(2)}, u32[]{:S(2)}) %all-to-all-start) | async-done | bytes 1622048 | tf_op jit(solution)/shard_map/all_to_all | solution.py:17
  59.9 12.2 %collective-permute-start = (f32[8,128]{1,0:T(8,128)S(1)}, f32[8,128]{1,0:T(8,128)S(1)}, u32[]{:S(2)}, u32[]{:S(2)}) collective-permute-start(f32[8,128]{1,0:T(8,128)S(1)} %get-tuple-element.23), channel_id=1, source_target_pairs={{0,64},{64,128},{128,192},{192,256},{256,320},{320,384},{384,448},... | collective-permute-start | bytes 12296 | tf_op jit(solution)/shard_map/ppermute | solution.py:389
  72.3 3.0 %collective-permute-done.halo_ref = f32[8,128]{1,0:T(8,128)S(1)} collective-permute-done((f32[8,128]{1,0:T(8,128)S(1)}, f32[8,128]{1,0:T(8,128)S(1)}, u32[]{:S(2)}, u32[]{:S(2)}) %collective-permute-start) | collective-permute-done | bytes 4128 | tf_op jit(solution)/shard_map/ppermute | solution.py:389
  76.9 8.8 %all-to-all-start.1 = ((bf16[64,8,128]{2,1,0:T(8,128)(2,1)}), bf16[64,8,128]{2,1,0:T(8,128)(2,1)S(1)}, u32[]{:S(2)}, u32[]{:S(2)}) async-start(bf16[64,8,128]{2,1,0:T(8,128)(2,1)} %get-tuple-element.26), calls=%async_computation.1 | async-start | bytes 262144 | tf_op jit(solution)/shard_map/all_to_all | solution.py:17
  87.8 2.1 dynamic-slice_bitcast_fusion.3
  90.0 4.4 %collective-permute-start.2 = (bf16[1024,384]{1,0:T(8,128)(2,1)}, bf16[1024,384]{1,0:T(8,128)(2,1)S(1)}, u32[]{:S(2)}, u32[]{:S(2)}) collective-permute-start(bf16[1024,384]{1,0:T(8,128)(2,1)} %dynamic-slice_bitcast_fusion.3), channel_id=1, source_target_pairs={{0,2},{1,3},{2,0},{3,1},{4,6},{5,7},{6,4},{7,5},{8,10},{9,11},{10,... | collective-permute-start | bytes 2359304 | tf_op jit(solution)/shard_map/ppermute | solution.py:410
  94.5 8.8 %all-to-all-done.1.got_ref = bf16[64,8,128]{2,1,0:T(8,128)(2,1)S(1)} async-done(((bf16[64,8,128]{2,1,0:T(8,128)(2,1)}), bf16[64,8,128]{2,1,0:T(8,128)(2,1)S(1)}, u32[]{:S(2)}, u32[]{:S(2)}) %all-to-all-start.1) | async-done | bytes 131104 | tf_op jit(solution)/shard_map/all_to_all | solution.py:17
  103.4 19.5 %all_to_all.40.back_ref = bf16[64,8,128]{2,1,0:T(8,128)(2,1)S(1)} all-to-all(bf16[64,8,128]{2,1,0:T(8,128)(2,1)S(1)} %tile_sum.1), channel_id=1, replica_groups=mesh['seq'=8,'exp'=16,'hid'=4] {'exp','hid'}, dimensions={0} | all-to-all | bytes 262144 | tf_op jit(solution)/shard_map/all_to_all | solution.py:17
  124.7 7.9 %all-to-all-start.3 = ((f32[8,24,128]{2,1,0:T(8,128)}), f32[8,24,128]{2,1,0:T(8,128)S(1)}, u32[]{:S(2)}, u32[]{:S(2)}) async-start(f32[8,24,128]{2,1,0:T(8,128)} %get-tuple-element.29), calls=%async_computation.3 | async-start | bytes 196608 | tf_op jit(solution)/shard_map/all_to_all | solution.py:17
  132.6 5.0 %all-to-all-done.3.all_ref = f32[8,24,128]{2,1,0:T(8,128)S(1)} async-done(((f32[8,24,128]{2,1,0:T(8,128)}), f32[8,24,128]{2,1,0:T(8,128)S(1)}, u32[]{:S(2)}, u32[]{:S(2)}) %all-to-all-start.3) | async-done | bytes 98336 | tf_op jit(solution)/shard_map/all_to_all | solution.py:17
  138.9 4.0 %all-to-all-start.4 = ((bf16[4,192,128]{2,1,0:T(8,128)(2,1)}), bf16[4,192,128]{2,1,0:T(8,128)(2,1)}, u32[]{:S(2)}, u32[]{:S(2)}) async-start(bf16[4,192,128]{2,1,0:T(8,128)(2,1)} %gate.1), calls=%async_computation.4 | async-start | bytes 393216 | tf_op jit(solution)/shard_map/all_to_all | solution.py:17
  144.2 3.9 %all-to-all-done.4.gated_ref = bf16[4,192,128]{2,1,0:T(8,128)(2,1)} async-done(((bf16[4,192,128]{2,1,0:T(8,128)(2,1)}), bf16[4,192,128]{2,1,0:T(8,128)(2,1)}, u32[]{:S(2)}, u32[]{:S(2)}) %all-to-all-start.4) | async-done | bytes 196640 | tf_op jit(solution)/shard_map/all_to_all | solution.py:17
  150.4 3.6 %all-to-all-start.5 = ((bf16[16,8,1536]{2,1,0:T(8,128)(2,1)}), bf16[16,8,1536]{2,1,0:T(8,128)(2,1)S(1)}, u32[]{:S(2)}, u32[]{:S(2)}) async-start(bf16[16,8,1536]{2,1,0:T(8,128)(2,1)} %copy-done.4), calls=%async_computation.5 | async-start | bytes 786432 | tf_op jit(solution)/shard_map/all_to_all | solution.py:17
  156.0 3.0 %dynamic-slice_bitcast_fusion = (bf16[1024,384]{1,0:T(8,128)(2,1)}, bf16[1024,384]{1,0:T(8,128)(2,1)S(1)}, bf16[1024,384]{1,0:T(8,128)(2,1)}) fusion(bf16[4,1024,384]{2,1,0:T(8,128)(2,1)} %bitcast.47, s32[]{:T(128)S(6)} %select_n.65, s32[]{:T(128)S(6)} %select_n.63, s32[]{:T(128)S(6)} %select_n.61), kind=kLoop, calls=%fused_computation.3 | loop fusion | bytes 4718604 | tf_op jit(solution)/shard_map/jit(dynamic_index_in_dim)/squeeze | solution.py:407
  159.1 2.8 %collective-permute-start.4 = (bf16[1024,384]{1,0:T(8,128)(2,1)}, bf16[1024,384]{1,0:T(8,128)(2,1)S(1)}, u32[]{:S(2)}, u32[]{:S(2)}) collective-permute-start(bf16[1024,384]{1,0:T(8,128)(2,1)} %get-tuple-element.43), channel_id=1, source_target_pairs={{0,3},{1,0},{2,1},{3,2},{4,7},{5,4},{6,5},{7,6},{8,11},{9,8},{10,9... | collective-permute-start | bytes 2359304 | tf_op jit(solution)/shard_map/ppermute | solution.py:410
  161.8 2.5 %collective-permute-start.3 = (bf16[1024,384]{1,0:T(8,128)(2,1)S(1)}, bf16[1024,384]{1,0:T(8,128)(2,1)S(1)}, u32[]{:S(2)}, u32[]{:S(2)}) collective-permute-start(bf16[1024,384]{1,0:T(8,128)(2,1)S(1)} %get-tuple-element.44), channel_id=1, source_target_pairs={{0,1},{1,2},{2,3},{3,0},{4,5},{5,6},{6,7},{7,4},{8,9},{9,10},{10,1... | collective-permute-start | bytes 2359304 | tf_op jit(solution)/shard_map/ppermute | solution.py:410
  164.9 5.2 %all-to-all-done.5.parts_ref = bf16[16,8,1536]{2,1,0:T(8,128)(2,1)S(1)} async-done(((bf16[16,8,1536]{2,1,0:T(8,128)(2,1)}), bf16[16,8,1536]{2,1,0:T(8,128)(2,1)S(1)}, u32[]{:S(2)}, u32[]{:S(2)}) %all-to-all-start.5) | async-done | bytes 393248 | tf_op jit(solution)/shard_map/all_to_all | solution.py:17
  171.0 12.8 %all-to-all-start.6 = ((bf16[16,8,384]{2,1,0:T(8,128)(2,1)}), bf16[16,8,384]{2,1,0:T(8,128)(2,1)S(1)}, u32[]{:S(2)}, u32[]{:S(2)}) async-start(bf16[16,8,384]{2,1,0:T(8,128)(2,1)} %get-tuple-element.35), calls=%async_computation.6 | async-start | bytes 196608 | tf_op jit(solution)/shard_map/all_to_all | solution.py:17
  191.2 4.5 %all-to-all-done.6.got_ref = bf16[16,8,384]{2,1,0:T(8,128)(2,1)S(1)} async-done(((bf16[16,8,384]{2,1,0:T(8,128)(2,1)}), bf16[16,8,384]{2,1,0:T(8,128)(2,1)S(1)}, u32[]{:S(2)}, u32[]{:S(2)}) %all-to-all-start.6) | async-done | bytes 98336 | tf_op jit(solution)/shard_map/all_to_all | solution.py:17
  195.8 16.5 %all_gather.27.tok_ref = bf16[384,1024]{1,0:T(8,128)(2,1)S(1)} all-gather(bf16[48,1024]{1,0:T(8,128)(2,1)S(1)} %slots.1), channel_id=1, replica_groups=mesh['seq'=8,'exp'=16,'hid'=4] {'seq'}, dimensions={0}, use_global_device_ids=true | all-gather | bytes 884736 | tf_op jit(solution)/shard_map/all_gather | solution.py:506
  214.7 3.5 %all-to-all-start.7 = ((bf16[4,400,384]{2,1,0:T(8,128)(2,1)}), bf16[4,400,384]{2,1,0:T(8,128)(2,1)S(1)}, u32[]{:S(2)}, u32[]{:S(2)}) async-start(bf16[4,400,384]{2,1,0:T(8,128)(2,1)} %copy-done), calls=%async_computation.7 | async-start | bytes 2457600 | tf_op jit(solution)/shard_map/all_to_all | solution.py:17
  218.9 16.3 %all-to-all-done.7.part_ref = bf16[4,400,384]{2,1,0:T(8,128)(2,1)S(1)} async-done(((bf16[4,400,384]{2,1,0:T(8,128)(2,1)}), bf16[4,400,384]{2,1,0:T(8,128)(2,1)S(1)}, u32[]{:S(2)}, u32[]{:S(2)}) %all-to-all-start.7) | async-done | bytes 1228832 | tf_op jit(solution)/shard_map/all_to_all | solution.py:17
  (116 shorter events, 31.1 us)
Async XLA Ops:
  7.2 40.0 %all-gather.7.cloned.1.call-start = ((), (), s32[]{:S(2)}) async-start(), calls=%async_computation.8 | async-start | bytes 1179648 | tf_op jit(solution)/shard_map/all_gather | solution.py:342
  7.9 77.9 %all-gather.9.cloned.1.call-start = ((), (), s32[]{:S(2)}) async-start(), calls=%async_computation.9 | async-start | bytes 1179648 | tf_op jit(solution)/shard_map/all_gather | solution.py:353
  42.0 17.1 %all-to-all-start = ((bf16[4,48,4224]{2,1,0:T(8,128)(2,1)}), bf16[4,48,4224]{2,1,0:T(8,128)(2,1)S(1)}, u32[]{:S(2)}, u32[]{:S(2)}) async-start(bf16[4,48,4224]{2,1,0:T(8,128)(2,1)} %rows.1), calls=%async_computation | async-start | bytes 3244032 | tf_op jit(solution)/shard_map/all_to_all | solution.py:17
  46.2 12.9 %copy-start.12 = (f32[4096]{0:T(1024)S(1)}, f32[4096]{0:T(1024)}, u32[]{:S(2)}) copy-start(f32[4096]{0:T(1024)} %param.17) | copy-start | bytes 49156
  46.2 96.7 %all-gather.11.cloned.1.call-start = ((), (), s32[]{:S(2)}) async-start(), calls=%async_computation.10 | async-start | bytes 1179648 | tf_op jit(solution)/shard_map/all_gather | solution.py:402
  46.2 30.1 %collective-permute-start.1 = (bf16[128,512]{1,0:T(8,128)(2,1)S(1)}, bf16[128,512]{1,0:T(8,128)(2,1)S(1)}, u32[]{:S(2)}, u32[]{:S(2)}) collective-permute-start(bf16[128,512]{1,0:T(8,128)(2,1)S(1)} %copy-done.21), channel_id=1, source_target_pairs={{0,0},{1,128},{2,256},{3,384},{64,64},{65,192},{66,320},{67,448},{... | collective-permute-start | bytes 393224 | tf_op jit(solution)/shard_map/ppermute | solution.py:357
  48.5 23.8 %copy-start.15 = (f32[16,128]{1,0:T(8,128)S(1)}, f32[16,128]{1,0:T(8,128)}, u32[]{:S(2)}) copy-start(f32[16,128]{1,0:T(8,128)} %param.25) | copy-start | bytes 24580
  48.5 23.8 %copy-start.16 = (f32[4,128]{1,0:T(4,128)S(1)}, f32[4,128]{1,0:T(4,128)}, u32[]{:S(2)}) copy-start(f32[4,128]{1,0:T(4,128)} %param.20) | copy-start | bytes 6148
  48.5 23.8 %copy-start.18 = (f32[128]{0:T(128)S(1)}, f32[128]{0:T(128)}, u32[]{:S(2)}) copy-start(f32[128]{0:T(128)} %param.21) | copy-start | bytes 1540
  48.5 23.8 %copy-start.19 = (f32[128]{0:T(128)S(1)}, f32[128]{0:T(128)}, u32[]{:S(2)}) copy-start(f32[128]{0:T(128)} %param.24) | copy-start | bytes 1540
  48.5 23.8 %copy-start.20 = (f32[128]{0:T(128)S(1)}, f32[128]{0:T(128)}, u32[]{:S(2)}) copy-start(f32[128]{0:T(128)} %param.26) | copy-start | bytes 1540
  59.1 26.6 %copy-start.17 = (s32[3,2]{0,1:T(2,128)S(1)}, s32[3,2]{0,1:T(2,128)}, u32[]{:S(2)}) copy-start(s32[3,2]{0,1:T(2,128)} %param.29) | copy-start | bytes 76
  59.1 26.6 %copy-start.22 = (bf16[3,2]{0,1:T(2,128)(2,1)S(1)}, bf16[3,2]{0,1:T(2,128)(2,1)}, u32[]{:S(2)}) copy-start(bf16[3,2]{0,1:T(2,128)(2,1)} %param.30) | copy-start | bytes 40
  59.9 15.4 %collective-permute-start = (f32[8,128]{1,0:T(8,128)S(1)}, f32[8,128]{1,0:T(8,128)S(1)}, u32[]{:S(2)}, u32[]{:S(2)}) collective-permute-start(f32[8,128]{1,0:T(8,128)S(1)} %get-tuple-element.23), channel_id=1, source_target_pairs={{0,64},{64,128},{128,192},{192,256},{256,320},{320,384},{384,448},... | collective-permute-start | bytes 12296 | tf_op jit(solution)/shard_map/ppermute | solution.py:389
  76.9 26.4 %all-to-all-start.1 = ((bf16[64,8,128]{2,1,0:T(8,128)(2,1)}), bf16[64,8,128]{2,1,0:T(8,128)(2,1)S(1)}, u32[]{:S(2)}, u32[]{:S(2)}) async-start(bf16[64,8,128]{2,1,0:T(8,128)(2,1)} %get-tuple-element.26), calls=%async_computation.1 | async-start | bytes 262144 | tf_op jit(solution)/shard_map/all_to_all | solution.py:17
  87.8 35.1 %copy-start.13 = (bf16[256,128]{1,0:T(8,128)(2,1)S(1)}, bf16[256,128]{1,0:T(8,128)(2,1)}, u32[]{:S(2)}) copy-start(bf16[256,128]{1,0:T(8,128)(2,1)} %wdt_ref.1) | copy-start | bytes 196612
  90.0 54.3 %collective-permute-start.2 = (bf16[1024,384]{1,0:T(8,128)(2,1)}, bf16[1024,384]{1,0:T(8,128)(2,1)S(1)}, u32[]{:S(2)}, u32[]{:S(2)}) collective-permute-start(bf16[1024,384]{1,0:T(8,128)(2,1)} %dynamic-slice_bitcast_fusion.3), channel_id=1, source_target_pairs={{0,2},{1,3},{2,0},{3,1},{4,6},{5,7},{6,4},{7,5},{8,10},{9,11},{10,... | collective-permute-start | bytes 2359304 | tf_op jit(solution)/shard_map/ppermute | solution.py:410
  124.7 12.9 %all-to-all-start.3 = ((f32[8,24,128]{2,1,0:T(8,128)}), f32[8,24,128]{2,1,0:T(8,128)S(1)}, u32[]{:S(2)}, u32[]{:S(2)}) async-start(f32[8,24,128]{2,1,0:T(8,128)} %get-tuple-element.29), calls=%async_computation.3 | async-start | bytes 196608 | tf_op jit(solution)/shard_map/all_to_all | solution.py:17
  138.9 9.2 %all-to-all-start.4 = ((bf16[4,192,128]{2,1,0:T(8,128)(2,1)}), bf16[4,192,128]{2,1,0:T(8,128)(2,1)}, u32[]{:S(2)}, u32[]{:S(2)}) async-start(bf16[4,192,128]{2,1,0:T(8,128)(2,1)} %gate.1), calls=%async_computation.4 | async-start | bytes 393216 | tf_op jit(solution)/shard_map/all_to_all | solution.py:17
  150.4 19.7 %all-to-all-start.5 = ((bf16[16,8,1536]{2,1,0:T(8,128)(2,1)}), bf16[16,8,1536]{2,1,0:T(8,128)(2,1)S(1)}, u32[]{:S(2)}, u32[]{:S(2)}) async-start(bf16[16,8,1536]{2,1,0:T(8,128)(2,1)} %copy-done.4), calls=%async_computation.5 | async-start | bytes 786432 | tf_op jit(solution)/shard_map/all_to_all | solution.py:17
  159.1 25.5 %collective-permute-start.4 = (bf16[1024,384]{1,0:T(8,128)(2,1)}, bf16[1024,384]{1,0:T(8,128)(2,1)S(1)}, u32[]{:S(2)}, u32[]{:S(2)}) collective-permute-start(bf16[1024,384]{1,0:T(8,128)(2,1)} %get-tuple-element.43), channel_id=1, source_target_pairs={{0,3},{1,0},{2,1},{3,2},{4,7},{5,4},{6,5},{7,6},{8,11},{9,8},{10,9... | collective-permute-start | bytes 2359304 | tf_op jit(solution)/shard_map/ppermute | solution.py:410
  161.8 23.6 %collective-permute-start.3 = (bf16[1024,384]{1,0:T(8,128)(2,1)S(1)}, bf16[1024,384]{1,0:T(8,128)(2,1)S(1)}, u32[]{:S(2)}, u32[]{:S(2)}) collective-permute-start(bf16[1024,384]{1,0:T(8,128)(2,1)S(1)} %get-tuple-element.44), channel_id=1, source_target_pairs={{0,1},{1,2},{2,3},{3,0},{4,5},{5,6},{6,7},{7,4},{8,9},{9,10},{10,1... | collective-permute-start | bytes 2359304 | tf_op jit(solution)/shard_map/ppermute | solution.py:410
  171.0 24.7 %all-to-all-start.6 = ((bf16[16,8,384]{2,1,0:T(8,128)(2,1)}), bf16[16,8,384]{2,1,0:T(8,128)(2,1)S(1)}, u32[]{:S(2)}, u32[]{:S(2)}) async-start(bf16[16,8,384]{2,1,0:T(8,128)(2,1)} %get-tuple-element.35), calls=%async_computation.6 | async-start | bytes 196608 | tf_op jit(solution)/shard_map/all_to_all | solution.py:17
  214.7 20.5 %all-to-all-start.7 = ((bf16[4,400,384]{2,1,0:T(8,128)(2,1)}), bf16[4,400,384]{2,1,0:T(8,128)(2,1)S(1)}, u32[]{:S(2)}, u32[]{:S(2)}) async-start(bf16[4,400,384]{2,1,0:T(8,128)(2,1)} %copy-done), calls=%async_computation.7 | async-start | bytes 2457600 | tf_op jit(solution)/shard_map/all_to_all | solution.py:17
  (16 other events, 36.3 us)
Sparse Core Ops, SparseCore 0:
  10.1 36.9 all-gather.6
  49.3 31.7 all-gather.8
  83.2 30.0 all-gather.10

commit v7 on v5

--- a/solution.py
+++ b/solution.py
@@ -355,7 +355,6 @@
         (s * n_hid + h, (h * per + s % per) * n_hid + s // per) for s in range(n_seq) for h in range(n_hid)
     ]
     w_out_here = lax.ppermute(w_out, ("seq", "hid"), route)
-    w_out_all = lax.all_gather(w_out_here, "seq", axis=0, tiled=False)
     w_maps = w_xproj[:, rank:]
     w_maps = jnp.concatenate(
         [w_xproj[:, :rank]] + [jnp.pad(w_maps, ((0, 0), (32 * r, 96 - 32 * r))) for r in range(rows)], 1
@@ -400,6 +399,8 @@
     )
 
     got = exchange(tiles, ("exp", "hid"))
+    got, w_out_here = lax.optimization_barrier((got, w_out_here))
+    w_out_all = lax.all_gather(w_out_here, "seq", axis=0, tiled=False)
     back = exchange(call(tile_sum_kernel, "tile_sum", like(got.shape, BF16), [], got, routes, gate_in, unread=1), ("exp", "hid"))
 
     def pick(w, d):

time: 247 us -> 253 us (1.024)
  starting transfers between devices: 74.2 us -> 64.3 us
  waiting for transfers between devices: 54.3 us -> 63.6 us
  blocking collectives: 68.5 us -> 75.1 us
    all_to_all x7, waiting for transfers between devices: 53 us -> 61.5 us  [exchange(): return lax.all_to_all(x, axis, split_axis=0, concat_axis=0, tiled=True)]
    all_to_all x1, blocking collectives: 19.5 us -> 26.1 us  [exchange(): return lax.all_to_all(x, axis, split_axis=0, concat_axis=0, tiled=True)]
    all_to_all x7, starting transfers between devices: 47.8 us -> 43 us  [exchange(): return lax.all_to_all(x, axis, split_axis=0, concat_axis=0, tiled=True)]
    ppermute x1, starting transfers between devices: 16 us -> 12.3 us  [shards(): halo = lax.ppermute(tail, 'seq', [(i, i + 1) for i in range(n_seq - 1)])]
where the time goes in v7:
time: 253 us; the launch traced here: 251 us
  blocking collectives  75.1 us (30%)
  starting transfers between devices  64.3 us (25%)
  waiting for transfers between devices  63.6 us (25%)
  local copies, waits for them, and re-layouts  20.5 us (8%)
  between operations  14.3 us (6%)
  Pallas kernels  12.8 us (5%)
    all_to_all x7, waiting for transfers between devices, exchange(): return lax.all_to_all(x, axis, split_axis=0, concat_axis=0, tiled=True)  61.5 us
    all_to_all x7, starting transfers between devices, exchange(): return lax.all_to_all(x, axis, split_axis=0, concat_axis=0, tiled=True)  43 us
    all_gather x1, blocking collectives, shards(): over_exp = lax.all_gather(x_in, 'exp', axis=0, tiled=False)  32.5 us
    all_to_all x1, blocking collectives, exchange(): return lax.all_to_all(x, axis, split_axis=0, concat_axis=0, tiled=True)  26.1 us
    all_gather x1, blocking collectives, shards(): all_slots = lax.all_gather(slots, 'seq', axis=0, tiled=True)  16.5 us
    pallas_call x15, Pallas kernels, call(): pl.pallas_call(body, out_shape=out_shape, in_specs=[smem] * scalars + [vm...  12.8 us
    ppermute x1, starting transfers between devices, shards(): halo = lax.ppermute(tail, 'seq', [(i, i + 1) for i in range(n_seq - 1)])  12.3 us
    unnamed x48, local copies, waits for them, and re-layouts  12 us
  transfers between devices with their start and end apart: 15, of which 8 were waited for; matrix products, arithmetic and copies ran while one was open for 4% of the time, Pallas kernels for 3%

profile of v7, /device:TPU:1, one launch (start us, length us, event | category | flops | bytes accessed | tf_op | source)
XLA Modules:
  0.0 251.3 jit_solution(13773687687984992411)
XLA Ops:
  7.9 32.5 %all-gather.2.x_ref = bf16[16,3,4096]{2,1,0:T(4,128)(2,1)S(1)} all-gather(bf16[1,3,4096]{2,1,0:T(4,128)(2,1)} %bitcast.54), channel_id=2, replica_groups=mesh['seq'=8,'exp'=16,'hid'=4] {'exp'}, dimensions={0}, use_global_device_ids=true | all-gather | bytes 417792 | tf_op jit(solution)/shard_map/all_gather | solution.py:344
  41.9 4.1 %all-to-all-start = ((bf16[4,48,4224]{2,1,0:T(8,128)(2,1)}), bf16[4,48,4224]{2,1,0:T(8,128)(2,1)S(1)}, u32[]{:S(2)}, u32[]{:S(2)}) async-start(bf16[4,48,4224]{2,1,0:T(8,128)(2,1)} %rows.1), calls=%async_computation | async-start | bytes 3244032 | tf_op jit(solution)/shard_map/all_to_all | solution.py:17
  48.5 10.5 %all-to-all-done.x_ref = bf16[4,48,4224]{2,1,0:T(8,128)(2,1)S(1)} async-done(((bf16[4,48,4224]{2,1,0:T(8,128)(2,1)}), bf16[4,48,4224]{2,1,0:T(8,128)(2,1)S(1)}, u32[]{:S(2)}, u32[]{:S(2)}) %all-to-all-start) | async-done | bytes 1622048 | tf_op jit(solution)/shard_map/all_to_all | solution.py:17
  59.7 12.3 %collective-permute-start = (f32[8,128]{1,0:T(8,128)S(1)}, f32[8,128]{1,0:T(8,128)S(1)}, u32[]{:S(2)}, u32[]{:S(2)}) collective-permute-start(f32[8,128]{1,0:T(8,128)S(1)} %get-tuple-element.23), channel_id=1, source_target_pairs={{0,64},{64,128},{128,192},{192,256},{256,320},{320,384},{384,448},... | collective-permute-start | bytes 12296 | tf_op jit(solution)/shard_map/ppermute | solution.py:389
  73.7 8.2 %all-to-all-start.1 = ((bf16[64,8,128]{2,1,0:T(8,128)(2,1)}), bf16[64,8,128]{2,1,0:T(8,128)(2,1)S(1)}, u32[]{:S(2)}, u32[]{:S(2)}) async-start(bf16[64,8,128]{2,1,0:T(8,128)(2,1)} %get-tuple-element.24), calls=%async_computation.1 | async-start | bytes 262144 | tf_op jit(solution)/shard_map/all_to_all | solution.py:17
  82.7 16.2 %all-to-all-done.1.got_ref = bf16[64,8,128]{2,1,0:T(8,128)(2,1)S(1)} async-done(((bf16[64,8,128]{2,1,0:T(8,128)(2,1)}), bf16[64,8,128]{2,1,0:T(8,128)(2,1)S(1)}, u32[]{:S(2)}, u32[]{:S(2)}) %all-to-all-start.1) | async-done | bytes 131104 | tf_op jit(solution)/shard_map/all_to_all | solution.py:17
  101.0 2.1 dynamic-slice_bitcast_fusion.3
  103.1 3.0 %collective-permute-start.2 = (bf16[1024,384]{1,0:T(8,128)(2,1)}, bf16[1024,384]{1,0:T(8,128)(2,1)S(1)}, u32[]{:S(2)}, u32[]{:S(2)}) collective-permute-start(bf16[1024,384]{1,0:T(8,128)(2,1)} %dynamic-slice_bitcast_fusion.3), channel_id=1, source_target_pairs={{0,2},{1,3},{2,0},{3,1},{4,6},{5,7},{6,4},{7,5},{8,10},{9,11},{10,... | collective-permute-start | bytes 2359304 | tf_op jit(solution)/shard_map/ppermute | solution.py:410
  106.3 26.1 %all_to_all.40.back_ref = bf16[64,8,128]{2,1,0:T(8,128)(2,1)S(1)} all-to-all(bf16[64,8,128]{2,1,0:T(8,128)(2,1)S(1)} %tile_sum.1), channel_id=1, replica_groups=mesh['seq'=8,'exp'=16,'hid'=4] {'exp','hid'}, dimensions={0} | all-to-all | bytes 262144 | tf_op jit(solution)/shard_map/all_to_all | solution.py:17
  132.4 1.8 scan.1
  134.2 6.8 %all-to-all-start.3 = ((f32[8,24,128]{2,1,0:T(8,128)}), f32[8,24,128]{2,1,0:T(8,128)S(1)}, u32[]{:S(2)}, u32[]{:S(2)}) async-start(f32[8,24,128]{2,1,0:T(8,128)} %get-tuple-element.29), calls=%async_computation.3 | async-start | bytes 196608 | tf_op jit(solution)/shard_map/all_to_all | solution.py:17
  141.0 5.0 %all-to-all-done.3.all_ref = f32[8,24,128]{2,1,0:T(8,128)S(1)} async-done(((f32[8,24,128]{2,1,0:T(8,128)}), f32[8,24,128]{2,1,0:T(8,128)S(1)}, u32[]{:S(2)}, u32[]{:S(2)}) %all-to-all-start.3) | async-done | bytes 98336 | tf_op jit(solution)/shard_map/all_to_all | solution.py:17
  147.2 4.0 %all-to-all-start.4 = ((bf16[4,192,128]{2,1,0:T(8,128)(2,1)}), bf16[4,192,128]{2,1,0:T(8,128)(2,1)}, u32[]{:S(2)}, u32[]{:S(2)}) async-start(bf16[4,192,128]{2,1,0:T(8,128)(2,1)} %gate.1), calls=%async_computation.4 | async-start | bytes 393216 | tf_op jit(solution)/shard_map/all_to_all | solution.py:17
  152.6 3.9 %all-to-all-done.4.gated_ref = bf16[4,192,128]{2,1,0:T(8,128)(2,1)} async-done(((bf16[4,192,128]{2,1,0:T(8,128)(2,1)}), bf16[4,192,128]{2,1,0:T(8,128)(2,1)}, u32[]{:S(2)}, u32[]{:S(2)}) %all-to-all-start.4) | async-done | bytes 196640 | tf_op jit(solution)/shard_map/all_to_all | solution.py:17
  158.8 3.6 %all-to-all-start.5 = ((bf16[16,8,1536]{2,1,0:T(8,128)(2,1)}), bf16[16,8,1536]{2,1,0:T(8,128)(2,1)S(1)}, u32[]{:S(2)}, u32[]{:S(2)}) async-start(bf16[16,8,1536]{2,1,0:T(8,128)(2,1)} %copy-done.4), calls=%async_computation.5 | async-start | bytes 786432 | tf_op jit(solution)/shard_map/all_to_all | solution.py:17
  164.4 3.0 %dynamic-slice_bitcast_fusion = (bf16[1024,384]{1,0:T(8,128)(2,1)}, bf16[1024,384]{1,0:T(8,128)(2,1)S(1)}, bf16[1024,384]{1,0:T(8,128)(2,1)}) fusion(bf16[4,1024,384]{2,1,0:T(8,128)(2,1)} %bitcast.47, s32[]{:T(128)S(6)} %select_n.65, s32[]{:T(128)S(6)} %select_n.63, s32[]{:T(128)S(6)} %select_n.61), kind=kLoop, calls=%fused_computation.3 | loop fusion | bytes 4718604 | tf_op jit(solution)/shard_map/jit(dynamic_index_in_dim)/squeeze | solution.py:407
  167.4 2.8 %collective-permute-start.4 = (bf16[1024,384]{1,0:T(8,128)(2,1)}, bf16[1024,384]{1,0:T(8,128)(2,1)S(1)}, u32[]{:S(2)}, u32[]{:S(2)}) collective-permute-start(bf16[1024,384]{1,0:T(8,128)(2,1)} %get-tuple-element.43), channel_id=1, source_target_pairs={{0,3},{1,0},{2,1},{3,2},{4,7},{5,4},{6,5},{7,6},{8,11},{9,8},{10,9... | collective-permute-start | bytes 2359304 | tf_op jit(solution)/shard_map/ppermute | solution.py:410
  170.2 2.5 collective-permute-start.3
  173.3 5.2 %all-to-all-done.5.parts_ref = bf16[16,8,1536]{2,1,0:T(8,128)(2,1)S(1)} async-done(((bf16[16,8,1536]{2,1,0:T(8,128)(2,1)}), bf16[16,8,1536]{2,1,0:T(8,128)(2,1)S(1)}, u32[]{:S(2)}, u32[]{:S(2)}) %all-to-all-start.5) | async-done | bytes 393248 | tf_op jit(solution)/shard_map/all_to_all | solution.py:17
  179.4 12.8 %all-to-all-start.6 = ((bf16[16,8,384]{2,1,0:T(8,128)(2,1)}), bf16[16,8,384]{2,1,0:T(8,128)(2,1)S(1)}, u32[]{:S(2)}, u32[]{:S(2)}) async-start(bf16[16,8,384]{2,1,0:T(8,128)(2,1)} %get-tuple-element.35), calls=%async_computation.6 | async-start | bytes 196608 | tf_op jit(solution)/shard_map/all_to_all | solution.py:17
  199.6 4.5 %all-to-all-done.6.got_ref = bf16[16,8,384]{2,1,0:T(8,128)(2,1)S(1)} async-done(((bf16[16,8,384]{2,1,0:T(8,128)(2,1)}), bf16[16,8,384]{2,1,0:T(8,128)(2,1)S(1)}, u32[]{:S(2)}, u32[]{:S(2)}) %all-to-all-start.6) | async-done | bytes 98336 | tf_op jit(solution)/shard_map/all_to_all | solution.py:17
  204.1 16.5 %all_gather.27.tok_ref = bf16[384,1024]{1,0:T(8,128)(2,1)S(1)} all-gather(bf16[48,1024]{1,0:T(8,128)(2,1)S(1)} %slots.1), channel_id=1, replica_groups=mesh['seq'=8,'exp'=16,'hid'=4] {'seq'}, dimensions={0}, use_global_device_ids=true | all-gather | bytes 884736 | tf_op jit(solution)/shard_map/all_gather | solution.py:506
  223.1 3.5 %all-to-all-start.7 = ((bf16[4,400,384]{2,1,0:T(8,128)(2,1)}), bf16[4,400,384]{2,1,0:T(8,128)(2,1)S(1)}, u32[]{:S(2)}, u32[]{:S(2)}) async-start(bf16[4,400,384]{2,1,0:T(8,128)(2,1)} %copy-done), calls=%async_computation.7 | async-start | bytes 2457600 | tf_op jit(solution)/shard_map/all_to_all | solution.py:17
  227.3 16.3 %all-to-all-done.7.part_ref = bf16[4,400,384]{2,1,0:T(8,128)(2,1)S(1)} async-done(((bf16[4,400,384]{2,1,0:T(8,128)(2,1)}), bf16[4,400,384]{2,1,0:T(8,128)(2,1)S(1)}, u32[]{:S(2)}, u32[]{:S(2)}) %all-to-all-start.7) | async-done | bytes 1228832 | tf_op jit(solution)/shard_map/all_to_all | solution.py:17
  (116 shorter events, 29.9 us)
Async XLA Ops:
  7.2 39.9 %all-gather.7.cloned.1.call-start = ((), (), s32[]{:S(2)}) async-start(), calls=%async_computation.8 | async-start | bytes 1179648 | tf_op jit(solution)/shard_map/all_gather | solution.py:342
  41.9 17.0 %all-to-all-start = ((bf16[4,48,4224]{2,1,0:T(8,128)(2,1)}), bf16[4,48,4224]{2,1,0:T(8,128)(2,1)S(1)}, u32[]{:S(2)}, u32[]{:S(2)}) async-start(bf16[4,48,4224]{2,1,0:T(8,128)(2,1)} %rows.1), calls=%async_computation | async-start | bytes 3244032 | tf_op jit(solution)/shard_map/all_to_all | solution.py:17
  46.1 52.9 %all-gather.9.cloned.1.call-start = ((), (), s32[]{:S(2)}) async-start(), calls=%async_computation.9 | async-start | bytes 1179648 | tf_op jit(solution)/shard_map/all_gather | solution.py:353
  48.4 23.8 %copy-start.15 = (f32[16,128]{1,0:T(8,128)S(1)}, f32[16,128]{1,0:T(8,128)}, u32[]{:S(2)}) copy-start(f32[16,128]{1,0:T(8,128)} %param.25) | copy-start | bytes 24580
  48.4 23.8 %copy-start.16 = (f32[4,128]{1,0:T(4,128)S(1)}, f32[4,128]{1,0:T(4,128)}, u32[]{:S(2)}) copy-start(f32[4,128]{1,0:T(4,128)} %param.20) | copy-start | bytes 6148
  48.4 23.7 %copy-start.18 = (f32[128]{0:T(128)S(1)}, f32[128]{0:T(128)}, u32[]{:S(2)}) copy-start(f32[128]{0:T(128)} %param.21) | copy-start | bytes 1540
  48.4 23.7 %copy-start.19 = (f32[128]{0:T(128)S(1)}, f32[128]{0:T(128)}, u32[]{:S(2)}) copy-start(f32[128]{0:T(128)} %param.24) | copy-start | bytes 1540
  48.4 23.7 %copy-start.20 = (f32[128]{0:T(128)S(1)}, f32[128]{0:T(128)}, u32[]{:S(2)}) copy-start(f32[128]{0:T(128)} %param.26) | copy-start | bytes 1540
  58.9 23.1 %copy-start.21 = (bf16[128,512]{1,0:T(8,128)(2,1)S(1)}, bf16[128,512]{1,0:T(8,128)(2,1)}, u32[]{:S(2)}) copy-start(bf16[128,512]{1,0:T(8,128)(2,1)} %param.27) | copy-start | bytes 393220
  58.9 40.0 %copy-start.17 = (s32[3,2]{0,1:T(2,128)S(1)}, s32[3,2]{0,1:T(2,128)}, u32[]{:S(2)}) copy-start(s32[3,2]{0,1:T(2,128)} %param.29) | copy-start | bytes 76
  58.9 40.0 %copy-start.22 = (bf16[3,2]{0,1:T(2,128)(2,1)S(1)}, bf16[3,2]{0,1:T(2,128)(2,1)}, u32[]{:S(2)}) copy-start(bf16[3,2]{0,1:T(2,128)(2,1)} %param.30) | copy-start | bytes 40
  59.7 13.1 %collective-permute-start = (f32[8,128]{1,0:T(8,128)S(1)}, f32[8,128]{1,0:T(8,128)S(1)}, u32[]{:S(2)}, u32[]{:S(2)}) collective-permute-start(f32[8,128]{1,0:T(8,128)S(1)} %get-tuple-element.23), channel_id=1, source_target_pairs={{0,64},{64,128},{128,192},{192,256},{256,320},{320,384},{384,448},... | collective-permute-start | bytes 12296 | tf_op jit(solution)/shard_map/ppermute | solution.py:389
  73.7 25.2 %all-to-all-start.1 = ((bf16[64,8,128]{2,1,0:T(8,128)(2,1)}), bf16[64,8,128]{2,1,0:T(8,128)(2,1)S(1)}, u32[]{:S(2)}, u32[]{:S(2)}) async-start(bf16[64,8,128]{2,1,0:T(8,128)(2,1)} %get-tuple-element.24), calls=%async_computation.1 | async-start | bytes 262144 | tf_op jit(solution)/shard_map/all_to_all | solution.py:17
  81.9 69.3 %all-gather.11.cloned.1.call-start = ((), (), s32[]{:S(2)}) async-start(), calls=%async_computation.10 | async-start | bytes 1179648 | tf_op jit(solution)/shard_map/all_gather | solution.py:403
  82.0 0.7 collective-permute-start.1
  101.0 31.4 %copy-start.13 = (bf16[256,128]{1,0:T(8,128)(2,1)S(1)}, bf16[256,128]{1,0:T(8,128)(2,1)}, u32[]{:S(2)}) copy-start(bf16[256,128]{1,0:T(8,128)(2,1)} %wdt_ref.1) | copy-start | bytes 196612
  103.1 49.5 %collective-permute-start.2 = (bf16[1024,384]{1,0:T(8,128)(2,1)}, bf16[1024,384]{1,0:T(8,128)(2,1)S(1)}, u32[]{:S(2)}, u32[]{:S(2)}) collective-permute-start(bf16[1024,384]{1,0:T(8,128)(2,1)} %dynamic-slice_bitcast_fusion.3), channel_id=1, source_target_pairs={{0,2},{1,3},{2,0},{3,1},{4,6},{5,7},{6,4},{7,5},{8,10},{9,11},{10,... | collective-permute-start | bytes 2359304 | tf_op jit(solution)/shard_map/ppermute | solution.py:410
  134.2 11.8 %all-to-all-start.3 = ((f32[8,24,128]{2,1,0:T(8,128)}), f32[8,24,128]{2,1,0:T(8,128)S(1)}, u32[]{:S(2)}, u32[]{:S(2)}) async-start(f32[8,24,128]{2,1,0:T(8,128)} %get-tuple-element.29), calls=%async_computation.3 | async-start | bytes 196608 | tf_op jit(solution)/shard_map/all_to_all | solution.py:17
  147.2 9.2 %all-to-all-start.4 = ((bf16[4,192,128]{2,1,0:T(8,128)(2,1)}), bf16[4,192,128]{2,1,0:T(8,128)(2,1)}, u32[]{:S(2)}, u32[]{:S(2)}) async-start(bf16[4,192,128]{2,1,0:T(8,128)(2,1)} %gate.1), calls=%async_computation.4 | async-start | bytes 393216 | tf_op jit(solution)/shard_map/all_to_all | solution.py:17
  158.8 19.7 %all-to-all-start.5 = ((bf16[16,8,1536]{2,1,0:T(8,128)(2,1)}), bf16[16,8,1536]{2,1,0:T(8,128)(2,1)S(1)}, u32[]{:S(2)}, u32[]{:S(2)}) async-start(bf16[16,8,1536]{2,1,0:T(8,128)(2,1)} %copy-done.4), calls=%async_computation.5 | async-start | bytes 786432 | tf_op jit(solution)/shard_map/all_to_all | solution.py:17
  167.4 25.5 %collective-permute-start.4 = (bf16[1024,384]{1,0:T(8,128)(2,1)}, bf16[1024,384]{1,0:T(8,128)(2,1)S(1)}, u32[]{:S(2)}, u32[]{:S(2)}) collective-permute-start(bf16[1024,384]{1,0:T(8,128)(2,1)} %get-tuple-element.43), channel_id=1, source_target_pairs={{0,3},{1,0},{2,1},{3,2},{4,7},{5,4},{6,5},{7,6},{8,11},{9,8},{10,9... | collective-permute-start | bytes 2359304 | tf_op jit(solution)/shard_map/ppermute | solution.py:410
  170.2 23.6 %collective-permute-start.3 = (bf16[1024,384]{1,0:T(8,128)(2,1)S(1)}, bf16[1024,384]{1,0:T(8,128)(2,1)S(1)}, u32[]{:S(2)}, u32[]{:S(2)}) collective-permute-start(bf16[1024,384]{1,0:T(8,128)(2,1)S(1)} %get-tuple-element.44), channel_id=1, source_target_pairs={{0,1},{1,2},{2,3},{3,0},{4,5},{5,6},{6,7},{7,4},{8,9},{9,10},{10,1... | collective-permute-start | bytes 2359304 | tf_op jit(solution)/shard_map/ppermute | solution.py:410
  179.4 24.7 %all-to-all-start.6 = ((bf16[16,8,384]{2,1,0:T(8,128)(2,1)}), bf16[16,8,384]{2,1,0:T(8,128)(2,1)S(1)}, u32[]{:S(2)}, u32[]{:S(2)}) async-start(bf16[16,8,384]{2,1,0:T(8,128)(2,1)} %get-tuple-element.35), calls=%async_computation.6 | async-start | bytes 196608 | tf_op jit(solution)/shard_map/all_to_all | solution.py:17
  223.1 20.5 %all-to-all-start.7 = ((bf16[4,400,384]{2,1,0:T(8,128)(2,1)}), bf16[4,400,384]{2,1,0:T(8,128)(2,1)S(1)}, u32[]{:S(2)}, u32[]{:S(2)}) async-start(bf16[4,400,384]{2,1,0:T(8,128)(2,1)} %copy-done), calls=%async_computation.7 | async-start | bytes 2457600 | tf_op jit(solution)/shard_map/all_to_all | solution.py:17
  (16 other events, 60.5 us)
Sparse Core Ops, SparseCore 0:
  10.1 36.7 all-gather.6
  49.1 35.2 all-gather.8
  99.0 26.5 all-gather.10
